TPU v7x, 32 devices: a whole 2x2x4 slice. The times are simulated.
32 devices in a mesh: fsdp: 8 (over z, y), dp: 4 (over x, core).
Axes of the slice: x: 2, y: 2, z: 4, core: 2. Of those that a mesh axis runs over, the one named last changes fastest.
Arguments:
- inputs: bfloat16 [2, 12288, 1024], P(None, ('fsdp', 'dp')), may hold values from -6 to 6
- cotangent: bfloat16 [2, 12288, 1024], P(None, ('fsdp', 'dp')), may hold values from -6 to 6
- lengths: int32 [2, 32], P(None, ('fsdp', 'dp')), may hold values from 96 to 384, as said below
- attention_weights: float32 [4, 1024, 1024], P(None, 'fsdp')
- attention_momentum: float32 [4, 1024, 1024], P(None, 'fsdp')
- attention_average: float32 [4, 1024, 1024], P(None, 'fsdp'), may hold values from -0.1875 to 0.1875
- ffn_inputs: float32 [2, 1024, 2816], P(None, 'fsdp'), may hold values from -0.1875 to 0.1875
- ffn_inputs_momentum: float32 [2, 1024, 2816], P(None, 'fsdp')
- ffn_inputs_average: float32 [2, 1024, 2816], P(None, 'fsdp'), may hold values from -0.1875 to 0.1875
- ffn_output: float32 [2816, 1024], P('fsdp'), may hold values from -0.109375 to 0.109375
- ffn_output_momentum: float32 [2816, 1024], P('fsdp')
- ffn_output_average: float32 [2816, 1024], P('fsdp'), may hold values from -0.109375 to 0.109375
- gains: float32 [3, 1024], P(None, 'fsdp'), may hold values from 0.5 to 1.5
- gains_momentum: float32 [3, 1024], P(None, 'fsdp')
- gains_average: float32 [3, 1024], P(None, 'fsdp'), may hold values from 0.5 to 1.5
Outputs:
- output: bfloat16 [2, 12288, 1024], P(None, ('fsdp', 'dp'))
- input_grad: float32 [2, 12288, 1024], P(None, ('fsdp', 'dp'))
- attention_momentum_new: float32 [4, 1024, 1024], P(None, 'fsdp')
- attention_average_new: float32 [4, 1024, 1024], P(None, 'fsdp')
- attention_weights_new: float32 [4, 1024, 1024], P(None, 'fsdp')
- ffn_inputs_momentum_new: float32 [2, 1024, 2816], P(None, 'fsdp')
- ffn_inputs_average_new: float32 [2, 1024, 2816], P(None, 'fsdp')
- ffn_inputs_new: float32 [2, 1024, 2816], P(None, 'fsdp')
- ffn_output_momentum_new: float32 [2816, 1024], P('fsdp')
- ffn_output_average_new: float32 [2816, 1024], P('fsdp')
- ffn_output_new: float32 [2816, 1024], P('fsdp')
- gains_momentum_new: float32 [3, 1024], P(None, 'fsdp')
- gains_average_new: float32 [3, 1024], P(None, 'fsdp')
- gains_new: float32 [3, 1024], P(None, 'fsdp')
Inputs may be any that keep to these rules, and one draw needn't show every extreme that they name: `lengths`: in every micro-batch one sequence has exactly 384 valid positions.
All inputs are finite; a program needn't handle non-finite values.
Results may differ from a plain program's by a relative error of at most 0.013.
Values may be sent and summed in bfloat16 or wider, within the bound.
No kernel may reach another device: no remote copies, remote signals or barrier semaphores. Data moves between devices by JAX's collectives and lax.ppermute only.
A program may use at most 320 MiB of HBM per device.

v0:
```python
import functools
import math

import jax
import jax.numpy as jnp
from jax import lax
from jax.experimental import pallas as pl
from jax.experimental.pallas import tpu as pltpu
from jax.sharding import PartitionSpec as P

HEAD_DIM = 128
PAIR = 2 * HEAD_DIM
GAIN_ROWS = 16

lower_bound = 0.9
momentum_decay = 0.9
average_decay = 0.7
weight_decay = 0.0005
matrix_rate = 0.03
gain_rate = 0.1
low = jnp.bfloat16
wide = jnp.float32
TILE_F = 256
VMEM_BYTES = 60 * 1024 * 1024


def mm(left, right):
    return jnp.dot(left, right, preferred_element_type=wide)


def mm_nt(left, right):
    return lax.dot_general(left, right, (((1,), (1,)), ((), ())), preferred_element_type=wide)


def mm_tn(left, right):
    return lax.dot_general(left, right, (((0,), (0,)), ((), ())), preferred_element_type=wide)


def sigmoid(u):
    return 0.5 * jnp.tanh(0.5 * u) + 0.5


def whole(shape):
    return pl.BlockSpec(shape, lambda *_: (0,) * len(shape), pipeline_mode=pl.Buffered(1))


def split_sum(ones_matrix, tensor):
    high = tensor.astype(low)
    rest = (tensor - high.astype(wide)).astype(low)
    return mm(ones_matrix, high) + mm(ones_matrix, rest)


def causal_mask(length, lower):
    rows = lax.broadcasted_iota(jnp.int32, (length, length), 0)
    columns = lax.broadcasted_iota(jnp.int32, (length, length), 1)
    return rows >= columns if lower else rows <= columns


def triangle(length, lower):
    return causal_mask(length, lower).astype(wide).astype(low)


def decay_parts(f_pre, lower_ones):
    share = sigmoid(f_pre)
    gate = lower_bound + (1.0 - lower_bound) * share
    keys_in = (1.0 - lower_bound) * (1.0 - share)
    cumulative = split_sum(lower_ones, jnp.log(gate))
    middle_row = cumulative.shape[0] // 2
    cumulative = cumulative - cumulative[middle_row : middle_row + 1, :]
    return share, gate, keys_in, cumulative


def first_norm(x_ref, gain_row):
    rows = x_ref[...].astype(wide)
    scale = lax.rsqrt(jnp.mean(rows * rows, axis=-1, keepdims=True) + 1e-06)
    return rows * scale, scale


def lanes_of(half, size):
    return pl.ds(pl.multiple_of(half * size, size), size)


def mixer_forward_first_kernel(
    slot, half_ref, x_ref, w_ref, gains_ref, on_ref, q_ref, f_ref, v_ref, o_ref, g_ref, h_s
):
    @pl.when(pl.program_id(0) == 0)
    def _():
        g_ref[...] = gains_ref[...].astype(wide)[: g_ref.shape[0], :]

    mixer_forward_kernel(
        slot, half_ref, x_ref, w_ref, g_ref, on_ref, q_ref, f_ref, v_ref, o_ref, h_s
    )


def mixer_forward_kernel(
    slot, half_ref, x_ref, w_ref, g_ref, on_ref, q_ref, f_ref, v_ref, o_ref, h_s
):
    @pl.when(pl.program_id(0) == 0)
    def _():
        normed, _ = first_norm(x_ref, None)
        h_s[...] = (normed * g_ref[0:1, :]).astype(low)

    gain_o = g_ref[1:2, lanes_of(half_ref[0] * pl.num_programs(0) + pl.program_id(0), PAIR)]
    pre = mm(h_s[...], w_ref[...])
    q_ref[...] = pre[:, :PAIR]
    f_ref[...] = pre[:, PAIR : 2 * PAIR]
    v_ref[...] = pre[:, 2 * PAIR :].astype(low)
    lower_ones = triangle(slot, True)
    causal = causal_mask(slot, True)
    for sequence in range(x_ref.shape[0] // slot):
        rows = slice(sequence * slot, (sequence + 1) * slot)
        q_pre = q_ref[rows, :]
        _, _, keys_in, cumulative = decay_parts(f_ref[rows, :], lower_ones)
        grown = jnp.exp(-cumulative)
        decayed_q = (q_pre * sigmoid(q_pre) * jnp.exp(cumulative)).astype(low)
        grown_k = (keys_in * grown).astype(low)
        values = v_ref[rows, :]
        for head in range(2):
            lanes = slice(head * HEAD_DIM, (head + 1) * HEAD_DIM)
            scores = mm_nt(decayed_q[:, lanes], grown_k[:, lanes])
            out = mm(jnp.where(causal, scores, 0.0).astype(low), values[:, lanes])
            scale = lax.rsqrt(jnp.mean(out * out, axis=-1, keepdims=True) + 1e-05)
            o_ref[rows, lanes] = out.astype(low)
            on_ref[rows, lanes] = (out * scale * gain_o[:, lanes]).astype(low)


def mixer_forward_last_kernel(
    slot,
    half_ref,
    x_ref,
    w_ref,
    g_ref,
    before_hbm,
    woo_hbm,
    wom_hbm,
    on_ref,
    q_ref,
    f_ref,
    v_ref,
    o_ref,
    x1_hbm,
    h2_ref,
    h2t_ref,
    h_s,
    on_s,
    x1_s,
    wo_s,
    semaphores,
):
    step = pl.program_id(0)
    half = before_hbm.shape[1]
    here, there = lanes_of(half_ref[0], half), lanes_of(1 - half_ref[0], half)
    sources = (
        (before_hbm, on_s.at[:, there]),
        (woo_hbm.at[:, pl.ds(3 * half, half)], wo_s.at[:, here]),
        (wom_hbm.at[:, pl.ds(3 * half, half)], wo_s.at[:, there]),
    )
    fetches = [
        pltpu.make_async_copy(source, target, semaphores.at[number])
        for number, (source, target) in enumerate(sources)
    ]

    @pl.when(step == 0)
    def _():
        for fetch in fetches:
            fetch.start()

    mixer_forward_kernel(
        slot, half_ref, x_ref, w_ref, g_ref, on_ref, q_ref, f_ref, v_ref, o_ref, h_s
    )
    on_s[:, lanes_of(half_ref[0] * pl.num_programs(0) + step, PAIR)] = on_ref[...]

    @pl.when(step == pl.num_programs(0) - 1)
    def _():
        for fetch in fetches:
            fetch.wait()
        x1 = x_ref[...].astype(wide) + mm(on_s[...], wo_s[...])
        x1_s[...] = x1
        leaving = pltpu.make_async_copy(x1_s, x1_hbm, semaphores.at[3])
        leaving.start()
        scale = lax.rsqrt(jnp.mean(x1 * x1, axis=-1, keepdims=True) + 1e-06)
        normed = x1 * scale * g_ref[2:3, :]
        h2_ref[...] = normed.astype(low)
        h2t_ref[...] = normed.T.astype(low)
        leaving.wait()


def norm_rows_kernel(x_ref, out_ref):
    normed, _ = first_norm(x_ref, None)
    out_ref[...] = normed.T.astype(low)


def norm_rows(rows):
    count, width = rows.shape
    return pl.pallas_call(
        norm_rows_kernel,
        in_specs=[pl.BlockSpec(memory_space=pltpu.VMEM)],
        out_specs=pl.BlockSpec(memory_space=pltpu.VMEM),
        out_shape=jax.ShapeDtypeStruct((width, count), low),
        compiler_params=pltpu.CompilerParams(vmem_limit_bytes=VMEM_BYTES),
        name="norm_rows",
    )(rows)


def mixer_forward(half, rows, weights, slot, gains=None, ending=None):
    count, width = rows.shape
    pairs = width // PAIR // 2
    by_pair = pl.BlockSpec((count, PAIR), lambda j, _: (0, j))
    struct = jax.ShapeDtypeStruct
    shape = lambda kind: struct((count, width // 2), kind)
    in_specs = [whole(rows.shape), pl.BlockSpec((width, 3 * PAIR), lambda j, _: (0, j))]
    operands = [half, rows, weights]
    out_specs = [by_pair] * 5
    out_shape = [shape(low), shape(wide), shape(wide), shape(low), shape(low)]
    scratch = [pltpu.VMEM((count, width), low)]
    if ending is None:
        kernel = mixer_forward_first_kernel
        in_specs += [whole(gains.shape)]
        operands += [gains]
        out_specs += [whole((8, width))]
        out_shape += [struct((8, width), wide)]
    if ending is not None:
        kernel = mixer_forward_last_kernel
        anywhere = pl.BlockSpec(memory_space=pl.ANY)
        in_specs += [whole(ending[0].shape), anywhere, anywhere, anywhere]
        operands += [ending[0], ending[1], weights, ending[2]]
        out_specs += [anywhere, whole((count, width)), whole((width, count))]
        out_shape += [
            struct((count, width), wide),
            struct((count, width), low),
            struct((width, count), low),
        ]
        scratch += [
            pltpu.VMEM((count, width), low),
            pltpu.VMEM((count, width), wide),
            pltpu.VMEM((width, width), low),
            pltpu.SemaphoreType.DMA((4,)),
        ]
    return pl.pallas_call(
        functools.partial(kernel, slot),
        grid_spec=pltpu.PrefetchScalarGridSpec(
            num_scalar_prefetch=1,
            grid=(pairs,),
            in_specs=in_specs,
            out_specs=out_specs,
            scratch_shapes=scratch,
        ),
        out_shape=out_shape,
        compiler_params=pltpu.CompilerParams(vmem_limit_bytes=VMEM_BYTES),
        cost_estimate=pl.CostEstimate(
            flops=count * width * 4 * width + 10 * count * slot * width,
            bytes_accessed=count * width * 12 + width * width * 4,
            transcendentals=count * width * 3,
        ),
        name="mixer_forward",
    )(*operands)


def store_down(out_ref, tile, owners):
    _, stride, down_rows = owners
    block = math.gcd(down_rows, tile.shape[0])
    first = pl.program_id(0) * (tile.shape[0] // block)
    for part in range(tile.shape[0] // block):
        owner = (first + part) // (down_rows // block)
        inside = (first + part) % (down_rows // block)
        start = pl.multiple_of(owner * stride + inside * block, block)
        out_ref[pl.ds(start, block), :] = tile[part * block : (part + 1) * block, :]


def ffn_kernel(
    owners,
    core_ref,
    h_ref,
    ht_ref,
    e_ref,
    wm_ref,
    wu_ref,
    wdm_ref,
    wdo_ref,
    x1_hbm,
    onm_hbm,
    ono_hbm,
    wom_hbm,
    woo_hbm,
    m_ref,
    g_ref,
    gm_ref,
    gu_ref,
    gdm_hbm,
    gdo_hbm,
    out_hbm,
    dx1_hbm,
    don_hbm,
    *scratch,
):
    gu_w, gu_g, down_g, down_w, mid_s, dh_s, on_s, x1_s, wo_s, out_s, gdm_s, gdo_s = scratch[:12]
    in_semaphores, out_semaphores, down_semaphores = scratch[12:]
    step, last = pl.program_id(0), pl.num_programs(0) - 1
    half, tile = wdm_ref.shape[1], wm_ref.shape[1]
    mine, other = lanes_of(core_ref[0], half), lanes_of(1 - core_ref[0], half)
    kind, kind_other = lanes_of(core_ref[0], tile), lanes_of(1 - core_ref[0], tile)
    count, stride, down_rows = owners

    width = on_s.shape[1]
    sources = (
        (x1_hbm, x1_s),
        (onm_hbm, on_s.at[:, mine]),
        (ono_hbm, on_s.at[:, other]),
        (wom_hbm.at[:, pl.ds(3 * half, half)], wo_s.at[:, mine]),
        (woo_hbm.at[:, pl.ds(3 * half, half)], wo_s.at[:, other]),
    )
    fetches = [
        pltpu.make_async_copy(source, target, in_semaphores.at[number])
        for number, (source, target) in enumerate(sources)
    ]

    def down_copies(owner):
        rows = pl.ds(pl.multiple_of(owner * stride, math.gcd(stride, 32)), down_rows)
        return [
            pltpu.make_async_copy(held.at[rows, :], out.at[rows, :], down_semaphores.at[side, owner])
            for side, (held, out) in enumerate(((gdm_s, gdm_hbm), (gdo_s, gdo_hbm)))
        ]

    @pl.when(step == 0)
    def _():
        dh_s[...] = jnp.zeros_like(dh_s)
        for fetch in fetches:
            fetch.start()

    gu_w[:, kind] = wm_ref[...]
    gu_w[:, kind_other] = wu_ref[...]
    hidden_rows = pl.ds(pl.multiple_of(step * tile, tile), tile)
    down_w[hidden_rows, mine] = wdm_ref[...]
    down_w[hidden_rows, other] = wdo_ref[...]
    pre = mm(h_ref[...], gu_w[...])
    a, b = pre[:, :tile], pre[:, tile:]
    share = sigmoid(a)
    swish = a * share
    mid = (swish * b).astype(low)
    mid_s[:, lanes_of(step, tile)] = mid
    d_mid = mm_nt(e_ref[...], down_w[hidden_rows, :])
    down_g[...] = mm_tn(mid, e_ref[...]).astype(low)
    d_a = (d_mid * b * (share + swish * (1.0 - share))).astype(low)
    d_b = (d_mid * swish).astype(low)
    d_pre = jnp.concatenate([d_a, d_b], axis=1)
    dh_s[...] += mm_nt(d_pre, gu_w[...])
    gu_g[...] = mm(ht_ref[...], d_pre).astype(low)
    blocks = tile // HEAD_DIM
    for side, block in enumerate((core_ref[1], 1 - core_ref[1])):
        gm_ref[side] = gu_g[:, lanes_of(core_ref[0] * blocks + block, HEAD_DIM)]
        gu_ref[side] = gu_g[:, lanes_of((1 - core_ref[0]) * blocks + block, HEAD_DIM)]
    store_down(gdm_s, down_g[:, mine], owners)
    store_down(gdo_s, down_g[:, other], owners)

    done = (step + 1) * tile // down_rows

    @pl.when(done > step * tile // down_rows)
    def _():
        for copy in down_copies(done - 1):
            copy.start()

    @pl.when(step == last)
    def _():
        for fetch in fetches:
            fetch.wait()
        x1 = x1_s[...]
        x2 = x1 + mm(mid_s[...], down_w[...])
        positions = lax.broadcasted_iota(jnp.int32, (out_s.shape[0] // m_ref.shape[0], 1), 0)
        for sequence in range(m_ref.shape[0]):
            rows = slice(sequence * positions.shape[0], (sequence + 1) * positions.shape[0])
            valid = (positions < m_ref[sequence]).astype(wide)
            out_s[rows, :] = (x2[rows, :] * valid).astype(low)
        leaving = [pltpu.make_async_copy(out_s, out_hbm, out_semaphores.at[0])]
        leaving[-1].start()
        scale = lax.rsqrt(jnp.mean(x1 * x1, axis=-1, keepdims=True) + 1e-06)
        normed = x1 * scale
        scaled = dh_s[...] * g_ref[2:3, :]
        d_x1 = e_ref[...].astype(wide) + scale * (
            scaled - normed * jnp.mean(scaled * normed, axis=-1, keepdims=True)
        )
        dh_s[...] = d_x1
        leaving.append(pltpu.make_async_copy(dh_s, dx1_hbm, out_semaphores.at[1]))
        leaving[-1].start()
        d_1 = mid_s.at[:, pl.ds(0, width)]
        d_1[...] = d_x1.astype(low)
        d_mixed = mid_s.at[:, pl.ds(width, width)]
        d_mixed[...] = mm_nt(d_1[...], wo_s[...]).astype(low)
        leaving.append(pltpu.make_async_copy(d_mixed, don_hbm, out_semaphores.at[2]))
        leaving[-1].start()
        rows = stride - down_rows
        grad_o = mm_tn(on_s[...], d_1[...]).astype(low)
        down_w[pl.ds(0, width), :] = grad_o
        for columns, held, out in ((mine, gdm_s, gdm_hbm), (other, gdo_s, gdo_hbm)):
            for owner in range(count):
                target = slice(owner * stride + down_rows, (owner + 1) * stride)
                held[target, :] = down_w[owner * rows : (owner + 1) * rows, columns]
                copy = pltpu.make_async_copy(
                    held.at[target, :], out.at[target, :], out_semaphores.at[len(leaving)]
                )
                copy.start()
                leaving.append(copy)
        for owner in range(count):
            leaving += down_copies(owner)
        for copy in leaving:
            copy.wait()


def ffn(core, h2, h2t, errors, w_gu, w_d, x1, mixed, w_a, lengths, gains8, owners):
    count, width = h2.shape
    half = width // 2
    hidden = w_gu[0].shape[1]
    full = whole((count, width))
    in_tile = pl.BlockSpec((width, TILE_F), lambda j, _: (0, j))
    out_tile = pl.BlockSpec((TILE_F, half), lambda j, _: (j, 0))
    grad_tile = pl.BlockSpec((2, width, HEAD_DIM), lambda j, _: (0, 0, j))
    anywhere = pl.BlockSpec(memory_space=pl.ANY)
    down_shape = (owners[0] * owners[1], half)
    struct = jax.ShapeDtypeStruct
    vmem = pltpu.VMEM
    return pl.pallas_call(
        functools.partial(ffn_kernel, owners),
        grid_spec=pltpu.PrefetchScalarGridSpec(
            num_scalar_prefetch=1,
            grid=(hidden // TILE_F,),
            in_specs=[full, whole(h2t.shape), full, in_tile, in_tile, out_tile, out_tile]
            + [anywhere] * 5
            + [pl.BlockSpec(memory_space=pltpu.SMEM), whole((8, width))],
            out_specs=[grad_tile, grad_tile] + [anywhere] * 5,
            scratch_shapes=[
                vmem((width, 2 * TILE_F), low),
                vmem((width, 2 * TILE_F), low),
                vmem((TILE_F, width), low),
                vmem((hidden, width), low),
                vmem((count, hidden), low),
                vmem((count, width), wide),
                vmem((count, width), low),
                vmem((count, width), wide),
                vmem((width, width), low),
                vmem((count, width), low),
                vmem(down_shape, low),
                vmem(down_shape, low),
                pltpu.SemaphoreType.DMA((5,)),
                pltpu.SemaphoreType.DMA((3 + 2 * owners[0],)),
                pltpu.SemaphoreType.DMA((2, owners[0])),
            ],
        ),
        out_shape=[struct((2, width, hidden // 2), low)] * 2
        + [struct(down_shape, low)] * 2
        + [
            struct((count, width), low),
            struct((count, width), wide),
            struct((count, width), low),
        ],
        compiler_params=pltpu.CompilerParams(vmem_limit_bytes=VMEM_BYTES),
        cost_estimate=pl.CostEstimate(
            flops=18 * count * width * hidden,
            bytes_accessed=count * width * 20 + width * hidden * 12,
            transcendentals=count * hidden,
        ),
        name="ffn",
    )(core, h2, h2t, errors, *w_gu, *w_d, x1, *mixed, *w_a, lengths, gains8)


def mixer_backward_kernel(
    slot,
    per_half,
    first,
    half_ref,
    nt_hbm,
    g_ref,
    q_ref,
    f_ref,
    v_ref,
    o_ref,
    don_ref,
    *outs,
):
    grad_ref, dpre_hbm, nt_s, dpre_ref, semaphores = outs[-5:]
    fetch = pltpu.make_async_copy(nt_hbm, nt_s, semaphores.at[0])
    fetch.start()
    gain_o = g_ref[1:2, lanes_of(half_ref[0] * per_half + first + pl.program_id(0), PAIR)]
    lower_ones = triangle(slot, True)
    upper_ones = triangle(slot, False)
    causal_t = causal_mask(slot, False)
    for sequence in range(q_ref.shape[0] // slot):
        rows = slice(sequence * slot, (sequence + 1) * slot)
        d_on = don_ref[rows, :].astype(wide)
        out = o_ref[rows, :].astype(wide)
        d_out_parts = []
        for head in range(2):
            lanes = slice(head * HEAD_DIM, (head + 1) * HEAD_DIM)
            out_h, d_on_h = out[:, lanes], d_on[:, lanes]
            scale = lax.rsqrt(jnp.mean(out_h * out_h, axis=-1, keepdims=True) + 1e-05)
            normed = out_h * scale
            scaled = d_on_h * gain_o[:, lanes]
            inner = jnp.mean(scaled * normed, axis=-1, keepdims=True)
            d_out_parts.append((scale * (scaled - normed * inner)).astype(low))

        q_pre = q_ref[rows, :]
        share, gate, keys_in, cumulative = decay_parts(f_ref[rows, :], lower_ones)
        grown = jnp.exp(-cumulative)
        shrunk = jnp.exp(cumulative)
        q_share = sigmoid(q_pre)
        decayed_q = (q_pre * q_share * shrunk).astype(low)
        grown_k = (keys_in * grown).astype(low)
        values = v_ref[rows, :]
        dq_parts, dk_parts, dv_parts = [], [], []
        for head in range(2):
            lanes = slice(head * HEAD_DIM, (head + 1) * HEAD_DIM)
            q_h, k_h, v_h = decayed_q[:, lanes], grown_k[:, lanes], values[:, lanes]
            d_out = d_out_parts[head]
            scores = jnp.where(causal_t, mm_nt(k_h, q_h), 0.0).astype(low)
            d_scores = jnp.where(causal_t, mm_nt(v_h, d_out), 0.0).astype(low)
            dv_parts.append(mm(scores, d_out))
            dk_parts.append(mm(d_scores, q_h))
            dq_parts.append(mm_tn(d_scores, k_h))
        d_decayed = jnp.concatenate(dq_parts, axis=1)
        d_grown = jnp.concatenate(dk_parts, axis=1)
        d_value = jnp.concatenate(dv_parts, axis=1)
        d_cumulative = decayed_q.astype(wide) * d_decayed - grown_k.astype(wide) * d_grown
        d_log = split_sum(upper_ones, d_cumulative)
        d_query = d_decayed * shrunk
        d_key = d_grown * grown
        d_q_pre = d_query * q_share * (1.0 + q_pre * (1.0 - q_share))
        d_f_pre = (1.0 - lower_bound) * (d_log / gate - d_key) * share * (1.0 - share)
        dpre_ref[rows, :PAIR] = d_q_pre.astype(low)
        dpre_ref[rows, PAIR : 2 * PAIR] = d_f_pre.astype(low)
        dpre_ref[rows, 2 * PAIR :] = d_value.astype(low)

    columns = pl.ds(first * 3 * PAIR, 3 * PAIR)
    leaving = pltpu.make_async_copy(dpre_ref, dpre_hbm.at[:, columns], semaphores.at[1])
    leaving.start()
    fetch.wait()
    gain_column = g_ref[...].T[:, 0:1]
    grad = (mm(nt_s[...], dpre_ref[...]) * gain_column).astype(low)
    grad_ref[...] = grad.reshape(grad_ref.shape)
    leaving.wait()


def mixer_backward(half, n1t, gains8, kept, d_mixed, slot, shard, pairs=(0, 1), before=()):
    width, count = n1t.shape
    per_half = width // PAIR // 2
    first = pairs[0]
    by_pair = pl.BlockSpec((count, PAIR), lambda j, _: (0, first + j))
    from_whole = pl.BlockSpec((count, PAIR), lambda j, half: (0, half[0] * per_half + first + j))
    struct = jax.ShapeDtypeStruct
    return pl.pallas_call(
        functools.partial(mixer_backward_kernel, slot, per_half, first),
        grid_spec=pltpu.PrefetchScalarGridSpec(
            num_scalar_prefetch=1,
            grid=(len(pairs),),
            in_specs=[pl.BlockSpec(memory_space=pl.ANY), whole(gains8.shape)]
            + [by_pair] * 4
            + [from_whole]
            + [pl.BlockSpec(memory_space=pl.ANY)] * len(before),
            out_specs=[
                pl.BlockSpec(
                    (width // shard, 1, shard, 3 * PAIR), lambda j, _: (0, first + j, 0, 0)
                ),
                pl.BlockSpec(memory_space=pl.ANY),
            ],
            scratch_shapes=[
                pltpu.VMEM((width, count), low),
                pltpu.VMEM((count, 3 * PAIR), low),
                pltpu.SemaphoreType.DMA((2,)),
            ],
        ),
        out_shape=[
            struct((width // shard, per_half, shard, 3 * PAIR), low),
            struct((count, per_half * 3 * PAIR), low),
        ],
        input_output_aliases={8 + k: k for k in range(len(before))},
        compiler_params=pltpu.CompilerParams(vmem_limit_bytes=VMEM_BYTES),
        cost_estimate=pl.CostEstimate(
            flops=len(pairs) * (count * width * 6 * PAIR + 20 * count * slot * PAIR),
            bytes_accessed=len(pairs) * (count * width * 5 + width * PAIR * 6),
            transcendentals=len(pairs) * count * PAIR * 6,
        ),
        name="mixer_backward",
    )(half, n1t, gains8, *kept, d_mixed, *before)


def input_gradient_rows_kernel(
    x_ref, g_ref, dm_ref, do_ref, wm_ref, wo_ref, dx1_ref, dx_ref
):
    d_h1 = mm_nt(dm_ref[...], wm_ref[...]) + mm_nt(do_ref[...], wo_ref[...])
    normed, scale = first_norm(x_ref, None)
    scaled = d_h1 * g_ref[0:1, :]
    dx_ref[...] = dx1_ref[...] + scale * (
        scaled - normed * jnp.mean(scaled * normed, axis=-1, keepdims=True)
    )


def input_gradient(rows, gains8, d_pre, weights, d_x1):
    count, width = rows.shape
    block = count // 2
    columns = d_pre[0].shape[1]
    by_rows = lambda columns: pl.BlockSpec((block, columns), lambda j: (j, 0))
    weight_spec = pl.BlockSpec((width, columns), lambda j: (0, 0), pipeline_mode=pl.Buffered(1))
    return pl.pallas_call(
        input_gradient_rows_kernel,
        grid=(count // block,),
        in_specs=[by_rows(width), whole(gains8.shape)]
        + [by_rows(columns)] * 2
        + [weight_spec] * 2
        + [by_rows(width)],
        out_specs=by_rows(width),
        out_shape=jax.ShapeDtypeStruct((count, width), wide),
        compiler_params=pltpu.CompilerParams(vmem_limit_bytes=VMEM_BYTES),
        cost_estimate=pl.CostEstimate(
            flops=6 * count * width * width,
            bytes_accessed=count * width * 16 + width * width * 6,
            transcendentals=0,
        ),
        name="input_gradient",
    )(rows, gains8, *d_pre, *weights, d_x1)


def update(weight, momentum, average, gradient, step_rate):
    new_momentum = momentum_decay * momentum + gradient
    direction = gradient + momentum_decay * new_momentum + weight_decay * weight
    new_weight = weight - step_rate * direction
    new_average = average_decay * average + (1.0 - average_decay) * new_weight
    return (new_momentum, new_average, new_weight)


def update_kernel(pick, step_rate, sum_count, core_ref, w_ref, m_ref, a_ref, *refs):
    sums, outs, dots_ref = refs[:sum_count], refs[-4:-1], refs[-1]
    weight = w_ref[...]
    gradient = pick(core_ref[0], *[s[...] for s in sums]).astype(wide).reshape(weight.shape)
    results = update(weight, m_ref[...], a_ref[...], gradient, step_rate)
    for out, result in zip(outs, results):
        out[...] = result
    product = weight.astype(low).astype(wide) * gradient
    total = product[..., :HEAD_DIM]
    for start in range(HEAD_DIM, product.shape[-1], HEAD_DIM):
        total = total + product[..., start : start + HEAD_DIM]
    dots_ref[...] = total.reshape(dots_ref.shape)


def update_call(
    core, state, sums, grid, state_spec, sum_specs, pick, step_rate, name, before=()
):
    struct = jax.ShapeDtypeStruct(state[0].shape, wide)
    size = math.prod(state[0].shape)
    rows = state_spec.block_shape[-2]
    steps = math.prod(grid)
    tail = grid[1:]

    def dots_index(*indices):
        place = indices[0]
        for length, index in zip(tail, indices[1:]):
            place = place * length + index
        return (place, 0, 0)

    return pl.pallas_call(
        functools.partial(update_kernel, pick, step_rate, len(sums)),
        grid_spec=pltpu.PrefetchScalarGridSpec(
            num_scalar_prefetch=1,
            grid=grid,
            in_specs=[state_spec] * 3
            + sum_specs
            + [pl.BlockSpec(memory_space=pl.ANY)] * len(before),
            out_specs=[state_spec] * 3 + [pl.BlockSpec((1, rows, HEAD_DIM), dots_index)],
        ),
        out_shape=[struct] * 3 + [jax.ShapeDtypeStruct((steps, rows, HEAD_DIM), wide)],
        input_output_aliases={4 + len(sums) + k: k for k in range(len(before))},
        compiler_params=pltpu.CompilerParams(vmem_limit_bytes=VMEM_BYTES),
        cost_estimate=pl.CostEstimate(flops=12 * size, bytes_accessed=26 * size, transcendentals=0),
        name=name,
    )(core, *state, *sums, *before)


def update_attention_kernel(
    pick, step_rate, gain_step, core_ref, w_ref, m_ref, a_ref, qfv_ref, out_ref, *refs
):
    if gain_step is None:
        update_kernel(pick, step_rate, 2, core_ref, w_ref, m_ref, a_ref, qfv_ref, out_ref, *refs)
        return
    *held, dots_s = refs
    own_dots, up_dots, gate_dots, g_ref, gm_ref, ga_ref = held[:6]
    outs, gain_outs = held[-6:-3], held[-3:]
    kind = pl.program_id(0)
    dots = dots_s.at[kind]
    update_kernel(
        pick, step_rate, 2, core_ref, w_ref, m_ref, a_ref, qfv_ref, out_ref, *outs, dots
    )

    @pl.when(kind == pl.num_programs(0) - 1)
    def _():
        shard = dots_s.shape[1]
        sums = [own_dots[k] + dots_s[k] for k in range(4)]
        two = (up_dots[...] + gate_dots[...]).reshape(shard, HEAD_DIM)
        columns = [
            jnp.sum(total, axis=1, keepdims=True) for total in (sums[0] + sums[1] + sums[2], sums[3], two)
        ]
        lanes = lax.broadcasted_iota(jnp.int32, (shard, HEAD_DIM), 1)
        table = jnp.where(lanes == 1, columns[1], columns[2])
        table = jnp.where(lanes == 0, columns[0], table)
        gain = g_ref[...]
        gradient = table.T[:3, :] / gain.astype(low).astype(wide)
        results = update(gain, gm_ref[...], ga_ref[...], gradient, gain_step)
        for out, result in zip(gain_outs, results):
            out[...] = result


def update_attention(half_ref, state, qfv, out, step_rate, gains=None):
    _, shard, width = state[0].shape
    down_rows = out.shape[0] - shard

    def pick(core_index, proj, last):
        gradient = last[down_rows:].astype(wide)
        for kind in range(3):
            parts = [proj[pair * shard :, kind * PAIR :][:shard, :PAIR] for pair in range(2)]
            chosen = jnp.concatenate(parts, axis=1).astype(wide)
            gradient = jnp.where(pl.program_id(0) == kind, chosen, gradient)
        return gradient

    struct = jax.ShapeDtypeStruct
    state_spec = pl.BlockSpec((1, shard, width // 2), lambda kind, half: (kind, 0, half[0]))
    in_specs = [state_spec] * 3 + [whole(qfv.shape), whole(out.shape)]
    out_specs = [state_spec] * 3
    out_shape = [struct(state[0].shape, wide)] * 3
    operands = [half_ref, *state, qfv, out]
    aliases, scratch, gain_step = {}, [], None
    if gains is None:
        out_specs += [pl.BlockSpec((1, shard, HEAD_DIM), lambda kind, half: (kind, 0, 0))]
        out_shape += [struct((4, shard, HEAD_DIM), wide)]
    else:
        before, dots, gain_state, gain_step = gains
        in_specs += [whole(part.shape) for part in (*dots, *gain_state)]
        operands += [*dots, *gain_state]
        aliases = {len(operands) + k: k for k in range(3)}
        in_specs += [pl.BlockSpec(memory_space=pl.ANY)] * 3
        operands += list(before)
        out_specs += [whole(gain_state[0].shape)] * 3
        out_shape += [struct(gain_state[0].shape, wide)] * 3
        scratch = [pltpu.VMEM((4, shard, HEAD_DIM), wide)]
    size = math.prod(state[0].shape) // 2
    return pl.pallas_call(
        functools.partial(update_attention_kernel, pick, step_rate, gain_step),
        grid_spec=pltpu.PrefetchScalarGridSpec(
            num_scalar_prefetch=1,
            grid=(4,),
            in_specs=in_specs,
            out_specs=out_specs,
            scratch_shapes=scratch,
        ),
        out_shape=out_shape,
        input_output_aliases=aliases,
        compiler_params=pltpu.CompilerParams(vmem_limit_bytes=VMEM_BYTES),
        cost_estimate=pl.CostEstimate(flops=12 * size, bytes_accessed=26 * size, transcendentals=0),
        name="update_attention",
    )(*operands)


def update_ffn_in(kind_ref, state, totals, step_rate, before):
    _, shard, hidden = state[0].shape
    block = shard // 2

    def pick(_, even, odd):
        blocks = []
        for start in range(0, hidden // 2, HEAD_DIM):
            blocks += [even[:, start : start + HEAD_DIM], odd[:, start : start + HEAD_DIM]]
        return jnp.concatenate(blocks, axis=1)

    return update_call(
        kind_ref,
        state,
        totals,
        (2,),
        pl.BlockSpec((1, block, hidden), lambda j, kind: (kind[0], j, 0)),
        [pl.BlockSpec((block, hidden // 2), lambda j, _: (j, 0))] * 2,
        pick,
        step_rate,
        "update_ffn_in",
        before,
    )


def update_ffn_out(core, state, sums, step_rate):
    shard, width = state[0].shape

    def pick(core_index, mine, other):
        own = pl.program_id(0) == core_index
        return jnp.where(own, mine[:shard].astype(wide), other[:shard].astype(wide))

    return update_call(
        core,
        state,
        sums,
        (2,),
        pl.BlockSpec((shard, width // 2), lambda j, _: (0, j)),
        [whole(total.shape) for total in sums],
        pick,
        step_rate,
        "update_ffn_out",
    )


def pack_kernel(core_ref, w_ref, out_ref):
    half = w_ref.shape[2]
    for pair in range(half // PAIR):
        for kind in range(3):
            start = (pair * 3 + kind) * PAIR
            piece = w_ref[kind, :, pair * PAIR : (pair + 1) * PAIR]
            out_ref[:, start : start + PAIR] = piece.astype(low)
    out_ref[:, 3 * half : 4 * half] = w_ref[3].astype(low)


def pack_attention(core, weights):
    _, shard, width = weights.shape
    half = width // 2
    return pl.pallas_call(
        pack_kernel,
        grid_spec=pltpu.PrefetchScalarGridSpec(
            num_scalar_prefetch=1,
            grid=(1,),
            in_specs=[pl.BlockSpec((4, shard, half), lambda j, core: (0, 0, core[0]))],
            out_specs=whole((shard, 4 * half)),
        ),
        out_shape=jax.ShapeDtypeStruct((shard, 4 * half), low),
        name="pack_attention",
    )(core, weights)


RING = 8


def ring_place(index):
    return jnp.where(index % 2 == 0, index // 2, RING - 1 - index // 2)


def ring_member(place):
    place = place % RING
    return jnp.where(place < RING // 2, 2 * place, 2 * RING - 1 - 2 * place)


CYCLE = (0, 2, 4, 6, 7, 5, 3, 1)


def ring_next(tensor):
    replicas = lax.axis_size("dp")
    pairs = []
    for place_of, member in enumerate(CYCLE):
        for replica in range(replicas):
            target = CYCLE[(place_of + (1 if replica % 2 == 0 else -1)) % RING]
            pairs.append((member * replicas + replica, target * replicas + replica))
    return lax.ppermute(tensor, ("fsdp", "dp"), pairs)


def ring_shift(tensor, way):
    pairs = [(member, CYCLE[(at + way) % RING]) for at, member in enumerate(CYCLE)]
    return lax.ppermute(tensor, "fsdp", pairs)


def core_swap(tensor):
    return lax.ppermute(tensor, "dp", [(d, d ^ 1) for d in range(lax.axis_size("dp"))])


def column_swap(tensor):
    return lax.ppermute(tensor, "dp", [(d, d ^ 2) for d in range(lax.axis_size("dp"))])


def pack_all_kernel(
    core_ref, column_ref, w_ref, up_ref, other_ref, down_ref, g_ref, out_ref, across_ref
):
    across_ref[...] = other_ref[0].astype(low)
    shard = w_ref.shape[1]
    half = w_ref.shape[2]
    for pair in range(half // PAIR):
        for kind in range(3):
            start = (pair * 3 + kind) * PAIR
            piece = w_ref[kind, :, pair * PAIR : (pair + 1) * PAIR]
            out_ref[:, start : start + PAIR] = piece.astype(low)
    out_ref[:, 3 * half : 4 * half] = w_ref[3].astype(low)
    start = 4 * half
    out_ref[:, start : start + up_ref.shape[2]] = up_ref[0].astype(low)
    start += up_ref.shape[2]
    for first, count in down_parts(down_ref.shape[0], shard):
        out_ref[:count, start : start + half] = down_ref[first : first + count, :].astype(low)
        if count < shard:
            out_ref[count:, start : start + half] = jnp.zeros((shard - count, half), low)
            rows = lax.broadcasted_iota(jnp.int32, (GAIN_ROWS, g_ref.shape[1]), 0)
            gains = jnp.where(rows == 1, g_ref[1:2, :], g_ref[2:3, :])
            gains = jnp.where(rows == 0, g_ref[0:1, :], gains)
            gains = jnp.where(rows < 3, gains, 0.0).astype(low)
            out_ref[count : count + GAIN_ROWS, start : start + g_ref.shape[1]] = gains
        start += half


def down_parts(down_rows, shard):
    return [(start, min(shard, down_rows - start)) for start in range(0, down_rows, shard)]


def pack_all(core, column, weights, up, down, gains):
    _, shard, width = weights.shape
    half = width // 2
    parts = len(down_parts(down.shape[0], shard))
    columns = 4 * half + up.shape[2] // 2 + parts * half
    return pl.pallas_call(
        pack_all_kernel,
        grid_spec=pltpu.PrefetchScalarGridSpec(
            num_scalar_prefetch=2,
            grid=(1,),
            in_specs=[
                pl.BlockSpec((4, shard, half), lambda j, core, column: (0, 0, core[0])),
                pl.BlockSpec(
                    (1, shard, up.shape[2] // 2), lambda j, core, column: (core[0], 0, column[0])
                ),
                pl.BlockSpec(
                    (1, shard, up.shape[2] // 2),
                    lambda j, core, column: (core[0], 0, 1 - column[0]),
                ),
                pl.BlockSpec((down.shape[0], half), lambda j, core, column: (0, core[0])),
                whole(gains.shape),
            ],
            out_specs=[whole((shard, columns)), whole((shard, up.shape[2] // 2))],
        ),
        out_shape=[
            jax.ShapeDtypeStruct((shard, columns), low),
            jax.ShapeDtypeStruct((shard, up.shape[2] // 2), low),
        ],
        compiler_params=pltpu.CompilerParams(vmem_limit_bytes=VMEM_BYTES),
        name="pack_all",
    )(core, column, weights, up, up, down, gains)


def place_kernel(which, kept, shapes, origin_ref, column_ref, *refs):
    pieces, outs, semaphores = refs[: len(which)], refs[-1 - len(kept) : -1], refs[-1]
    targets = dict(zip(kept, outs))
    shard, first, up_columns, down_rows, half = shapes
    copies = []

    def copy(source, target):
        copies.append(pltpu.make_async_copy(source, target, semaphores.at[len(copies)]))

    for piece, (origin, across) in zip(pieces, which):
        owner = origin_ref[origin]
        rows = pl.ds(pl.multiple_of(owner * shard, 16), shard)
        if across:
            copy(piece, targets[1].at[rows, lanes_of(1 - column_ref[0], up_columns)])
            continue
        copy(piece.at[:, pl.ds(0, first)], targets[0].at[rows, :])
        own = targets[1].at[rows, lanes_of(column_ref[0], up_columns)]
        copy(piece.at[:, pl.ds(first, up_columns)], own)
        lane = first + up_columns
        for start, count in down_parts(down_rows, shard):
            target = pl.ds(pl.multiple_of(owner * down_rows + start, 16), count)
            copy(piece.at[pl.ds(0, count), pl.ds(lane, half)], targets[2].at[target, :])
            if count < shard:
                source = piece.at[pl.ds(count, GAIN_ROWS), pl.ds(lane, shard)]
                copy(source, targets[3].at[:, lanes_of(owner, shard)])
            lane += half
    for one in copies:
        one.start()
    for one in copies:
        one.wait()


def place(origins, column, which, pieces, arrays, kept, shapes):
    anywhere = pl.BlockSpec(memory_space=pl.ANY)
    shard, first, up_columns, down_rows, half = shapes
    kinds = [(RING * shard, first), (RING * shard, 2 * up_columns), (RING * down_rows, half)]
    kinds.append((GAIN_ROWS, RING * shard))
    held = [] if arrays is None else list(arrays)
    size = sum(math.prod(piece.shape) for piece in pieces)
    before = 2 + len(pieces)
    return pl.pallas_call(
        functools.partial(place_kernel, which, kept, shapes),
        grid_spec=pltpu.PrefetchScalarGridSpec(
            num_scalar_prefetch=2,
            grid=(1,),
            in_specs=[whole(piece.shape) for piece in pieces] + [anywhere] * len(held),
            out_specs=[anywhere] * len(kept),
            scratch_shapes=[pltpu.SemaphoreType.DMA((8 * len(pieces),))],
        ),
        out_shape=[jax.ShapeDtypeStruct(kinds[k], pieces[0].dtype) for k in kept],
        input_output_aliases={before + k: k for k in range(len(held))},
        compiler_params=pltpu.CompilerParams(vmem_limit_bytes=VMEM_BYTES),
        cost_estimate=pl.CostEstimate(flops=0, bytes_accessed=8 * size, transcendentals=0),
        name="place",
    )(origins, column, *pieces, *held)


def after(tensor, *others):
    return lax.optimization_barrier((tensor, *others))[0]


def core_way():
    return 1 - 2 * (lax.axis_index("dp") % 2)


def ring_origins():
    steps = jnp.array((0, -1, -2, -3, -4, 1, 2, 3), jnp.int32)
    return ring_member(ring_place(lax.axis_index("fsdp")) + steps + RING).astype(jnp.int32)


class RingSumOverColumns:
    def __init__(self, mine, arrived):
        self.arrays = (mine, arrived)
        place = ring_place(lax.axis_index("fsdp"))
        self.rows = mine.shape[1] // RING
        self.starts = [
            ring_member(place - core_way() * (s + 1) + 2 * RING) * self.rows for s in range(RING)
        ]
        self.sent, self.came, self.totals = [], [], []

    def part(self, side, step):
        shape = (1, self.rows, self.arrays[0].shape[2])
        parts = [
            lax.dynamic_slice(array, (side, self.starts[step], 0), shape)[0]
            for array in self.arrays
        ]
        return parts[0].astype(wide) + parts[1].astype(wide)

    def cross(self):
        self.sent.append(self.part(1, len(self.sent)).astype(low))
        self.came.append(column_swap(self.sent[-1]))

    def term(self):
        step = len(self.totals)
        return self.part(0, step) + self.came[step].astype(wide)

    def begin(self, *others):
        self.came[0] = after(self.came[0], *others) if others else self.came[0]
        self.totals.append(self.term().astype(low))

    def step(self, arriving=()):
        total, ahead = self.totals[-1], self.came[len(self.totals)]
        moved = ring_next(after(total, ahead) if len(self.totals) > 1 else total)
        moved = after(moved, *arriving) if arriving else moved
        self.totals.append((moved.astype(wide) + self.term()).astype(low))

    def last(self):
        return self.totals[-1]


class RingSum:
    def __init__(self, mine, arrived):
        self.mine, self.arrived = mine, arrived
        place = ring_place(lax.axis_index("fsdp"))
        self.owners = [ring_member(place - core_way() * (s + 1) + 2 * RING) for s in range(RING)]
        self.totals = []

    def term(self):
        parts = []
        for own, arrived in zip(self.mine, self.arrived):
            rows = own.shape[0] // RING
            start = self.owners[len(self.totals)] * rows
            part = lax.dynamic_slice_in_dim(own, start, rows, 0).astype(wide)
            parts.append(part + lax.dynamic_slice_in_dim(arrived, start, rows, 0).astype(wide))
        return parts[0] if len(parts) == 1 else jnp.concatenate(parts, axis=0)

    def begin(self, *others):
        if others:
            self.mine = [after(self.mine[0], *others), *self.mine[1:]]
        self.totals.append(self.term().astype(low))

    def step(self, *before, arriving=()):
        total = self.totals[-1]
        moved = ring_next(after(total, *before) if before else total)
        moved = after(moved, *arriving) if arriving else moved
        self.totals.append((moved.astype(wide) + self.term().astype(wide)).astype(low))

    def last(self):
        return self.totals[-1]


def gather_rows(shard):
    mine = lax.all_gather(shard, "fsdp", axis=0, tiled=True)
    return mine, core_swap(mine)


def core_sum(mine, other):
    return (mine.astype(wide) + core_swap(other).astype(wide)).astype(low)


def scatter_rows(both):
    return lax.psum_scatter(both, "fsdp", scatter_dimension=0, tiled=True)


def over_columns(total):
    total = (total.astype(wide) + column_swap(total).astype(wide)).astype(low)
    return total, core_swap(total)


def on_device(
    inputs,
    cotangent,
    lengths,
    attention_weights,
    attention_momentum,
    attention_average,
    ffn_inputs,
    ffn_inputs_momentum,
    ffn_inputs_average,
    ffn_output,
    ffn_output_momentum,
    ffn_output_average,
    gains,
    gains_momentum,
    gains_average,
):
    micro_count, slot, width = inputs.shape
    hidden = ffn_inputs.shape[2]
    shard, down_rows = ffn_inputs.shape[1], ffn_output.shape[0]
    fsdp_size = lax.axis_size("fsdp")
    replicas = lax.axis_size("dp")
    ringed = fsdp_size == RING
    core = lax.axis_index("dp") % 2
    column = lax.axis_index("dp") // 2
    count = micro_count * slot
    half = width // 2
    core_ref = core.astype(jnp.int32).reshape(1)
    other_ref = 1 - core_ref
    column_ref = column.astype(jnp.int32).reshape(1)
    is_first = core == 0

    rows = inputs.reshape(count, width)
    n1t = norm_rows(rows)
    positions = jnp.arange(slot, dtype=jnp.int32)
    valid = (positions[None, :] < lengths).astype(wide).reshape(count, 1)
    errors = (cotangent.reshape(count, width).astype(wide) * valid).astype(low)

    if ringed:
        origins = ring_origins()
        first = 4 * half
        shapes = (shard, first, hidden // 2, down_rows, half)
        packed, own_across = pack_all(
            core_ref, column_ref, attention_weights, ffn_inputs, ffn_output, gains
        )
        wholes, there, which_there = None, [own_across], [(0, True)]
        here, which = [packed], [(0, False)]
        for step in range(1, 6):
            if step <= 3:
                onward = [ring_shift(here[0], 1), ring_shift(here[-1], -1)]
            elif step == 4:
                onward = [ring_next(jnp.where(is_first, *here))]
            across = []
            if step > 1:
                across = [column_swap(piece[:, first : first + hidden // 2]) for piece in here]
            wholes = place(
                origins, column_ref, which + which_there, here + there, wholes, (0, 1, 2, 3), shapes
            )
            if step == 5:
                break
            extra = [errors, n1t] if step == 2 else []
            tied = list(lax.optimization_barrier((*onward, *across, *wholes, *extra)))
            here, rest = tied[: len(onward)], tied[len(onward) :]
            there, wholes = rest[: len(across)], rest[len(across) : len(across) + 4]
            which_there = [(origin, True) for origin, _ in which] if across else []
            which = [(origin, False) for origin in [step, step + 4][: len(onward)]]
        w_a, gain_rows = (wholes[0], core_swap(wholes[0])), wholes[3]
    else:
        w_a = gather_rows(pack_attention(core_ref, attention_weights))
        gain_rows = lax.all_gather(gains.astype(low), "fsdp", axis=1, tiled=True)
        gain_rows = jnp.pad(gain_rows, ((0, GAIN_ROWS - 3), (0, 0)))
        w_gu = gather_rows(
            lax.dynamic_index_in_dim(ffn_inputs, core, 0, keepdims=False).astype(low)
        )
        w_d = gather_rows(lax.dynamic_slice_in_dim(ffn_output, core * half, half, 1).astype(low))
    mixed_mine, *kept_mine, gains8 = mixer_forward(core_ref, rows, w_a[0], slot, gain_rows)
    if ringed:
        (across,) = lax.optimization_barrier((*across, mixed_mine, w_a[1]))[:1]
        (w_gu_mine,) = place(origins, column_ref, [(4, True)], [across], [wholes[1]], (1,), shapes)
        wholes = [wholes[0], w_gu_mine, wholes[2], wholes[3]]
        rows = after(rows, *wholes[1:3])
        w_gu, w_d = [(array, core_swap(array)) for array in wholes[1:3]]
    mixed_other, *rest = mixer_forward(
        other_ref, rows, w_a[1], slot, None, (gains8, mixed_mine, w_a[0])
    )
    kept_other, (x1, h2, h2t) = rest[:4], rest[4:]
    owners = (RING, down_rows + shard, down_rows)
    if not ringed:
        owners = (1, hidden + width, hidden)
    places = jnp.concatenate([core_ref, column_ref])
    *grad_gu, gd_mine, gd_other, output, d_x1, d_mixed = ffn(
        places, h2, h2t, errors, w_gu, w_d, x1, (mixed_mine, mixed_other), w_a, lengths[:, 0], gains8, owners
    )

    gm, gu = grad_gu
    arrived_gu = core_swap(gu)
    mine_do, arrived_do = [gd_mine], [core_swap(gd_other)]
    by_owner = (fsdp_size * 2 * shard, 3 * PAIR)
    d_pre = []
    for call in range(4):
        from_half, kept = (other_ref, kept_other) if call < 2 else (core_ref, kept_mine)
        if ringed and call == 1:
            sum_gu = RingSumOverColumns(after(gm, d_pre[0]), arrived_gu)
            sum_gu.cross()
            sum_gu.cross()
            n1t = after(n1t, *sum_gu.sent)
        elif ringed and call > 1:
            sum_gu.cross()
            ahead = [sum_gu.came[2]] if call == 3 else []
            n1t = after(n1t, sum_gu.last(), sum_do.last(), sum_gu.sent[-1], *ahead)
        grads = mixer_backward(
            from_half,
            n1t,
            gains8,
            kept,
            d_mixed,
            slot,
            shard,
            (call % 2,),
            grads if call % 2 else (),
        )
        d_pre.append(grads[1])
        if call == 1:
            grad_other = grads[0]
            if ringed:
                sum_do = RingSum(mine_do, arrived_do)
                sum_do.begin(d_pre[-1])
                sum_gu.begin(d_pre[-1])
                grad_other = after(grad_other, sum_gu.last(), sum_do.last())
            arrived_qfv = [core_swap(grad_other.reshape(by_owner))]
        elif ringed and call > 1:
            sum_do.step(arriving=(d_pre[-1],))
            sum_gu.step(arriving=(d_pre[-1],))
    mine_qfv = [grads[0].reshape(by_owner)]

    def finish_input(*others):
        late = after(d_pre[3], *others) if others else d_pre[3]
        return input_gradient(rows, gains8, (late, d_pre[1]), w_a, d_x1)

    if ringed:
        sum_qfv = RingSum(mine_qfv, arrived_qfv)
        sum_qfv.begin()
        input_grad = None
        for step in range(1, RING - 1):
            if len(sum_gu.came) < RING:
                sum_gu.cross()
            if len(sum_gu.totals) < RING:
                first = [sum_gu.last(), sum_qfv.last()]
                sum_do.step(*{1: first, 4: [input_grad]}.get(step, []))
                sum_gu.step()
            sum_qfv.step()
            if step == 2:
                input_grad = finish_input(sum_qfv.last(), sum_gu.came[5])
        total_gu, total_do = sum_gu.last(), sum_do.last()
    else:
        both = (gm.astype(wide) + arrived_gu.astype(wide)).astype(low)
        here = (both[0].astype(wide) + column_swap(both[1]).astype(wide)).astype(low)
        total_gu = scatter_rows(here)
        both = (gd_mine.astype(wide) + arrived_do[0].astype(wide)).astype(low)
        total_do = jnp.concatenate(
            [scatter_rows(both[:hidden]), scatter_rows(both[hidden:])], axis=0
        )
        total_qfv = scatter_rows(
            (mine_qfv[0].astype(wide) + arrived_qfv[0].astype(wide)).astype(low)
        )
        input_grad = finish_input()
    scale_rows = 1.0 / math.sqrt(count * fsdp_size * replicas)
    matrix_step = matrix_rate * scale_rows
    attention_state = (attention_weights, attention_momentum, attention_average)
    ffn_in_state = (ffn_inputs, ffn_inputs_momentum, ffn_inputs_average)
    ffn_out_state = (ffn_output, ffn_output_momentum, ffn_output_average)
    sum_do = over_columns(total_do)
    there = column_swap(total_gu)
    even = jnp.where(column == 0, total_gu, there)
    odd = jnp.where(column == 0, there, total_gu)
    sum_gu = (even, odd), (core_swap(even), core_swap(odd))
    *new_out, _ = update_ffn_out(core_ref, ffn_out_state, sum_do, matrix_step)
    *new_in, dots_up = update_ffn_in(core_ref, ffn_in_state, sum_gu[0], matrix_step, ())
    *new_in, dots_gate = update_ffn_in(other_ref, ffn_in_state, sum_gu[1], matrix_step, new_in)
    if ringed:
        sum_qfv.step(arriving=(new_out[0],))
        total_qfv = sum_qfv.last()
    there = after(column_swap(total_qfv), new_in[0])
    sum_qfv = (total_qfv.astype(wide) + there.astype(wide)).astype(low)
    *own, dots_own = update_attention(
        core_ref, attention_state, sum_qfv, sum_do[0], matrix_step
    )
    theirs = after(core_swap(sum_qfv), own[0])
    gain_state = (gains, gains_momentum, gains_average)
    *new_attention, gains_m, gains_a, gains_w = update_attention(
        other_ref,
        attention_state,
        theirs,
        sum_do[1],
        matrix_step,
        (own, (dots_own, dots_up, dots_gate), gain_state, gain_rate * scale_rows),
    )
    return (
        output.reshape(micro_count, slot, width),
        input_grad.reshape(micro_count, slot, width),
        *new_attention,
        *new_in,
        *new_out,
        gains_m,
        gains_a,
        gains_w,
    )


def solution(mesh):
    rows_split = P(None, ("fsdp", "dp"), None)
    middle_split = P(None, "fsdp", None)
    first_split = P("fsdp", None)
    gains_split = P(None, "fsdp")
    in_specs = (
        (rows_split, rows_split, P(None, ("fsdp", "dp")))
        + (middle_split,) * 6
        + (first_split,) * 3
        + (gains_split,) * 3
    )
    out_specs = (
        (rows_split, rows_split)
        + (middle_split,) * 6
        + (first_split,) * 3
        + (gains_split,) * 3
    )
    return jax.shard_map(
        on_device, mesh=mesh, in_specs=in_specs, out_specs=out_specs, check_vma=False
    )
```

profile of v0, /device:TPU:0, one launch (start us, length us, event | category | flops | bytes accessed | tf_op | source)
XLA Modules:
  0.0 388.3 jit_solution(1658854180507729804)
XLA Ops:
  0.7 3.1 pack_all.1
  3.8 3.0 collective-permute-start
  7.3 3.3 place.6
  10.7 24.4 %collective-permute-done.refs_0_ = bf16[128,4992]{1,0:T(8,128)(2,1)S(1)} collective-permute-done((bf16[128,4992]{1,0:T(8,128)(2,1)}, bf16[128,4992]{1,0:T(8,128)(2,1)S(1)}, u32[]{:S(2)}, u32[]{:S(2)}) %collective-permute-start) | collective-permute-done | bytes 1277984 | tf_op jit(solution)/shard_map/ppermute | solution.py:854
  35.0 1.5 collective-permute-done.1.refs_1_
  37.6 1.6 collective-permute-start.2
  40.7 1.6 collective-permute-start.4
  42.8 3.4 norm_rows.1.nt_hbm
  46.2 2.9 fusion.e_ref
  49.1 3.9 %place.7 = (bf16[1024,2048]{1,0:T(8,128)(2,1)}, bf16[1024,2816]{1,0:T(8,128)(2,1)}, bf16[2816,512]{1,0:T(8,128)(2,1)}, bf16[16,1024]{1,0:T(8,128)(2,1)}) custom-call(s32[8]{0:T(128)} %compare_select_fusion.2.origin_ref, s32[1]{0:T(128)} %bitcast.1.column_ref, ...), custom_call_target="tpu_custom_call", output_to_operand_aliasing={{0}: (4, {}), {1}: (5, {}), {2}: (6, {}), {3}: (7, {})} | custom-call | bytes 10223616 | tf_op jit(solution)/shard_map/place/pallas_call | solution.py:969
  53.0 3.9 %collective-permute-done.5.refs_3_ = bf16[128,1408]{1,0:T(8,128)(2,1)} collective-permute-done((bf16[128,1408]{1,0:T(8,128)(2,1)S(1)}, bf16[128,1408]{1,0:T(8,128)(2,1)}, u32[]{:S(2)}, u32[]{:S(2)}) %collective-permute-start.5) | collective-permute-done | bytes 360480 | tf_op jit(solution)/shard_map/ppermute | solution.py:862
  57.0 9.4 %collective-permute-done.2.refs_0_ = bf16[128,4992]{1,0:T(8,128)(2,1)} collective-permute-done((bf16[128,4992]{1,0:T(8,128)(2,1)S(1)}, bf16[128,4992]{1,0:T(8,128)(2,1)}, u32[]{:S(2)}, u32[]{:S(2)}) %collective-permute-start.2) | collective-permute-done | bytes 1277984 | tf_op jit(solution)/shard_map/ppermute | solution.py:854
  66.3 1.4 collective-permute-done.3.refs_1_
  68.8 1.6 collective-permute-start.6
  72.8 1.6 collective-permute-start.8
  74.9 4.5 %place.8 = (bf16[1024,2048]{1,0:T(8,128)(2,1)}, bf16[1024,2816]{1,0:T(8,128)(2,1)}, bf16[2816,512]{1,0:T(8,128)(2,1)}, bf16[16,1024]{1,0:T(8,128)(2,1)}) custom-call(s32[8]{0:T(128)} %compare_select_fusion.2.origin_ref, s32[1]{0:T(128)} %bitcast.1.column_ref, ...), custom_call_target="tpu_custom_call", output_to_operand_aliasing={{0}: (6, {}), {1}: (7, {}), {2}: (8, {}), {3}: (9, {})} | custom-call | bytes 13107200 | tf_op jit(solution)/shard_map/place/pallas_call | solution.py:969
  79.4 4.7 %collective-permute-done.8.refs_2_ = bf16[128,1408]{1,0:T(8,128)(2,1)} collective-permute-done((bf16[128,1408]{1,0:T(8,128)(2,1)S(1)}, bf16[128,1408]{1,0:T(8,128)(2,1)}, u32[]{:S(2)}, u32[]{:S(2)}) %collective-permute-start.8) | collective-permute-done | bytes 360480 | tf_op jit(solution)/shard_map/ppermute | solution.py:862
  84.2 3.9 collective-permute-done.9.refs_3_
  88.0 8.5 %collective-permute-done.6.refs_0_ = bf16[128,4992]{1,0:T(8,128)(2,1)S(1)} collective-permute-done((bf16[128,4992]{1,0:T(8,128)(2,1)}, bf16[128,4992]{1,0:T(8,128)(2,1)S(1)}, u32[]{:S(2)}, u32[]{:S(2)}) %collective-permute-start.6) | collective-permute-done | bytes 1277984 | tf_op jit(solution)/shard_map/ppermute | solution.py:854
  99.1 1.8 collective-permute-start.10
  101.0 1.6 collective-permute-start.11
  103.1 4.5 %place.9 = (bf16[1024,2048]{1,0:T(8,128)(2,1)}, bf16[1024,2816]{1,0:T(8,128)(2,1)}, bf16[2816,512]{1,0:T(8,128)(2,1)}, bf16[16,1024]{1,0:T(8,128)(2,1)}) custom-call(s32[8]{0:T(128)} %compare_select_fusion.2.origin_ref, s32[1]{0:T(128)} %bitcast.1.column_ref, ...), custom_call_target="tpu_custom_call", output_to_operand_aliasing={{0}: (6, {}), {1}: (7, {}), {2}: (8, {}), {3}: (9, {})} | custom-call | bytes 13107200 | tf_op jit(solution)/shard_map/place/pallas_call | solution.py:969
  107.6 2.6 collective-permute-done.11.refs_1_
  110.2 4.0 %collective-permute-done.12.refs_2_ = bf16[128,1408]{1,0:T(8,128)(2,1)} collective-permute-done((bf16[128,1408]{1,0:T(8,128)(2,1)S(1)}, bf16[128,1408]{1,0:T(8,128)(2,1)}, u32[]{:S(2)}, u32[]{:S(2)}) %collective-permute-start.12) | collective-permute-done | bytes 360480 | tf_op jit(solution)/shard_map/ppermute | solution.py:862
  114.2 2.8 collective-permute-done.10.refs_0_
  116.9 3.6 place.10
  121.7 1.5 collective-permute-start.13
  123.2 9.9 %mixer_forward.2 = (bf16[768,512]{1,0:T(8,128)(2,1)}, f32[768,512]{1,0:T(8,128)}, f32[768,512]{1,0:T(8,128)}, bf16[768,512]{1,0:T(8,128)(2,1)}, bf16[768,512]{1,0:T(8,128)(2,1)}, /*index=5*/f32[8,1024]{1,0:T(8,128)}) custom-call(s32[1]{0:T(128)} %bitcast.core_ref.half_ref, bf16[768,1024]{1,0:T(8,128)(2,1)} %bitcast.82, ...), custom_call_target="tpu_custom_call" | custom-call | flops 6241124352 | bytes 13631488 | tf_op jit(solution)/shard_map/mixer_forward/pallas_call | solution.py:239
  133.9 2.7 place.11.wm_ref
  137.7 15.3 %mixer_forward.3 = (bf16[768,512]{1,0:T(8,128)(2,1)}, f32[768,512]{1,0:T(8,128)}, f32[768,512]{1,0:T(8,128)}, bf16[768,512]{1,0:T(8,128)(2,1)}, bf16[768,512]{1,...) custom-call(s32[1]{0:T(128)S(6)} %sub.55.half_ref.core_ref, ...), custom_call_target="tpu_custom_call" | custom-call | flops 6241124352 | bytes 13631488 | tf_op jit(solution)/shard_map/mixer_forward/pallas_call | solution.py:239
  153.1 58.1 %ffn.1 = (bf16[2,1024,1408]{2,1,0:T(8,128)(2,1)}, bf16[2,1024,1408]{2,1,0:T(8,128)(2,1)}, bf16[3840,512]{1,0:T(8,128)(2,1)}, bf16[3840,512]{1,0:T(8,128)(2,1)}, ...) custom-call(s32[2]{0:T(128)} %pad_add_fusion.core_ref, ...), custom_call_target="tpu_custom_call" | custom-call | flops 39862665216 | bytes 50331648 | tf_op jit(solution)/shard_map/ffn/pallas_call | solution.py:420
  211.7 8.6 %mixer_backward.4 = (bf16[8,2,128,768]{3,2,1,0:T(8,128)(2,1)}, bf16[768,1536]{1,0:T(8,128)(2,1)}) custom-call(s32[1]{0:T(128)S(6)} %sub.55.half_ref.core_ref, bf16[1024,768]{1,0:T(8,128)(2,1)} %norm_rows.1.nt_hbm, f32[8,1024]{1,0:T(8,128)} %get-tuple-element.194.g_ref, f32[768,512]{1,0:T(8,128)} %get-tuple-element.201.q_ref, ...), custom_call_target="tpu_custom_call" | custom-call | flops 2717908992 | bytes 5505024 | tf_op jit(solution)/shard_map/mixer_backward/pallas_call | solution.py:547
  221.0 4.3 %fusion.21 = (bf16[128,1408]{1,0:T(8,128)(2,1)}, bf16[128,1408]{1,0:T(8,128)(2,1)}, bf16[128,1408]{1,0:T(8,128)(2,1)}, bf16[128,1408]{1,0:T(8,128)(2,1)}, bf16[1...) fusion(bf16[2,1024,1408]{2,1,0:T(8,128)(2,1)} %collective-permu, ...), kind=kLoop, calls=%fused_computation.57 | loop fusion | flops 5767168 | bytes 8650784 | tf_op jit(solution)/shard_map/convert_element_type | solution.py:1018
  226.1 8.5 %mixer_backward.5 = (bf16[8,2,128,768]{3,2,1,0:T(8,128)(2,1)}, bf16[768,1536]{1,0:T(8,128)(2,1)}) custom-call(s32[1]{0:T(128)S(6)} %sub.55.half_ref.core_ref, bf16[1024,768]{1,0:T(8,128)(2,1)} %norm_rows.1.nt_hbm, f32[8,1024]{1,0:T(8,128)} %get-tuple-element.194.g_ref, ...), custom_call_target="tpu_custom_call", output_to_operand_aliasing={{0}: (8, {}), {1}: (9, {})} | custom-call | flops 2717908992 | bytes 5505024 | tf_op jit(solution)/shard_map/mixer_backward/pallas_call | solution.py:547
  237.3 1.6 collective-permute-start.22
  241.8 8.5 %mixer_backward.6 = (bf16[8,2,128,768]{3,2,1,0:T(8,128)(2,1)}, bf16[768,1536]{1,0:T(8,128)(2,1)}) custom-call(s32[1]{0:T(128)} %bitcast.core_ref.half_ref, bf16[1024,768]{1,0:T(8,128)(2,1)} %norm_rows.1.nt_hbm, f32[8,1024]{1,0:T(8,128)} %get-tuple-element.194.g_ref, f32[768,512]{1,0:T(8,128)} %get-tuple-element.217.q_ref, ...), custom_call_target="tpu_custom_call" | custom-call | flops 2717908992 | bytes 5505024 | tf_op jit(solution)/shard_map/mixer_backward/pallas_call | solution.py:547
  253.4 2.0 fusion.14
  255.4 2.5 collective-permute-done.23
  258.7 8.5 %mixer_backward.7 = (bf16[8,2,128,768]{3,2,1,0:T(8,128)(2,1)}, bf16[768,1536]{1,0:T(8,128)(2,1)}) custom-call(s32[1]{0:T(128)} %bitcast.core_ref.half_ref, bf16[1024,768]{1,0:T(8,128)(2,1)} %norm_rows.1.nt_hbm, f32[8,1024]{1,0:T(8,128)} %get-tuple-element.194.g_ref, ...), custom_call_target="tpu_custom_call", output_to_operand_aliasing={{0}: (8, {}), {1}: (9, {})} | custom-call | flops 2717908992 | bytes 5505024 | tf_op jit(solution)/shard_map/mixer_backward/pallas_call | solution.py:547
  267.2 2.5 add_convert_fusion.6
  270.4 2.0 add_convert_fusion.17
  273.0 2.2 fusion.12
  278.9 1.5 collective-permute-done.25
  282.1 3.6 collective-permute-done.35
  286.3 1.5 add_convert_fusion.5
  287.9 1.6 collective-permute-done.44
  290.3 2.1 fusion.10
  296.0 2.9 collective-permute-done.36
  301.0 11.6 %input_gradient.1 = f32[768,1024]{1,0:T(8,128)} custom-call(bf16[768,1024]{1,0:T(8,128)(2,1)} %bitcast.84, f32[8,1024]{1,0:T(8,128)} %get-tuple-element.194.g_ref, bf16[768,1536]{1,0:T(8,128)(2,1)} %get-tuple-element.230.dm_ref, bf16[768,1536]{1,0:T(8,128)(2,1)} %get-tuple-element.211.do_ref, bf16[1024,2048]{1,0:T(8,128)(2,1)} %get-tuple-element.187.w_ref.wom_hbm.wm_ref, ...), custom_call_target="tpu_custom_call" | custom-call | flops 4831838208 | bytes 18874368 | tf_op jit(solution)/shard_map/input_gradient/pallas_call | solution.py:600
  314.5 1.5 add_convert_fusion.3
  319.1 2.7 collective-permute-done.29
  323.5 3.6 collective-permute-done.38
  329.0 1.9 collective-permute-done.47
  332.8 2.4 collective-permute-done.30
  336.8 3.6 collective-permute-done.39
  346.2 2.3 collective-permute-done.31
  348.5 1.9 add_convert_fusion.11
  351.8 1.4 collective-permute-done.51
  353.2 2.1 fusion.2
  356.5 4.6 %update_ffn_out.1 = (f32[352,1024]{1,0:T(8,128)}, f32[352,1024]{1,0:T(8,128)}, f32[352,1024]{1,0:T(8,128)}, f32[2,352,128]{2,1,0:T(8,128)}) custom-call(s32[1]{0:T(128)} %bitcast.core_ref.half_ref, f32[352,1024]{1,0:T(8,128)} %w_ref.7, f32[352,1024]{1,0:T(8,128)} %m_ref.5, f32[352,1024]{1,0:T(8,128)} %a_ref.5, ...), custom_call_target="tpu_custom_call" | custom-call | flops 4325376 | bytes 9371648 | tf_op jit(solution)/shard_map/update_ffn_out/pallas_call | solution.py:656
  367.4 4.0 %update_ffn_in.2 = (f32[2,128,2816]{2,1,0:T(8,128)}, f32[2,128,2816]{2,1,0:T(8,128)}, f32[2,128,2816]{2,1,0:T(8,128)}, f32[2,64,128]{2,1,0:T(8,128)}) custom-call(s32[1]{0:T(128)} %bitcast.core_ref.half_ref, f32[2,128,2816]{2,1,0:T(8,128)} %w_ref.9, f32[2,128,2816]{2,1,0:T(8,128)} %m_ref.7, f32[2,128,2816]{2,1,0:T(8,128)} %a_ref.7, ...), custom_call_target="tpu_custom_call" | custom-call | flops 8650752 | bytes 18743296 | tf_op jit(solution)/shard_map/update_ffn_in/pallas_call | solution.py:656
  372.3 4.0 %update_ffn_in.3 = (f32[2,128,2816]{2,1,0:T(8,128)}, f32[2,128,2816]{2,1,0:T(8,128)}, f32[2,128,2816]{2,1,0:T(8,128)}, f32[2,64,128]{2,1,0:T(8,128)}) custom-call(s32[1]{0:T(128)S(6)} %sub.55.half_ref.core_ref, f32[2,128,2816]{2,1,0:T(8,128)} %w_ref.9, f32[2,128,2816]{2,1,0:T(8,128)} %m_ref.7, ...), custom_call_target="tpu_custom_call", output_to_operand_aliasing={{0}: (6, {}), {1}: (7, {}), {2}: (8, {})} | custom-call | flops 8650752 | bytes 18743296 | tf_op jit(solution)/shard_map/update_ffn_in/pallas_call | solution.py:656
  377.2 4.7 %update_attention.2 = (f32[4,128,1024]{2,1,0:T(8,128)}, f32[4,128,1024]{2,1,0:T(8,128)}, f32[4,128,1024]{2,1,0:T(8,128)}, f32[4,128,128]{2,1,0:T(8,128)}) custom-call(s32[1]{0:T(128)} %bitcast.core_ref.half_ref, f32[4,128,1024]{2,1,0:T(8,128)} %w_ref.11, f32[4,128,1024]{2,1,0:T(8,128)} %m_ref.9, f32[4,128,1024]{2,1,0:T(8,128)} %a_ref.9, ...), custom_call_target="tpu_custom_call" | custom-call | flops 3145728 | bytes 6815744 | tf_op jit(solution)/shard_map/update_attention/pallas_call | solution.py:740
  382.7 5.1 %update_attention.3 = (f32[4,128,1024]{2,1,0:T(8,128)}, f32[4,128,1024]{2,1,0:T(8,128)}, f32[4,128,1024]{2,1,0:T(8,128)}, f32[3,128]{1,0:T(4,128)}, f32[3,128]{1,0:T(4,128)}, /*index=5*/f32[3,128]{1,0:T(4,128)}) custom-call(s32[1]{0:T(128)S(6)} %sub.55.half_ref.core_ref, ...), custom_call_target="tpu_custom_call", output_to_operand_aliasing={{0}: (12, {}), {1}: (13, {}), {2}: (14, {})} | custom-call | flops 3145728 | bytes 6815744 | tf_op jit(solution)/shard_map/update_attention/pallas_call | solution.py:740
  (158 shorter events, 68.3 us)
Async XLA Ops:
  0.7 6.1 %copy-start.23 = (s32[8]{0:T(128)S(1)}, s32[8]{0:T(128)}, u32[]{:S(2)}) copy-start(s32[8]{0:T(128)} %constant.225.clone) | copy-start | bytes 100
  3.8 39.0 %copy-start.22 = (s32[2,1]{0,1:T(1,128)S(1)}, s32[2,1]{0,1:T(1,128)}, u32[]{:S(2)}) copy-start(s32[2,1]{0,1:T(1,128)} %param.18) | copy-start | bytes 28
  3.8 31.2 %collective-permute-start = (bf16[128,4992]{1,0:T(8,128)(2,1)}, bf16[128,4992]{1,0:T(8,128)(2,1)S(1)}, u32[]{:S(2)}, u32[]{:S(2)}) collective-permute-start(bf16[128,4992]{1,0:T(8,128)(2,1)} %get-tuple-element.140.refs_0_), channel_id=1, source_target_pairs={{0,8},{8,16},{16,24},{24,28},{28,20},{20,12},{12,4},{4,0},{1,9},{9... | collective-permute-start | bytes 3833864 | tf_op jit(solution)/shard_map/ppermute | solution.py:854
  6.8 29.7 %collective-permute-start.1 = (bf16[128,4992]{1,0:T(8,128)(2,1)}, bf16[128,4992]{1,0:T(8,128)(2,1)S(1)}, u32[]{:S(2)}, u32[]{:S(2)}) collective-permute-start(bf16[128,4992]{1,0:T(8,128)(2,1)} %get-tuple-element.140.refs_0_), channel_id=1, source_target_pairs={{0,4},{8,0},{16,8},{24,16},{28,24},{20,28},{12,20},{4,12},{1,5},{9... | collective-permute-start | bytes 3833864 | tf_op jit(solution)/shard_map/ppermute | solution.py:854
  35.0 14.1 %copy-start.5 = (bf16[128,4992]{1,0:T(8,128)(2,1)}, bf16[128,4992]{1,0:T(8,128)(2,1)S(1)}, u32[]{:S(2)}) copy-start(bf16[128,4992]{1,0:T(8,128)(2,1)S(1)} %collective-permute-done.refs_0_) | copy-start | bytes 3833860
  37.6 28.7 %collective-permute-start.2 = (bf16[128,4992]{1,0:T(8,128)(2,1)S(1)}, bf16[128,4992]{1,0:T(8,128)(2,1)}, u32[]{:S(2)}, u32[]{:S(2)}) collective-permute-start(bf16[128,4992]{1,0:T(8,128)(2,1)S(1)} %collective-permute-done.refs_0_), channel_id=1, source_target_pairs={{0,8},{8,16},{16,24},{24,28},{28,20},{20,12},{12,4},{4,0},{1,9},{9... | collective-permute-start | bytes 3833864 | tf_op jit(solution)/shard_map/ppermute | solution.py:854
  39.2 28.6 %collective-permute-start.3 = (bf16[128,4992]{1,0:T(8,128)(2,1)}, bf16[128,4992]{1,0:T(8,128)(2,1)S(1)}, u32[]{:S(2)}, u32[]{:S(2)}) collective-permute-start(bf16[128,4992]{1,0:T(8,128)(2,1)} %copy-done.6), channel_id=1, source_target_pairs={{0,4},{8,0},{16,8},{24,16},{28,24},{20,28},{12,20},{4,12},{1,5},{9... | collective-permute-start | bytes 3833864 | tf_op jit(solution)/shard_map/ppermute | solution.py:854
  40.7 12.4 %collective-permute-start.4 = (bf16[128,1408]{1,0:T(8,128)(2,1)S(1)}, bf16[128,1408]{1,0:T(8,128)(2,1)}, u32[]{:S(2)}, u32[]{:S(2)}) collective-permute-start(bf16[128,1408]{1,0:T(8,128)(2,1)S(1)} %slice.21), channel_id=1, source_target_pairs={{0,2},{1,3},{2,0},{3,1},{4,6},{5,7},{6,4},{7,5},{8,10},{9,11},{10,... | collective-permute-start | bytes 1081352 | tf_op jit(solution)/shard_map/ppermute | solution.py:862
  42.2 14.7 %collective-permute-start.5 = (bf16[128,1408]{1,0:T(8,128)(2,1)S(1)}, bf16[128,1408]{1,0:T(8,128)(2,1)}, u32[]{:S(2)}, u32[]{:S(2)}) collective-permute-start(bf16[128,1408]{1,0:T(8,128)(2,1)S(1)} %slice.22), channel_id=1, source_target_pairs={{0,2},{1,3},{2,0},{3,1},{4,6},{5,7},{6,4},{7,5},{8,10},{9,11},{10,... | collective-permute-start | bytes 1081352 | tf_op jit(solution)/shard_map/ppermute | solution.py:862
  68.8 27.7 %collective-permute-start.6 = (bf16[128,4992]{1,0:T(8,128)(2,1)}, bf16[128,4992]{1,0:T(8,128)(2,1)S(1)}, u32[]{:S(2)}, u32[]{:S(2)}) collective-permute-start(bf16[128,4992]{1,0:T(8,128)(2,1)} %collective-permute-done.2.refs_0_), channel_id=1, source_target_pairs={{0,8},{8,16},{16,24},{24,28},{28,20},{20,12},{12,4},{4,0},{1,9},{9... | collective-permute-start | bytes 3833864 | tf_op jit(solution)/shard_map/ppermute | solution.py:854
  70.3 27.5 %collective-permute-start.7 = (bf16[128,4992]{1,0:T(8,128)(2,1)}, bf16[128,4992]{1,0:T(8,128)(2,1)S(1)}, u32[]{:S(2)}, u32[]{:S(2)}) collective-permute-start(bf16[128,4992]{1,0:T(8,128)(2,1)} %copy-done.4), channel_id=1, source_target_pairs={{0,4},{8,0},{16,8},{24,16},{28,24},{20,28},{12,20},{4,12},{1,5},{9... | collective-permute-start | bytes 3833864 | tf_op jit(solution)/shard_map/ppermute | solution.py:854
  72.8 11.3 %collective-permute-start.8 = (bf16[128,1408]{1,0:T(8,128)(2,1)S(1)}, bf16[128,1408]{1,0:T(8,128)(2,1)}, u32[]{:S(2)}, u32[]{:S(2)}) collective-permute-start(bf16[128,1408]{1,0:T(8,128)(2,1)S(1)} %slice.23), channel_id=1, source_target_pairs={{0,2},{1,3},{2,0},{3,1},{4,6},{5,7},{6,4},{7,5},{8,10},{9,11},{10,... | collective-permute-start | bytes 1081352 | tf_op jit(solution)/shard_map/ppermute | solution.py:862
  74.4 13.6 %collective-permute-start.9 = (bf16[128,1408]{1,0:T(8,128)(2,1)S(1)}, bf16[128,1408]{1,0:T(8,128)(2,1)}, u32[]{:S(2)}, u32[]{:S(2)}) collective-permute-start(bf16[128,1408]{1,0:T(8,128)(2,1)S(1)} %slice.24), channel_id=1, source_target_pairs={{0,2},{1,3},{2,0},{3,1},{4,6},{5,7},{6,4},{7,5},{8,10},{9,11},{10,... | collective-permute-start | bytes 1081352 | tf_op jit(solution)/shard_map/ppermute | solution.py:862
  96.5 6.6 %copy-start.2 = (bf16[128,4992]{1,0:T(8,128)(2,1)}, bf16[128,4992]{1,0:T(8,128)(2,1)S(1)}, u32[]{:S(2)}) copy-start(bf16[128,4992]{1,0:T(8,128)(2,1)S(1)} %collective-permute-done.6.refs_0_) | copy-start | bytes 3833860
  99.1 17.8 %collective-permute-start.10 = (bf16[128,4992]{1,0:T(8,128)(2,1)}, bf16[128,4992]{1,0:T(8,128)(2,1)}, u32[]{:S(2)}, u32[]{:S(2)}) collective-permute-start(bf16[128,4992]{1,0:T(8,128)(2,1)} %broadcast_select_fusion), channel_id=1, source_target_pairs={{0,8},{1,5},{2,10},{3,7},{8,16},{9,1},{10,18},{11,3},{16,24},{17,9... | collective-permute-start | bytes 3833864 | tf_op jit(solution)/shard_map/ppermute | solution.py:849
  101.0 9.2 %collective-permute-start.11 = (bf16[128,1408]{1,0:T(8,128)(2,1)S(1)}, bf16[128,1408]{1,0:T(8,128)(2,1)S(1)}, u32[]{:S(2)}, u32[]{:S(2)}) collective-permute-start(bf16[128,1408]{1,0:T(8,128)(2,1)S(1)} %slice.25), channel_id=1, source_target_pairs={{0,2},{1,3},{2,0},{3,1},{4,6},{5,7},{6,4},{7,5},{8,10},{9,11},{10,... | collective-permute-start | bytes 1081352 | tf_op jit(solution)/shard_map/ppermute | solution.py:862
  102.5 11.7 %collective-permute-start.12 = (bf16[128,1408]{1,0:T(8,128)(2,1)S(1)}, bf16[128,1408]{1,0:T(8,128)(2,1)}, u32[]{:S(2)}, u32[]{:S(2)}) collective-permute-start(bf16[128,1408]{1,0:T(8,128)(2,1)S(1)} %slice.26), channel_id=1, source_target_pairs={{0,2},{1,3},{2,0},{3,1},{4,6},{5,7},{6,4},{7,5},{8,10},{9,11},{10,... | collective-permute-start | bytes 1081352 | tf_op jit(solution)/shard_map/ppermute | solution.py:862
  110.2 6.7 %copy-start.19 = (bf16[128,1408]{1,0:T(8,128)(2,1)}, bf16[128,1408]{1,0:T(8,128)(2,1)S(1)}, u32[]{:S(2)}) copy-start(bf16[128,1408]{1,0:T(8,128)(2,1)S(1)} %collective-permute-done.11.refs_1_) | copy-start | bytes 1081348
  120.6 12.6 %collective-permute-start.14 = (bf16[1024,2048]{1,0:T(8,128)(2,1)}, bf16[1024,2048]{1,0:T(8,128)(2,1)}, u32[]{:S(2)}, u32[]{:S(2)}) collective-permute-start(bf16[1024,2048]{1,0:T(8,128)(2,1)} %get-tuple-element.187.w_ref.wom_hbm.wm_ref), channel_id=1, source_target_pairs={{0,1},{1,0},{2,3},{3,2},{4,5},{5,4},{6,7},{7,6},{8,9},{9,8},{10,11... | collective-permute-start | bytes 12582920 | tf_op jit(solution)/shard_map/ppermute | solution.py:858
  121.7 11.5 %collective-permute-start.13 = (bf16[128,1408]{1,0:T(8,128)(2,1)S(1)}, bf16[128,1408]{1,0:T(8,128)(2,1)S(1)}, u32[]{:S(2)}, u32[]{:S(2)}) collective-permute-start(bf16[128,1408]{1,0:T(8,128)(2,1)S(1)} %slice.27), channel_id=1, source_target_pairs={{0,2},{1,3},{2,0},{3,1},{4,6},{5,7},{6,4},{7,5},{8,10},{9,11},{10,... | collective-permute-start | bytes 1081352 | tf_op jit(solution)/shard_map/ppermute | solution.py:862
  136.6 16.5 %collective-permute-start.15 = (bf16[1024,2816]{1,0:T(8,128)(2,1)}, bf16[1024,2816]{1,0:T(8,128)(2,1)}, u32[]{:S(2)}, u32[]{:S(2)}) collective-permute-start(bf16[1024,2816]{1,0:T(8,128)(2,1)} %place.11.wm_ref), channel_id=1, source_target_pairs={{0,1},{1,0},{2,3},{3,2},{4,5},{5,4},{6,7},{7,6},{8,9},{9,8},{10,11... | collective-permute-start | bytes 17301512 | tf_op jit(solution)/shard_map/ppermute | solution.py:858
  136.9 16.2 %collective-permute-start.16 = (bf16[2816,512]{1,0:T(8,128)(2,1)S(1)}, bf16[2816,512]{1,0:T(8,128)(2,1)}, u32[]{:S(2)}, u32[]{:S(2)}) collective-permute-start(bf16[2816,512]{1,0:T(8,128)(2,1)S(1)} %copy-done), channel_id=1, source_target_pairs={{0,1},{1,0},{2,3},{3,2},{4,5},{5,4},{6,7},{7,6},{8,9},{9,8},{10,11... | collective-permute-start | bytes 8650760 | tf_op jit(solution)/shard_map/ppermute | solution.py:858
  211.1 9.8 %collective-permute-start.17 = (bf16[2,1024,1408]{2,1,0:T(8,128)(2,1)}, bf16[2,1024,1408]{2,1,0:T(8,128)(2,1)}, u32[]{:S(2)}, u32[]{:S(2)}) collective-permute-start(bf16[2,1024,1408]{2,1,0:T(8,128)(2,1)} %get-tuple-element.208), channel_id=1, source_target_pairs={{0,1},{1,0},{2,3},{3,2},{4,5},{5,4},{6,7},{7,6},{8,9},{9,8},{10,11... | collective-permute-start | bytes 17301512 | tf_op jit(solution)/shard_map/ppermute | solution.py:858
  211.4 23.2 %collective-permute-start.19 = (bf16[3840,512]{1,0:T(8,128)(2,1)}, bf16[3840,512]{1,0:T(8,128)(2,1)}, u32[]{:S(2)}, u32[]{:S(2)}) collective-permute-start(bf16[3840,512]{1,0:T(8,128)(2,1)} %get-tuple-element.215), channel_id=1, source_target_pairs={{0,1},{1,0},{2,3},{3,2},{4,5},{5,4},{6,7},{7,6},{8,9},{9,8},{10,11... | collective-permute-start | bytes 11796488 | tf_op jit(solution)/shard_map/ppermute | solution.py:858
  225.2 10.7 %collective-permute-start.18 = (bf16[128,1408]{1,0:T(8,128)(2,1)S(1)}, bf16[128,1408]{1,0:T(8,128)(2,1)S(1)}, u32[]{:S(2)}, u32[]{:S(2)}) collective-permute-start(bf16[128,1408]{1,0:T(8,128)(2,1)S(1)} %get-tuple-element.273), channel_id=1, source_target_pairs={{0,2},{1,3},{2,0},{3,1},{4,6},{5,7},{6,4},{7,5},{8,10},{9,11},{10,... | collective-permute-start | bytes 1081352 | tf_op jit(solution)/shard_map/ppermute | solution.py:862
  237.2 32.5 %collective-permute-start.24 = (bf16[2048,768]{1,0:T(8,128)(2,1)}, bf16[2048,768]{1,0:T(8,128)(2,1)}, u32[]{:S(2)}, u32[]{:S(2)}) collective-permute-start(bf16[2048,768]{1,0:T(8,128)(2,1)} %bitcast.86), channel_id=1, source_target_pairs={{0,1},{1,0},{2,3},{3,2},{4,5},{5,4},{6,7},{7,6},{8,9},{9,8},{10,11... | collective-permute-start | bytes 9437192 | tf_op jit(solution)/shard_map/ppermute | solution.py:858
  237.3 13.0 %collective-permute-start.22 = (bf16[480,512]{1,0:T(8,128)(2,1)S(1)}, bf16[480,512]{1,0:T(8,128)(2,1)S(1)}, u32[]{:S(2)}, u32[]{:S(2)}) collective-permute-start(bf16[480,512]{1,0:T(8,128)(2,1)S(1)} %add_convert_fusion.8), channel_id=1, source_target_pairs={{0,8},{1,5},{2,10},{3,7},{8,16},{9,1},{10,18},{11,3},{16,24},{17,9... | collective-permute-start | bytes 1474568 | tf_op jit(solution)/shard_map/ppermute | solution.py:849
  238.9 14.6 %collective-permute-start.21 = (bf16[128,1408]{1,0:T(8,128)(2,1)S(1)}, bf16[128,1408]{1,0:T(8,128)(2,1)S(1)}, u32[]{:S(2)}, u32[]{:S(2)}) collective-permute-start(bf16[128,1408]{1,0:T(8,128)(2,1)S(1)} %get-tuple-element.272), channel_id=1, source_target_pairs={{0,2},{1,3},{2,0},{3,1},{4,6},{5,7},{6,4},{7,5},{8,10},{9,11},{10,... | collective-permute-start | bytes 1081352 | tf_op jit(solution)/shard_map/ppermute | solution.py:862
  240.0 17.9 %collective-permute-start.23 = (bf16[128,1408]{1,0:T(8,128)(2,1)S(1)}, bf16[128,1408]{1,0:T(8,128)(2,1)S(1)}, u32[]{:S(2)}, u32[]{:S(2)}) collective-permute-start(bf16[128,1408]{1,0:T(8,128)(2,1)S(1)} %get-tuple-element.271), channel_id=1, source_target_pairs={{0,2},{1,3},{2,0},{3,1},{4,6},{5,7},{6,4},{7,5},{8,10},{9,11},{10,... | collective-permute-start | bytes 1081352 | tf_op jit(solution)/shard_map/ppermute | solution.py:862
  240.9 12.0 %collective-permute-start.20 = (bf16[128,1408]{1,0:T(8,128)(2,1)S(1)}, bf16[128,1408]{1,0:T(8,128)(2,1)S(1)}, u32[]{:S(2)}, u32[]{:S(2)}) collective-permute-start(bf16[128,1408]{1,0:T(8,128)(2,1)S(1)} %fusion.15), channel_id=1, source_target_pairs={{0,8},{1,5},{2,10},{3,7},{8,16},{9,1},{10,18},{11,3},{16,24},{17,9... | collective-permute-start | bytes 1081352 | tf_op jit(solution)/shard_map/ppermute | solution.py:849
  250.3 27.4 %collective-permute-start.43 = (bf16[128,1408]{1,0:T(8,128)(2,1)}, bf16[128,1408]{1,0:T(8,128)(2,1)}, u32[]{:S(2)}, u32[]{:S(2)}) collective-permute-start(bf16[128,1408]{1,0:T(8,128)(2,1)} %get-tuple-element.270), channel_id=1, source_target_pairs={{0,2},{1,3},{2,0},{3,1},{4,6},{5,7},{6,4},{7,5},{8,10},{9,11},{10,... | collective-permute-start | bytes 1081352 | tf_op jit(solution)/shard_map/ppermute | solution.py:862
  252.9 14.3 %collective-permute-start.33 = (bf16[480,512]{1,0:T(8,128)(2,1)S(1)}, bf16[480,512]{1,0:T(8,128)(2,1)}, u32[]{:S(2)}, u32[]{:S(2)}) collective-permute-start(bf16[480,512]{1,0:T(8,128)(2,1)S(1)} %add_convert_fusion.7), channel_id=1, source_target_pairs={{0,8},{1,5},{2,10},{3,7},{8,16},{9,1},{10,18},{11,3},{16,24},{17,9... | collective-permute-start | bytes 1474568 | tf_op jit(solution)/shard_map/ppermute | solution.py:849
  257.9 11.7 %collective-permute-start.34 = (bf16[128,1408]{1,0:T(8,128)(2,1)}, bf16[128,1408]{1,0:T(8,128)(2,1)S(1)}, u32[]{:S(2)}, u32[]{:S(2)}) collective-permute-start(bf16[128,1408]{1,0:T(8,128)(2,1)} %fusion.14), channel_id=1, source_target_pairs={{0,8},{1,5},{2,10},{3,7},{8,16},{9,1},{10,18},{11,3},{16,24},{17,9... | collective-permute-start | bytes 1081352 | tf_op jit(solution)/shard_map/ppermute | solution.py:849
  267.2 13.8 %copy-start.1 = (bf16[8,2,128,768]{3,2,1,0:T(8,128)(2,1)S(1)}, bf16[8,2,128,768]{3,2,1,0:T(8,128)(2,1)}, u32[]{:S(2)}) copy-start(bf16[8,2,128,768]{3,2,1,0:T(8,128)(2,1)} %get-tuple-element.227) | copy-start | bytes 9437188
  272.4 8.0 %collective-permute-start.25 = (bf16[256,768]{1,0:T(8,128)(2,1)}, bf16[256,768]{1,0:T(8,128)(2,1)S(1)}, u32[]{:S(2)}, u32[]{:S(2)}) collective-permute-start(bf16[256,768]{1,0:T(8,128)(2,1)} %add_convert_fusion.17), channel_id=1, source_target_pairs={{0,8},{1,5},{2,10},{3,7},{8,16},{9,1},{10,18},{11,3},{16,24},{17,9... | collective-permute-start | bytes 1179656 | tf_op jit(solution)/shard_map/ppermute | solution.py:849
  275.2 10.5 %collective-permute-start.35 = (bf16[480,512]{1,0:T(8,128)(2,1)}, bf16[480,512]{1,0:T(8,128)(2,1)}, u32[]{:S(2)}, u32[]{:S(2)}) collective-permute-start(bf16[480,512]{1,0:T(8,128)(2,1)} %add_convert_fusion.6), channel_id=1, source_target_pairs={{0,8},{1,5},{2,10},{3,7},{8,16},{9,1},{10,18},{11,3},{16,24},{17,9... | collective-permute-start | bytes 1474568 | tf_op jit(solution)/shard_map/ppermute | solution.py:849
  275.7 16.8 %collective-permute-start.45 = (bf16[128,1408]{1,0:T(8,128)(2,1)}, bf16[128,1408]{1,0:T(8,128)(2,1)S(1)}, u32[]{:S(2)}, u32[]{:S(2)}) collective-permute-start(bf16[128,1408]{1,0:T(8,128)(2,1)} %get-tuple-element.266), channel_id=1, source_target_pairs={{0,2},{1,3},{2,0},{3,1},{4,6},{5,7},{6,4},{7,5},{8,10},{9,11},{10,... | collective-permute-start | bytes 1081352 | tf_op jit(solution)/shard_map/ppermute | solution.py:862
  276.8 18.6 %collective-permute-start.27 = (bf16[128,1408]{1,0:T(8,128)(2,1)}, bf16[128,1408]{1,0:T(8,128)(2,1)S(1)}, u32[]{:S(2)}, u32[]{:S(2)}) collective-permute-start(bf16[128,1408]{1,0:T(8,128)(2,1)} %get-tuple-element.269), channel_id=1, source_target_pairs={{0,2},{1,3},{2,0},{3,1},{4,6},{5,7},{6,4},{7,5},{8,10},{9,11},{10,... | collective-permute-start | bytes 1081352 | tf_op jit(solution)/shard_map/ppermute | solution.py:862
  277.7 54.5 %collective-permute-start.48 = (bf16[128,1408]{1,0:T(8,128)(2,1)}, bf16[128,1408]{1,0:T(8,128)(2,1)}, u32[]{:S(2)}, u32[]{:S(2)}) collective-permute-start(bf16[128,1408]{1,0:T(8,128)(2,1)} %get-tuple-element.268), channel_id=1, source_target_pairs={{0,2},{1,3},{2,0},{3,1},{4,6},{5,7},{6,4},{7,5},{8,10},{9,11},{10,... | collective-permute-start | bytes 1081352 | tf_op jit(solution)/shard_map/ppermute | solution.py:862
  280.4 9.1 %collective-permute-start.44 = (bf16[128,1408]{1,0:T(8,128)(2,1)}, bf16[128,1408]{1,0:T(8,128)(2,1)S(1)}, u32[]{:S(2)}, u32[]{:S(2)}) collective-permute-start(bf16[128,1408]{1,0:T(8,128)(2,1)} %fusion.12), channel_id=1, source_target_pairs={{0,8},{1,5},{2,10},{3,7},{8,16},{9,1},{10,18},{11,3},{16,24},{17,9... | collective-permute-start | bytes 1081352 | tf_op jit(solution)/shard_map/ppermute | solution.py:849
  285.7 8.0 %collective-permute-start.26 = (bf16[256,768]{1,0:T(8,128)(2,1)S(1)}, bf16[256,768]{1,0:T(8,128)(2,1)S(1)}, u32[]{:S(2)}, u32[]{:S(2)}) collective-permute-start(bf16[256,768]{1,0:T(8,128)(2,1)S(1)} %add_convert_fusion.16), channel_id=1, source_target_pairs={{0,8},{1,5},{2,10},{3,7},{8,16},{9,1},{10,18},{11,3},{16,24},{17,9... | collective-permute-start | bytes 1179656 | tf_op jit(solution)/shard_map/ppermute | solution.py:849
  289.5 9.5 %collective-permute-start.36 = (bf16[480,512]{1,0:T(8,128)(2,1)S(1)}, bf16[480,512]{1,0:T(8,128)(2,1)S(1)}, u32[]{:S(2)}, u32[]{:S(2)}) collective-permute-start(bf16[480,512]{1,0:T(8,128)(2,1)S(1)} %add_convert_fusion.5), channel_id=1, source_target_pairs={{0,8},{1,5},{2,10},{3,7},{8,16},{9,1},{10,18},{11,3},{16,24},{17,9... | collective-permute-start | bytes 1474568 | tf_op jit(solution)/shard_map/ppermute | solution.py:849
  292.5 8.6 %copy-start.15 = (bf16[128,1408]{1,0:T(8,128)(2,1)}, bf16[128,1408]{1,0:T(8,128)(2,1)S(1)}, u32[]{:S(2)}) copy-start(bf16[128,1408]{1,0:T(8,128)(2,1)S(1)} %collective-permute-done.45) | copy-start | bytes 1081348
  292.5 53.2 %collective-permute-start.50 = (bf16[128,1408]{1,0:T(8,128)(2,1)}, bf16[128,1408]{1,0:T(8,128)(2,1)}, u32[]{:S(2)}, u32[]{:S(2)}) collective-permute-start(bf16[128,1408]{1,0:T(8,128)(2,1)} %get-tuple-element.267), channel_id=1, source_target_pairs={{0,2},{1,3},{2,0},{3,1},{4,6},{5,7},{6,4},{7,5},{8,10},{9,11},{10,... | collective-permute-start | bytes 1081352 | tf_op jit(solution)/shard_map/ppermute | solution.py:862
  293.7 22.7 %collective-permute-start.46 = (bf16[128,1408]{1,0:T(8,128)(2,1)}, bf16[128,1408]{1,0:T(8,128)(2,1)}, u32[]{:S(2)}, u32[]{:S(2)}) collective-permute-start(bf16[128,1408]{1,0:T(8,128)(2,1)} %fusion.10), channel_id=1, source_target_pairs={{0,8},{1,5},{2,10},{3,7},{8,16},{9,1},{10,18},{11,3},{16,24},{17,9... | collective-permute-start | bytes 1081352 | tf_op jit(solution)/shard_map/ppermute | solution.py:849
  295.5 17.2 %collective-permute-start.28 = (bf16[256,768]{1,0:T(8,128)(2,1)S(1)}, bf16[256,768]{1,0:T(8,128)(2,1)}, u32[]{:S(2)}, u32[]{:S(2)}) collective-permute-start(bf16[256,768]{1,0:T(8,128)(2,1)S(1)} %add_convert_fusion.15), channel_id=1, source_target_pairs={{0,8},{1,5},{2,10},{3,7},{8,16},{9,1},{10,18},{11,3},{16,24},{17,9... | collective-permute-start | bytes 1179656 | tf_op jit(solution)/shard_map/ppermute | solution.py:849
  300.3 14.2 %collective-permute-start.37 = (bf16[480,512]{1,0:T(8,128)(2,1)S(1)}, bf16[480,512]{1,0:T(8,128)(2,1)}, u32[]{:S(2)}, u32[]{:S(2)}) collective-permute-start(bf16[480,512]{1,0:T(8,128)(2,1)S(1)} %add_convert_fusion.4), channel_id=1, source_target_pairs={{0,8},{1,5},{2,10},{3,7},{8,16},{9,1},{10,18},{11,3},{16,24},{17,9... | collective-permute-start | bytes 1474568 | tf_op jit(solution)/shard_map/ppermute | solution.py:849
  314.0 7.8 %collective-permute-start.29 = (bf16[256,768]{1,0:T(8,128)(2,1)S(1)}, bf16[256,768]{1,0:T(8,128)(2,1)S(1)}, u32[]{:S(2)}, u32[]{:S(2)}) collective-permute-start(bf16[256,768]{1,0:T(8,128)(2,1)S(1)} %add_convert_fusion.14), channel_id=1, source_target_pairs={{0,8},{1,5},{2,10},{3,7},{8,16},{9,1},{10,18},{11,3},{16,24},{17,9... | collective-permute-start | bytes 1179656 | tf_op jit(solution)/shard_map/ppermute | solution.py:849
  316.1 14.9 %copy-start.14 = (bf16[128,1408]{1,0:T(8,128)(2,1)S(1)}, bf16[128,1408]{1,0:T(8,128)(2,1)}, u32[]{:S(2)}) copy-start(bf16[128,1408]{1,0:T(8,128)(2,1)} %copy-done.13) | copy-start | bytes 1081348
  316.1 11.0 %collective-permute-start.38 = (bf16[480,512]{1,0:T(8,128)(2,1)S(1)}, bf16[480,512]{1,0:T(8,128)(2,1)S(1)}, u32[]{:S(2)}, u32[]{:S(2)}) collective-permute-start(bf16[480,512]{1,0:T(8,128)(2,1)S(1)} %add_convert_fusion.3), channel_id=1, source_target_pairs={{0,8},{1,5},{2,10},{3,7},{8,16},{9,1},{10,18},{11,3},{16,24},{17,9... | collective-permute-start | bytes 1474568 | tf_op jit(solution)/shard_map/ppermute | solution.py:849
  317.8 13.2 %collective-permute-start.47 = (bf16[128,1408]{1,0:T(8,128)(2,1)S(1)}, bf16[128,1408]{1,0:T(8,128)(2,1)S(1)}, u32[]{:S(2)}, u32[]{:S(2)}) collective-permute-start(bf16[128,1408]{1,0:T(8,128)(2,1)S(1)} %fusion.8), channel_id=1, source_target_pairs={{0,8},{1,5},{2,10},{3,7},{8,16},{9,1},{10,18},{11,3},{16,24},{17,9... | collective-permute-start | bytes 1081352 | tf_op jit(solution)/shard_map/ppermute | solution.py:849
  323.0 12.2 %collective-permute-start.30 = (bf16[256,768]{1,0:T(8,128)(2,1)S(1)}, bf16[256,768]{1,0:T(8,128)(2,1)S(1)}, u32[]{:S(2)}, u32[]{:S(2)}) collective-permute-start(bf16[256,768]{1,0:T(8,128)(2,1)S(1)} %add_convert_fusion.13), channel_id=1, source_target_pairs={{0,8},{1,5},{2,10},{3,7},{8,16},{9,1},{10,18},{11,3},{16,24},{17,9... | collective-permute-start | bytes 1179656 | tf_op jit(solution)/shard_map/ppermute | solution.py:849
  328.5 12.0 %collective-permute-start.39 = (bf16[480,512]{1,0:T(8,128)(2,1)S(1)}, bf16[480,512]{1,0:T(8,128)(2,1)S(1)}, u32[]{:S(2)}, u32[]{:S(2)}) collective-permute-start(bf16[480,512]{1,0:T(8,128)(2,1)S(1)} %add_convert_fusion.2), channel_id=1, source_target_pairs={{0,8},{1,5},{2,10},{3,7},{8,16},{9,1},{10,18},{11,3},{16,24},{17,9... | collective-permute-start | bytes 1474568 | tf_op jit(solution)/shard_map/ppermute | solution.py:849
  332.2 12.1 %collective-permute-start.49 = (bf16[128,1408]{1,0:T(8,128)(2,1)S(1)}, bf16[128,1408]{1,0:T(8,128)(2,1)S(1)}, u32[]{:S(2)}, u32[]{:S(2)}) collective-permute-start(bf16[128,1408]{1,0:T(8,128)(2,1)S(1)} %fusion.6), channel_id=1, source_target_pairs={{0,8},{1,5},{2,10},{3,7},{8,16},{9,1},{10,18},{11,3},{16,24},{17,9... | collective-permute-start | bytes 1081352 | tf_op jit(solution)/shard_map/ppermute | solution.py:849
  336.3 12.2 %collective-permute-start.31 = (bf16[256,768]{1,0:T(8,128)(2,1)S(1)}, bf16[256,768]{1,0:T(8,128)(2,1)S(1)}, u32[]{:S(2)}, u32[]{:S(2)}) collective-permute-start(bf16[256,768]{1,0:T(8,128)(2,1)S(1)} %add_convert_fusion.12), channel_id=1, source_target_pairs={{0,8},{1,5},{2,10},{3,7},{8,16},{9,1},{10,18},{11,3},{16,24},{17,9... | collective-permute-start | bytes 1179656 | tf_op jit(solution)/shard_map/ppermute | solution.py:849
  341.8 9.1 %collective-permute-start.40 = (bf16[480,512]{1,0:T(8,128)(2,1)S(1)}, bf16[480,512]{1,0:T(8,128)(2,1)S(1)}, u32[]{:S(2)}, u32[]{:S(2)}) collective-permute-start(bf16[480,512]{1,0:T(8,128)(2,1)S(1)} %add_convert_fusion.1), channel_id=1, source_target_pairs={{0,2},{1,3},{2,0},{3,1},{4,6},{5,7},{6,4},{7,5},{8,10},{9,11},{10,... | collective-permute-start | bytes 1474568 | tf_op jit(solution)/shard_map/ppermute | solution.py:862
  345.7 7.5 %collective-permute-start.51 = (bf16[128,1408]{1,0:T(8,128)(2,1)S(1)}, bf16[128,1408]{1,0:T(8,128)(2,1)S(1)}, u32[]{:S(2)}, u32[]{:S(2)}) collective-permute-start(bf16[128,1408]{1,0:T(8,128)(2,1)S(1)} %fusion.4), channel_id=1, source_target_pairs={{0,8},{1,5},{2,10},{3,7},{8,16},{9,1},{10,18},{11,3},{16,24},{17,9... | collective-permute-start | bytes 1081352 | tf_op jit(solution)/shard_map/ppermute | solution.py:849
  350.4 10.7 %collective-permute-start.32 = (bf16[256,768]{1,0:T(8,128)(2,1)}, bf16[256,768]{1,0:T(8,128)(2,1)S(1)}, u32[]{:S(2)}, u32[]{:S(2)}) collective-permute-start(bf16[256,768]{1,0:T(8,128)(2,1)} %add_convert_fusion.11), channel_id=1, source_target_pairs={{0,8},{1,5},{2,10},{3,7},{8,16},{9,1},{10,18},{11,3},{16,24},{17,9... | collective-permute-start | bytes 1179656 | tf_op jit(solution)/shard_map/ppermute | solution.py:849
  351.8 4.7 %collective-permute-start.41 = (bf16[480,512]{1,0:T(8,128)(2,1)}, bf16[480,512]{1,0:T(8,128)(2,1)}, u32[]{:S(2)}, u32[]{:S(2)}) collective-permute-start(bf16[480,512]{1,0:T(8,128)(2,1)} %add_convert_fusion.refs_0_.out_ref), channel_id=1, source_target_pairs={{0,1},{1,0},{2,3},{3,2},{4,5},{5,4},{6,7},{7,6},{8,9},{9,8},{10,11... | collective-permute-start | bytes 1474568 | tf_op jit(solution)/shard_map/ppermute | solution.py:858
  355.3 10.1 %collective-permute-start.52 = (bf16[128,1408]{1,0:T(8,128)(2,1)}, bf16[128,1408]{1,0:T(8,128)(2,1)}, u32[]{:S(2)}, u32[]{:S(2)}) collective-permute-start(bf16[128,1408]{1,0:T(8,128)(2,1)} %fusion.2), channel_id=1, source_target_pairs={{0,2},{1,3},{2,0},{3,1},{4,6},{5,7},{6,4},{7,5},{8,10},{9,11},{10,... | collective-permute-start | bytes 1081352 | tf_op jit(solution)/shard_map/ppermute | solution.py:862
  363.1 13.2 %collective-permute-start.42 = (bf16[256,768]{1,0:T(8,128)(2,1)S(1)}, bf16[256,768]{1,0:T(8,128)(2,1)S(1)}, u32[]{:S(2)}, u32[]{:S(2)}) collective-permute-start(bf16[256,768]{1,0:T(8,128)(2,1)S(1)} %add_convert_fusion.10), channel_id=1, source_target_pairs={{0,2},{1,3},{2,0},{3,1},{4,6},{5,7},{6,4},{7,5},{8,10},{9,11},{10,... | collective-permute-start | bytes 1179656 | tf_op jit(solution)/shard_map/ppermute | solution.py:862
  366.5 4.9 %collective-permute-start.53 = (bf16[128,1408]{1,0:T(8,128)(2,1)S(1)}, bf16[128,1408]{1,0:T(8,128)(2,1)S(1)}, u32[]{:S(2)}, u32[]{:S(2)}) collective-permute-start(bf16[128,1408]{1,0:T(8,128)(2,1)S(1)} %get-tuple-element.275.refs_0_), channel_id=1, source_target_pairs={{0,1},{1,0},{2,3},{3,2},{4,5},{5,4},{6,7},{7,6},{8,9},{9,8},{10,11... | collective-permute-start | bytes 1081352 | tf_op jit(solution)/shard_map/ppermute | solution.py:858
  366.6 4.8 %collective-permute-start.54 = (bf16[128,1408]{1,0:T(8,128)(2,1)S(1)}, bf16[128,1408]{1,0:T(8,128)(2,1)S(1)}, u32[]{:S(2)}, u32[]{:S(2)}) collective-permute-start(bf16[128,1408]{1,0:T(8,128)(2,1)S(1)} %get-tuple-element.274.refs_1_), channel_id=1, source_target_pairs={{0,1},{1,0},{2,3},{3,2},{4,5},{5,4},{6,7},{7,6},{8,9},{9,8},{10,11... | collective-permute-start | bytes 1081352 | tf_op jit(solution)/shard_map/ppermute | solution.py:858
  376.4 5.5 %collective-permute-start.55 = (bf16[256,768]{1,0:T(8,128)(2,1)S(1)}, bf16[256,768]{1,0:T(8,128)(2,1)S(1)}, u32[]{:S(2)}, u32[]{:S(2)}) collective-permute-start(bf16[256,768]{1,0:T(8,128)(2,1)S(1)} %add_convert_fusion.9.qfv_ref), channel_id=1, source_target_pairs={{0,1},{1,0},{2,3},{3,2},{4,5},{5,4},{6,7},{7,6},{8,9},{9,8},{10,11... | collective-permute-start | bytes 1179656 | tf_op jit(solution)/shard_map/ppermute | solution.py:858
  (16 other events, 27.2 us)
where the time goes:
time: 392 us; the launch traced here: 388 us
  Pallas kernels  181 us (46%)
  waiting for transfers between devices  102 us (26%)
  other arithmetic  48.7 us (12%)
  starting transfers between devices  44.5 us (11%)
  local copies, waits for them, and re-layouts  11.1 us (3%)
    pallas_call x1, Pallas kernels, ffn(): pl.pallas_call(functools.partial(ffn_kernel, owners), grid_spec=pltpu.Pre...  58.1 us
    ppermute x6, waiting for transfers between devices, ring_shift(): return lax.ppermute(tensor, 'fsdp', pairs)  46.4 us
    pallas_call x4, Pallas kernels, mixer_backward(): pl.pallas_call(functools.partial(mixer_backward_kernel, slot, per_half, f...  34.1 us
    ppermute x22, waiting for transfers between devices, ring_next(): return lax.ppermute(tensor, ('fsdp', 'dp'), pairs)  31.6 us
    pallas_call x2, Pallas kernels, mixer_forward(): pl.pallas_call(functools.partial(kernel, slot), grid_spec=pltpu.PrefetchS...  25.2 us
    ppermute x18, waiting for transfers between devices, column_swap(): lax.ppermute(tensor, 'dp', [(d, d ^ 2) for d in range(lax.axis_size('dp'))])  22.9 us
    pallas_call x6, Pallas kernels, place(): pl.pallas_call(functools.partial(place_kernel, which, kept, shapes), grid...  22.6 us
    convert_element_type x14, other arithmetic, step(): (moved.astype(wide) + self.term().astype(wide)).astype(low)  20 us
  transfers between devices with their start and end apart: 56, of which 27 were waited for; matrix products, arithmetic and copies ran while one was open for 13% of the time, Pallas kernels for 28%

commit v1 on v0

--- a/solution.py
+++ b/solution.py
@@ -1216,8 +1216,13 @@
                 grad_other = after(grad_other, sum_gu.last(), sum_do.last())
             arrived_qfv = [core_swap(grad_other.reshape(by_owner))]
         elif ringed and call > 1:
-            sum_do.step(arriving=(d_pre[-1],))
-            sum_gu.step(arriving=(d_pre[-1],))
+            gate = d_pre[-1]
+            if call == 3:
+                sum_qfv = RingSum([grads[0].reshape(by_owner)], arrived_qfv)
+                sum_qfv.begin()
+                gate = sum_qfv.last()
+            sum_do.step(arriving=(gate,))
+            sum_gu.step(arriving=(gate,))
     mine_qfv = [grads[0].reshape(by_owner)]
 
     def finish_input(*others):
@@ -1225,8 +1230,6 @@
         return input_gradient(rows, gains8, (late, d_pre[1]), w_a, d_x1)
 
     if ringed:
-        sum_qfv = RingSum(mine_qfv, arrived_qfv)
-        sum_qfv.begin()
         input_grad = None
         for step in range(1, RING - 1):
             if len(sum_gu.came) < RING:

time: 392 us -> 391 us (level)
  transfers between devices with their start and end apart: 56 -> 56, of which waited for: 27 -> 29; matrix products, arithmetic and copies ran while one was open for 13% -> 13% of each run, Pallas kernels for 28% -> 28%
where the time goes in v1:
time: 391 us; the launch traced here: 386 us
  Pallas kernels  181 us (46%)
  waiting for transfers between devices  102 us (26%)
  other arithmetic  48.8 us (12%)
  starting transfers between devices  43.1 us (11%)
  local copies, waits for them, and re-layouts  10.4 us (3%)
    pallas_call x1, Pallas kernels, ffn(): pl.pallas_call(functools.partial(ffn_kernel, owners), grid_spec=pltpu.Pre...  58.1 us
    ppermute x6, waiting for transfers between devices, ring_shift(): return lax.ppermute(tensor, 'fsdp', pairs)  46.4 us
    pallas_call x4, Pallas kernels, mixer_backward(): pl.pallas_call(functools.partial(mixer_backward_kernel, slot, per_half, f...  34.2 us
    ppermute x22, waiting for transfers between devices, ring_next(): return lax.ppermute(tensor, ('fsdp', 'dp'), pairs)  30 us
    pallas_call x2, Pallas kernels, mixer_forward(): pl.pallas_call(functools.partial(kernel, slot), grid_spec=pltpu.PrefetchS...  25.2 us
    ppermute x18, waiting for transfers between devices, column_swap(): lax.ppermute(tensor, 'dp', [(d, d ^ 2) for d in range(lax.axis_size('dp'))])  24.5 us
    pallas_call x6, Pallas kernels, place(): pl.pallas_call(functools.partial(place_kernel, which, kept, shapes), grid...  22.7 us
    convert_element_type x14, other arithmetic, step(): (moved.astype(wide) + self.term().astype(wide)).astype(low)  19.8 us
  transfers between devices with their start and end apart: 56, of which 29 were waited for; matrix products, arithmetic and copies ran while one was open for 13% of the time, Pallas kernels for 28%

profile of v1, /device:TPU:0, one launch (start us, length us, event | category | flops | bytes accessed | tf_op | source)
XLA Modules:
  0.0 386.4 jit_solution(15345549032640645759)
XLA Ops:
  0.7 3.1 pack_all.1
  3.8 3.0 collective-permute-start
  7.3 3.3 place.6
  10.7 24.3 %collective-permute-done.refs_0_ = bf16[128,4992]{1,0:T(8,128)(2,1)S(1)} collective-permute-done((bf16[128,4992]{1,0:T(8,128)(2,1)}, bf16[128,4992]{1,0:T(8,128)(2,1)S(1)}, u32[]{:S(2)}, u32[]{:S(2)}) %collective-permute-start) | collective-permute-done | bytes 1277984 | tf_op jit(solution)/shard_map/ppermute | solution.py:854
  35.0 1.5 collective-permute-done.1.refs_1_
  37.6 1.6 collective-permute-start.2
  40.7 1.6 collective-permute-start.4
  42.8 3.4 norm_rows.1.nt_hbm
  46.2 2.9 fusion.e_ref
  49.1 3.9 %place.7 = (bf16[1024,2048]{1,0:T(8,128)(2,1)}, bf16[1024,2816]{1,0:T(8,128)(2,1)}, bf16[2816,512]{1,0:T(8,128)(2,1)}, bf16[16,1024]{1,0:T(8,128)(2,1)}) custom-call(s32[8]{0:T(128)} %compare_select_fusion.2.origin_ref, s32[1]{0:T(128)} %bitcast.1.column_ref, ...), custom_call_target="tpu_custom_call", output_to_operand_aliasing={{0}: (4, {}), {1}: (5, {}), {2}: (6, {}), {3}: (7, {})} | custom-call | bytes 10223616 | tf_op jit(solution)/shard_map/place/pallas_call | solution.py:969
  53.0 3.9 %collective-permute-done.5.refs_3_ = bf16[128,1408]{1,0:T(8,128)(2,1)} collective-permute-done((bf16[128,1408]{1,0:T(8,128)(2,1)S(1)}, bf16[128,1408]{1,0:T(8,128)(2,1)}, u32[]{:S(2)}, u32[]{:S(2)}) %collective-permute-start.5) | collective-permute-done | bytes 360480 | tf_op jit(solution)/shard_map/ppermute | solution.py:862
  57.0 9.4 %collective-permute-done.2.refs_0_ = bf16[128,4992]{1,0:T(8,128)(2,1)} collective-permute-done((bf16[128,4992]{1,0:T(8,128)(2,1)S(1)}, bf16[128,4992]{1,0:T(8,128)(2,1)}, u32[]{:S(2)}, u32[]{:S(2)}) %collective-permute-start.2) | collective-permute-done | bytes 1277984 | tf_op jit(solution)/shard_map/ppermute | solution.py:854
  68.8 1.6 collective-permute-start.6
  72.8 1.6 collective-permute-start.8
  74.9 4.6 %place.8 = (bf16[1024,2048]{1,0:T(8,128)(2,1)}, bf16[1024,2816]{1,0:T(8,128)(2,1)}, bf16[2816,512]{1,0:T(8,128)(2,1)}, bf16[16,1024]{1,0:T(8,128)(2,1)}) custom-call(s32[8]{0:T(128)} %compare_select_fusion.2.origin_ref, s32[1]{0:T(128)} %bitcast.1.column_ref, ...), custom_call_target="tpu_custom_call", output_to_operand_aliasing={{0}: (6, {}), {1}: (7, {}), {2}: (8, {}), {3}: (9, {})} | custom-call | bytes 13107200 | tf_op jit(solution)/shard_map/place/pallas_call | solution.py:969
  79.5 4.7 %collective-permute-done.8.refs_2_ = bf16[128,1408]{1,0:T(8,128)(2,1)} collective-permute-done((bf16[128,1408]{1,0:T(8,128)(2,1)S(1)}, bf16[128,1408]{1,0:T(8,128)(2,1)}, u32[]{:S(2)}, u32[]{:S(2)}) %collective-permute-start.8) | collective-permute-done | bytes 360480 | tf_op jit(solution)/shard_map/ppermute | solution.py:862
  84.2 3.9 collective-permute-done.9.refs_3_
  88.0 8.5 %collective-permute-done.6.refs_0_ = bf16[128,4992]{1,0:T(8,128)(2,1)S(1)} collective-permute-done((bf16[128,4992]{1,0:T(8,128)(2,1)}, bf16[128,4992]{1,0:T(8,128)(2,1)S(1)}, u32[]{:S(2)}, u32[]{:S(2)}) %collective-permute-start.6) | collective-permute-done | bytes 1277984 | tf_op jit(solution)/shard_map/ppermute | solution.py:854
  99.1 1.8 collective-permute-start.10
  101.0 1.6 collective-permute-start.11
  103.1 4.5 %place.9 = (bf16[1024,2048]{1,0:T(8,128)(2,1)}, bf16[1024,2816]{1,0:T(8,128)(2,1)}, bf16[2816,512]{1,0:T(8,128)(2,1)}, bf16[16,1024]{1,0:T(8,128)(2,1)}) custom-call(s32[8]{0:T(128)} %compare_select_fusion.2.origin_ref, s32[1]{0:T(128)} %bitcast.1.column_ref, ...), custom_call_target="tpu_custom_call", output_to_operand_aliasing={{0}: (6, {}), {1}: (7, {}), {2}: (8, {}), {3}: (9, {})} | custom-call | bytes 13107200 | tf_op jit(solution)/shard_map/place/pallas_call | solution.py:969
  107.6 2.6 collective-permute-done.11.refs_1_
  110.2 4.0 %collective-permute-done.12.refs_2_ = bf16[128,1408]{1,0:T(8,128)(2,1)} collective-permute-done((bf16[128,1408]{1,0:T(8,128)(2,1)S(1)}, bf16[128,1408]{1,0:T(8,128)(2,1)}, u32[]{:S(2)}, u32[]{:S(2)}) %collective-permute-start.12) | collective-permute-done | bytes 360480 | tf_op jit(solution)/shard_map/ppermute | solution.py:862
  114.2 2.8 collective-permute-done.10.refs_0_
  116.9 3.6 place.10
  121.7 1.6 collective-permute-start.13
  123.3 9.9 %mixer_forward.2 = (bf16[768,512]{1,0:T(8,128)(2,1)}, f32[768,512]{1,0:T(8,128)}, f32[768,512]{1,0:T(8,128)}, bf16[768,512]{1,0:T(8,128)(2,1)}, bf16[768,512]{1,0:T(8,128)(2,1)}, /*index=5*/f32[8,1024]{1,0:T(8,128)}) custom-call(s32[1]{0:T(128)} %bitcast.core_ref.half_ref, bf16[768,1024]{1,0:T(8,128)(2,1)} %bitcast.82, ...), custom_call_target="tpu_custom_call" | custom-call | flops 6241124352 | bytes 13631488 | tf_op jit(solution)/shard_map/mixer_forward/pallas_call | solution.py:239
  133.9 2.7 place.11.wm_ref
  137.8 15.3 %mixer_forward.3 = (bf16[768,512]{1,0:T(8,128)(2,1)}, f32[768,512]{1,0:T(8,128)}, f32[768,512]{1,0:T(8,128)}, bf16[768,512]{1,0:T(8,128)(2,1)}, bf16[768,512]{1,...) custom-call(s32[1]{0:T(128)S(6)} %sub.55.half_ref.core_ref, ...), custom_call_target="tpu_custom_call" | custom-call | flops 6241124352 | bytes 13631488 | tf_op jit(solution)/shard_map/mixer_forward/pallas_call | solution.py:239
  153.1 58.1 %ffn.1 = (bf16[2,1024,1408]{2,1,0:T(8,128)(2,1)}, bf16[2,1024,1408]{2,1,0:T(8,128)(2,1)}, bf16[3840,512]{1,0:T(8,128)(2,1)}, bf16[3840,512]{1,0:T(8,128)(2,1)}, ...) custom-call(s32[2]{0:T(128)} %pad_add_fusion.core_ref, ...), custom_call_target="tpu_custom_call" | custom-call | flops 39862665216 | bytes 50331648 | tf_op jit(solution)/shard_map/ffn/pallas_call | solution.py:420
  211.8 8.6 %mixer_backward.4 = (bf16[8,2,128,768]{3,2,1,0:T(8,128)(2,1)}, bf16[768,1536]{1,0:T(8,128)(2,1)}) custom-call(s32[1]{0:T(128)S(6)} %sub.55.half_ref.core_ref, bf16[1024,768]{1,0:T(8,128)(2,1)} %norm_rows.1.nt_hbm, f32[8,1024]{1,0:T(8,128)} %get-tuple-element.194.g_ref, f32[768,512]{1,0:T(8,128)} %get-tuple-element.201.q_ref, ...), custom_call_target="tpu_custom_call" | custom-call | flops 2717908992 | bytes 5505024 | tf_op jit(solution)/shard_map/mixer_backward/pallas_call | solution.py:547
  221.0 4.3 %fusion.21 = (bf16[128,1408]{1,0:T(8,128)(2,1)}, bf16[128,1408]{1,0:T(8,128)(2,1)}, bf16[128,1408]{1,0:T(8,128)(2,1)}, bf16[128,1408]{1,0:T(8,128)(2,1)}, bf16[1...) fusion(bf16[2,1024,1408]{2,1,0:T(8,128)(2,1)} %collective-permu, ...), kind=kLoop, calls=%fused_computation.57 | loop fusion | flops 5767168 | bytes 8650784 | tf_op jit(solution)/shard_map/convert_element_type | solution.py:1018
  226.2 8.6 %mixer_backward.5 = (bf16[8,2,128,768]{3,2,1,0:T(8,128)(2,1)}, bf16[768,1536]{1,0:T(8,128)(2,1)}) custom-call(s32[1]{0:T(128)S(6)} %sub.55.half_ref.core_ref, bf16[1024,768]{1,0:T(8,128)(2,1)} %norm_rows.1.nt_hbm, f32[8,1024]{1,0:T(8,128)} %get-tuple-element.194.g_ref, ...), custom_call_target="tpu_custom_call", output_to_operand_aliasing={{0}: (8, {}), {1}: (9, {})} | custom-call | flops 2717908992 | bytes 5505024 | tf_op jit(solution)/shard_map/mixer_backward/pallas_call | solution.py:547
  237.4 1.6 collective-permute-start.22
  241.8 8.5 %mixer_backward.6 = (bf16[8,2,128,768]{3,2,1,0:T(8,128)(2,1)}, bf16[768,1536]{1,0:T(8,128)(2,1)}) custom-call(s32[1]{0:T(128)} %bitcast.core_ref.half_ref, bf16[1024,768]{1,0:T(8,128)(2,1)} %norm_rows.1.nt_hbm, f32[8,1024]{1,0:T(8,128)} %get-tuple-element.194.g_ref, f32[768,512]{1,0:T(8,128)} %get-tuple-element.217.q_ref, ...), custom_call_target="tpu_custom_call" | custom-call | flops 2717908992 | bytes 5505024 | tf_op jit(solution)/shard_map/mixer_backward/pallas_call | solution.py:547
  253.6 2.0 fusion.14
  255.6 2.5 collective-permute-done.23
  258.8 8.5 %mixer_backward.7 = (bf16[8,2,128,768]{3,2,1,0:T(8,128)(2,1)}, bf16[768,1536]{1,0:T(8,128)(2,1)}) custom-call(s32[1]{0:T(128)} %bitcast.core_ref.half_ref, bf16[1024,768]{1,0:T(8,128)(2,1)} %norm_rows.1.nt_hbm, f32[8,1024]{1,0:T(8,128)} %get-tuple-element.194.g_ref, ...), custom_call_target="tpu_custom_call", output_to_operand_aliasing={{0}: (8, {}), {1}: (9, {})} | custom-call | flops 2717908992 | bytes 5505024 | tf_op jit(solution)/shard_map/mixer_backward/pallas_call | solution.py:547
  267.3 2.1 add_convert_fusion.17
  270.0 2.2 fusion.12
  272.3 2.3 add_convert_fusion.6
  279.6 4.1 %collective-permute-done.35 = bf16[480,512]{1,0:T(8,128)(2,1)} collective-permute-done((bf16[480,512]{1,0:T(8,128)(2,1)}, bf16[480,512]{1,0:T(8,128)(2,1)}, u32[]{:S(2)}, u32[]{:S(2)}) %collective-permute-start.35) | collective-permute-done | bytes 491552 | tf_op jit(solution)/shard_map/ppermute | solution.py:849
  284.2 1.5 add_convert_fusion.5
  285.7 1.7 collective-permute-done.44
  288.2 2.1 fusion.10
  294.6 2.3 collective-permute-done.36
  298.9 11.6 %input_gradient.1 = f32[768,1024]{1,0:T(8,128)} custom-call(bf16[768,1024]{1,0:T(8,128)(2,1)} %bitcast.84, f32[8,1024]{1,0:T(8,128)} %get-tuple-element.194.g_ref, bf16[768,1536]{1,0:T(8,128)(2,1)} %get-tuple-element.230.dm_ref, bf16[768,1536]{1,0:T(8,128)(2,1)} %get-tuple-element.211.do_ref, bf16[1024,2048]{1,0:T(8,128)(2,1)} %get-tuple-element.187.w_ref.wom_hbm.wm_ref, ...), custom_call_target="tpu_custom_call" | custom-call | flops 4831838208 | bytes 18874368 | tf_op jit(solution)/shard_map/input_gradient/pallas_call | solution.py:600
  312.2 1.5 add_convert_fusion.3
  313.7 1.5 collective-permute-start.38
  316.6 1.5 collective-permute-start.47
  318.1 1.6 collective-permute-done.29
  321.1 3.8 collective-permute-done.38
  326.6 2.2 collective-permute-done.47
  330.4 2.6 collective-permute-done.30
  334.5 3.8 collective-permute-done.39
  343.9 2.5 collective-permute-done.31
  346.4 1.9 add_convert_fusion.11
  351.0 2.1 fusion.2
  354.3 4.6 %update_ffn_out.1 = (f32[352,1024]{1,0:T(8,128)}, f32[352,1024]{1,0:T(8,128)}, f32[352,1024]{1,0:T(8,128)}, f32[2,352,128]{2,1,0:T(8,128)}) custom-call(s32[1]{0:T(128)} %bitcast.core_ref.half_ref, f32[352,1024]{1,0:T(8,128)} %w_ref.7, f32[352,1024]{1,0:T(8,128)} %m_ref.5, f32[352,1024]{1,0:T(8,128)} %a_ref.5, ...), custom_call_target="tpu_custom_call" | custom-call | flops 4325376 | bytes 9371648 | tf_op jit(solution)/shard_map/update_ffn_out/pallas_call | solution.py:656
  361.9 1.5 collective-permute-done.52
  365.4 4.0 %update_ffn_in.2 = (f32[2,128,2816]{2,1,0:T(8,128)}, f32[2,128,2816]{2,1,0:T(8,128)}, f32[2,128,2816]{2,1,0:T(8,128)}, f32[2,64,128]{2,1,0:T(8,128)}) custom-call(s32[1]{0:T(128)} %bitcast.core_ref.half_ref, f32[2,128,2816]{2,1,0:T(8,128)} %w_ref.9, f32[2,128,2816]{2,1,0:T(8,128)} %m_ref.7, f32[2,128,2816]{2,1,0:T(8,128)} %a_ref.7, ...), custom_call_target="tpu_custom_call" | custom-call | flops 8650752 | bytes 18743296 | tf_op jit(solution)/shard_map/update_ffn_in/pallas_call | solution.py:656
  370.3 4.0 %update_ffn_in.3 = (f32[2,128,2816]{2,1,0:T(8,128)}, f32[2,128,2816]{2,1,0:T(8,128)}, f32[2,128,2816]{2,1,0:T(8,128)}, f32[2,64,128]{2,1,0:T(8,128)}) custom-call(s32[1]{0:T(128)S(6)} %sub.55.half_ref.core_ref, f32[2,128,2816]{2,1,0:T(8,128)} %w_ref.9, f32[2,128,2816]{2,1,0:T(8,128)} %m_ref.7, ...), custom_call_target="tpu_custom_call", output_to_operand_aliasing={{0}: (6, {}), {1}: (7, {}), {2}: (8, {})} | custom-call | flops 8650752 | bytes 18743296 | tf_op jit(solution)/shard_map/update_ffn_in/pallas_call | solution.py:656
  375.3 4.8 %update_attention.2 = (f32[4,128,1024]{2,1,0:T(8,128)}, f32[4,128,1024]{2,1,0:T(8,128)}, f32[4,128,1024]{2,1,0:T(8,128)}, f32[4,128,128]{2,1,0:T(8,128)}) custom-call(s32[1]{0:T(128)} %bitcast.core_ref.half_ref, f32[4,128,1024]{2,1,0:T(8,128)} %w_ref.11, f32[4,128,1024]{2,1,0:T(8,128)} %m_ref.9, f32[4,128,1024]{2,1,0:T(8,128)} %a_ref.9, ...), custom_call_target="tpu_custom_call" | custom-call | flops 3145728 | bytes 6815744 | tf_op jit(solution)/shard_map/update_attention/pallas_call | solution.py:740
  380.8 5.1 %update_attention.3 = (f32[4,128,1024]{2,1,0:T(8,128)}, f32[4,128,1024]{2,1,0:T(8,128)}, f32[4,128,1024]{2,1,0:T(8,128)}, f32[3,128]{1,0:T(4,128)}, f32[3,128]{1,0:T(4,128)}, /*index=5*/f32[3,128]{1,0:T(4,128)}) custom-call(s32[1]{0:T(128)S(6)} %sub.55.half_ref.core_ref, ...), custom_call_target="tpu_custom_call", output_to_operand_aliasing={{0}: (12, {}), {1}: (13, {}), {2}: (14, {})} | custom-call | flops 3145728 | bytes 6815744 | tf_op jit(solution)/shard_map/update_attention/pallas_call | solution.py:740
  (156 shorter events, 66.1 us)
Async XLA Ops:
  0.7 6.1 %copy-start.22 = (s32[8]{0:T(128)S(1)}, s32[8]{0:T(128)}, u32[]{:S(2)}) copy-start(s32[8]{0:T(128)} %constant.225.clone) | copy-start | bytes 100
  3.8 39.0 %copy-start.21 = (s32[2,1]{0,1:T(1,128)S(1)}, s32[2,1]{0,1:T(1,128)}, u32[]{:S(2)}) copy-start(s32[2,1]{0,1:T(1,128)} %param.18) | copy-start | bytes 28
  3.8 31.2 %collective-permute-start = (bf16[128,4992]{1,0:T(8,128)(2,1)}, bf16[128,4992]{1,0:T(8,128)(2,1)S(1)}, u32[]{:S(2)}, u32[]{:S(2)}) collective-permute-start(bf16[128,4992]{1,0:T(8,128)(2,1)} %get-tuple-element.140.refs_0_), channel_id=1, source_target_pairs={{0,8},{8,16},{16,24},{24,28},{28,20},{20,12},{12,4},{4,0},{1,9},{9... | collective-permute-start | bytes 3833864 | tf_op jit(solution)/shard_map/ppermute | solution.py:854
  6.8 29.7 %collective-permute-start.1 = (bf16[128,4992]{1,0:T(8,128)(2,1)}, bf16[128,4992]{1,0:T(8,128)(2,1)S(1)}, u32[]{:S(2)}, u32[]{:S(2)}) collective-permute-start(bf16[128,4992]{1,0:T(8,128)(2,1)} %get-tuple-element.140.refs_0_), channel_id=1, source_target_pairs={{0,4},{8,0},{16,8},{24,16},{28,24},{20,28},{12,20},{4,12},{1,5},{9... | collective-permute-start | bytes 3833864 | tf_op jit(solution)/shard_map/ppermute | solution.py:854
  35.0 14.1 %copy-start.5 = (bf16[128,4992]{1,0:T(8,128)(2,1)}, bf16[128,4992]{1,0:T(8,128)(2,1)S(1)}, u32[]{:S(2)}) copy-start(bf16[128,4992]{1,0:T(8,128)(2,1)S(1)} %collective-permute-done.refs_0_) | copy-start | bytes 3833860
  37.6 28.7 %collective-permute-start.2 = (bf16[128,4992]{1,0:T(8,128)(2,1)S(1)}, bf16[128,4992]{1,0:T(8,128)(2,1)}, u32[]{:S(2)}, u32[]{:S(2)}) collective-permute-start(bf16[128,4992]{1,0:T(8,128)(2,1)S(1)} %collective-permute-done.refs_0_), channel_id=1, source_target_pairs={{0,8},{8,16},{16,24},{24,28},{28,20},{20,12},{12,4},{4,0},{1,9},{9... | collective-permute-start | bytes 3833864 | tf_op jit(solution)/shard_map/ppermute | solution.py:854
  39.2 28.6 %collective-permute-start.3 = (bf16[128,4992]{1,0:T(8,128)(2,1)}, bf16[128,4992]{1,0:T(8,128)(2,1)S(1)}, u32[]{:S(2)}, u32[]{:S(2)}) collective-permute-start(bf16[128,4992]{1,0:T(8,128)(2,1)} %copy-done.6), channel_id=1, source_target_pairs={{0,4},{8,0},{16,8},{24,16},{28,24},{20,28},{12,20},{4,12},{1,5},{9... | collective-permute-start | bytes 3833864 | tf_op jit(solution)/shard_map/ppermute | solution.py:854
  40.7 12.4 %collective-permute-start.4 = (bf16[128,1408]{1,0:T(8,128)(2,1)S(1)}, bf16[128,1408]{1,0:T(8,128)(2,1)}, u32[]{:S(2)}, u32[]{:S(2)}) collective-permute-start(bf16[128,1408]{1,0:T(8,128)(2,1)S(1)} %slice.21), channel_id=1, source_target_pairs={{0,2},{1,3},{2,0},{3,1},{4,6},{5,7},{6,4},{7,5},{8,10},{9,11},{10,... | collective-permute-start | bytes 1081352 | tf_op jit(solution)/shard_map/ppermute | solution.py:862
  42.2 14.7 %collective-permute-start.5 = (bf16[128,1408]{1,0:T(8,128)(2,1)S(1)}, bf16[128,1408]{1,0:T(8,128)(2,1)}, u32[]{:S(2)}, u32[]{:S(2)}) collective-permute-start(bf16[128,1408]{1,0:T(8,128)(2,1)S(1)} %slice.22), channel_id=1, source_target_pairs={{0,2},{1,3},{2,0},{3,1},{4,6},{5,7},{6,4},{7,5},{8,10},{9,11},{10,... | collective-permute-start | bytes 1081352 | tf_op jit(solution)/shard_map/ppermute | solution.py:862
  68.8 27.7 %collective-permute-start.6 = (bf16[128,4992]{1,0:T(8,128)(2,1)}, bf16[128,4992]{1,0:T(8,128)(2,1)S(1)}, u32[]{:S(2)}, u32[]{:S(2)}) collective-permute-start(bf16[128,4992]{1,0:T(8,128)(2,1)} %collective-permute-done.2.refs_0_), channel_id=1, source_target_pairs={{0,8},{8,16},{16,24},{24,28},{28,20},{20,12},{12,4},{4,0},{1,9},{9... | collective-permute-start | bytes 3833864 | tf_op jit(solution)/shard_map/ppermute | solution.py:854
  70.3 27.5 %collective-permute-start.7 = (bf16[128,4992]{1,0:T(8,128)(2,1)}, bf16[128,4992]{1,0:T(8,128)(2,1)S(1)}, u32[]{:S(2)}, u32[]{:S(2)}) collective-permute-start(bf16[128,4992]{1,0:T(8,128)(2,1)} %copy-done.4), channel_id=1, source_target_pairs={{0,4},{8,0},{16,8},{24,16},{28,24},{20,28},{12,20},{4,12},{1,5},{9... | collective-permute-start | bytes 3833864 | tf_op jit(solution)/shard_map/ppermute | solution.py:854
  72.8 11.3 %collective-permute-start.8 = (bf16[128,1408]{1,0:T(8,128)(2,1)S(1)}, bf16[128,1408]{1,0:T(8,128)(2,1)}, u32[]{:S(2)}, u32[]{:S(2)}) collective-permute-start(bf16[128,1408]{1,0:T(8,128)(2,1)S(1)} %slice.23), channel_id=1, source_target_pairs={{0,2},{1,3},{2,0},{3,1},{4,6},{5,7},{6,4},{7,5},{8,10},{9,11},{10,... | collective-permute-start | bytes 1081352 | tf_op jit(solution)/shard_map/ppermute | solution.py:862
  74.4 13.6 %collective-permute-start.9 = (bf16[128,1408]{1,0:T(8,128)(2,1)S(1)}, bf16[128,1408]{1,0:T(8,128)(2,1)}, u32[]{:S(2)}, u32[]{:S(2)}) collective-permute-start(bf16[128,1408]{1,0:T(8,128)(2,1)S(1)} %slice.24), channel_id=1, source_target_pairs={{0,2},{1,3},{2,0},{3,1},{4,6},{5,7},{6,4},{7,5},{8,10},{9,11},{10,... | collective-permute-start | bytes 1081352 | tf_op jit(solution)/shard_map/ppermute | solution.py:862
  96.5 6.6 %copy-start.2 = (bf16[128,4992]{1,0:T(8,128)(2,1)}, bf16[128,4992]{1,0:T(8,128)(2,1)S(1)}, u32[]{:S(2)}) copy-start(bf16[128,4992]{1,0:T(8,128)(2,1)S(1)} %collective-permute-done.6.refs_0_) | copy-start | bytes 3833860
  99.1 17.8 %collective-permute-start.10 = (bf16[128,4992]{1,0:T(8,128)(2,1)}, bf16[128,4992]{1,0:T(8,128)(2,1)}, u32[]{:S(2)}, u32[]{:S(2)}) collective-permute-start(bf16[128,4992]{1,0:T(8,128)(2,1)} %broadcast_select_fusion), channel_id=1, source_target_pairs={{0,8},{1,5},{2,10},{3,7},{8,16},{9,1},{10,18},{11,3},{16,24},{17,9... | collective-permute-start | bytes 3833864 | tf_op jit(solution)/shard_map/ppermute | solution.py:849
  101.0 9.2 %collective-permute-start.11 = (bf16[128,1408]{1,0:T(8,128)(2,1)S(1)}, bf16[128,1408]{1,0:T(8,128)(2,1)S(1)}, u32[]{:S(2)}, u32[]{:S(2)}) collective-permute-start(bf16[128,1408]{1,0:T(8,128)(2,1)S(1)} %slice.25), channel_id=1, source_target_pairs={{0,2},{1,3},{2,0},{3,1},{4,6},{5,7},{6,4},{7,5},{8,10},{9,11},{10,... | collective-permute-start | bytes 1081352 | tf_op jit(solution)/shard_map/ppermute | solution.py:862
  102.5 11.7 %collective-permute-start.12 = (bf16[128,1408]{1,0:T(8,128)(2,1)S(1)}, bf16[128,1408]{1,0:T(8,128)(2,1)}, u32[]{:S(2)}, u32[]{:S(2)}) collective-permute-start(bf16[128,1408]{1,0:T(8,128)(2,1)S(1)} %slice.26), channel_id=1, source_target_pairs={{0,2},{1,3},{2,0},{3,1},{4,6},{5,7},{6,4},{7,5},{8,10},{9,11},{10,... | collective-permute-start | bytes 1081352 | tf_op jit(solution)/shard_map/ppermute | solution.py:862
  110.2 6.7 %copy-start.18 = (bf16[128,1408]{1,0:T(8,128)(2,1)}, bf16[128,1408]{1,0:T(8,128)(2,1)S(1)}, u32[]{:S(2)}) copy-start(bf16[128,1408]{1,0:T(8,128)(2,1)S(1)} %collective-permute-done.11.refs_1_) | copy-start | bytes 1081348
  120.6 12.6 %collective-permute-start.14 = (bf16[1024,2048]{1,0:T(8,128)(2,1)}, bf16[1024,2048]{1,0:T(8,128)(2,1)}, u32[]{:S(2)}, u32[]{:S(2)}) collective-permute-start(bf16[1024,2048]{1,0:T(8,128)(2,1)} %get-tuple-element.187.w_ref.wom_hbm.wm_ref), channel_id=1, source_target_pairs={{0,1},{1,0},{2,3},{3,2},{4,5},{5,4},{6,7},{7,6},{8,9},{9,8},{10,11... | collective-permute-start | bytes 12582920 | tf_op jit(solution)/shard_map/ppermute | solution.py:858
  121.7 11.5 %collective-permute-start.13 = (bf16[128,1408]{1,0:T(8,128)(2,1)S(1)}, bf16[128,1408]{1,0:T(8,128)(2,1)S(1)}, u32[]{:S(2)}, u32[]{:S(2)}) collective-permute-start(bf16[128,1408]{1,0:T(8,128)(2,1)S(1)} %slice.27), channel_id=1, source_target_pairs={{0,2},{1,3},{2,0},{3,1},{4,6},{5,7},{6,4},{7,5},{8,10},{9,11},{10,... | collective-permute-start | bytes 1081352 | tf_op jit(solution)/shard_map/ppermute | solution.py:862
  136.6 16.5 %collective-permute-start.15 = (bf16[1024,2816]{1,0:T(8,128)(2,1)}, bf16[1024,2816]{1,0:T(8,128)(2,1)}, u32[]{:S(2)}, u32[]{:S(2)}) collective-permute-start(bf16[1024,2816]{1,0:T(8,128)(2,1)} %place.11.wm_ref), channel_id=1, source_target_pairs={{0,1},{1,0},{2,3},{3,2},{4,5},{5,4},{6,7},{7,6},{8,9},{9,8},{10,11... | collective-permute-start | bytes 17301512 | tf_op jit(solution)/shard_map/ppermute | solution.py:858
  136.9 16.2 %collective-permute-start.16 = (bf16[2816,512]{1,0:T(8,128)(2,1)S(1)}, bf16[2816,512]{1,0:T(8,128)(2,1)}, u32[]{:S(2)}, u32[]{:S(2)}) collective-permute-start(bf16[2816,512]{1,0:T(8,128)(2,1)S(1)} %copy-done), channel_id=1, source_target_pairs={{0,1},{1,0},{2,3},{3,2},{4,5},{5,4},{6,7},{7,6},{8,9},{9,8},{10,11... | collective-permute-start | bytes 8650760 | tf_op jit(solution)/shard_map/ppermute | solution.py:858
  211.2 9.8 %collective-permute-start.17 = (bf16[2,1024,1408]{2,1,0:T(8,128)(2,1)}, bf16[2,1024,1408]{2,1,0:T(8,128)(2,1)}, u32[]{:S(2)}, u32[]{:S(2)}) collective-permute-start(bf16[2,1024,1408]{2,1,0:T(8,128)(2,1)} %get-tuple-element.208), channel_id=1, source_target_pairs={{0,1},{1,0},{2,3},{3,2},{4,5},{5,4},{6,7},{7,6},{8,9},{9,8},{10,11... | collective-permute-start | bytes 17301512 | tf_op jit(solution)/shard_map/ppermute | solution.py:858
  211.5 23.3 %collective-permute-start.19 = (bf16[3840,512]{1,0:T(8,128)(2,1)}, bf16[3840,512]{1,0:T(8,128)(2,1)}, u32[]{:S(2)}, u32[]{:S(2)}) collective-permute-start(bf16[3840,512]{1,0:T(8,128)(2,1)} %get-tuple-element.215), channel_id=1, source_target_pairs={{0,1},{1,0},{2,3},{3,2},{4,5},{5,4},{6,7},{7,6},{8,9},{9,8},{10,11... | collective-permute-start | bytes 11796488 | tf_op jit(solution)/shard_map/ppermute | solution.py:858
  225.3 10.8 %collective-permute-start.18 = (bf16[128,1408]{1,0:T(8,128)(2,1)S(1)}, bf16[128,1408]{1,0:T(8,128)(2,1)S(1)}, u32[]{:S(2)}, u32[]{:S(2)}) collective-permute-start(bf16[128,1408]{1,0:T(8,128)(2,1)S(1)} %get-tuple-element.273), channel_id=1, source_target_pairs={{0,2},{1,3},{2,0},{3,1},{4,6},{5,7},{6,4},{7,5},{8,10},{9,11},{10,... | collective-permute-start | bytes 1081352 | tf_op jit(solution)/shard_map/ppermute | solution.py:862
  237.3 30.0 %collective-permute-start.24 = (bf16[2048,768]{1,0:T(8,128)(2,1)}, bf16[2048,768]{1,0:T(8,128)(2,1)}, u32[]{:S(2)}, u32[]{:S(2)}) collective-permute-start(bf16[2048,768]{1,0:T(8,128)(2,1)} %bitcast.86), channel_id=1, source_target_pairs={{0,1},{1,0},{2,3},{3,2},{4,5},{5,4},{6,7},{7,6},{8,9},{9,8},{10,11... | collective-permute-start | bytes 9437192 | tf_op jit(solution)/shard_map/ppermute | solution.py:858
  237.4 12.9 %collective-permute-start.22 = (bf16[480,512]{1,0:T(8,128)(2,1)S(1)}, bf16[480,512]{1,0:T(8,128)(2,1)S(1)}, u32[]{:S(2)}, u32[]{:S(2)}) collective-permute-start(bf16[480,512]{1,0:T(8,128)(2,1)S(1)} %add_convert_fusion.8), channel_id=1, source_target_pairs={{0,8},{1,5},{2,10},{3,7},{8,16},{9,1},{10,18},{11,3},{16,24},{17,9... | collective-permute-start | bytes 1474568 | tf_op jit(solution)/shard_map/ppermute | solution.py:849
  239.0 14.6 %collective-permute-start.21 = (bf16[128,1408]{1,0:T(8,128)(2,1)S(1)}, bf16[128,1408]{1,0:T(8,128)(2,1)S(1)}, u32[]{:S(2)}, u32[]{:S(2)}) collective-permute-start(bf16[128,1408]{1,0:T(8,128)(2,1)S(1)} %get-tuple-element.272), channel_id=1, source_target_pairs={{0,2},{1,3},{2,0},{3,1},{4,6},{5,7},{6,4},{7,5},{8,10},{9,11},{10,... | collective-permute-start | bytes 1081352 | tf_op jit(solution)/shard_map/ppermute | solution.py:862
  240.1 17.9 %collective-permute-start.23 = (bf16[128,1408]{1,0:T(8,128)(2,1)S(1)}, bf16[128,1408]{1,0:T(8,128)(2,1)S(1)}, u32[]{:S(2)}, u32[]{:S(2)}) collective-permute-start(bf16[128,1408]{1,0:T(8,128)(2,1)S(1)} %get-tuple-element.271), channel_id=1, source_target_pairs={{0,2},{1,3},{2,0},{3,1},{4,6},{5,7},{6,4},{7,5},{8,10},{9,11},{10,... | collective-permute-start | bytes 1081352 | tf_op jit(solution)/shard_map/ppermute | solution.py:862
  241.0 11.9 %collective-permute-start.20 = (bf16[128,1408]{1,0:T(8,128)(2,1)S(1)}, bf16[128,1408]{1,0:T(8,128)(2,1)S(1)}, u32[]{:S(2)}, u32[]{:S(2)}) collective-permute-start(bf16[128,1408]{1,0:T(8,128)(2,1)S(1)} %fusion.15), channel_id=1, source_target_pairs={{0,8},{1,5},{2,10},{3,7},{8,16},{9,1},{10,18},{11,3},{16,24},{17,9... | collective-permute-start | bytes 1081352 | tf_op jit(solution)/shard_map/ppermute | solution.py:849
  250.4 26.7 %collective-permute-start.43 = (bf16[128,1408]{1,0:T(8,128)(2,1)}, bf16[128,1408]{1,0:T(8,128)(2,1)}, u32[]{:S(2)}, u32[]{:S(2)}) collective-permute-start(bf16[128,1408]{1,0:T(8,128)(2,1)} %get-tuple-element.270), channel_id=1, source_target_pairs={{0,2},{1,3},{2,0},{3,1},{4,6},{5,7},{6,4},{7,5},{8,10},{9,11},{10,... | collective-permute-start | bytes 1081352 | tf_op jit(solution)/shard_map/ppermute | solution.py:862
  252.9 17.1 %collective-permute-start.33 = (bf16[480,512]{1,0:T(8,128)(2,1)S(1)}, bf16[480,512]{1,0:T(8,128)(2,1)}, u32[]{:S(2)}, u32[]{:S(2)}) collective-permute-start(bf16[480,512]{1,0:T(8,128)(2,1)S(1)} %add_convert_fusion.7), channel_id=1, source_target_pairs={{0,8},{1,5},{2,10},{3,7},{8,16},{9,1},{10,18},{11,3},{16,24},{17,9... | collective-permute-start | bytes 1474568 | tf_op jit(solution)/shard_map/ppermute | solution.py:849
  258.0 12.0 %collective-permute-start.34 = (bf16[128,1408]{1,0:T(8,128)(2,1)}, bf16[128,1408]{1,0:T(8,128)(2,1)}, u32[]{:S(2)}, u32[]{:S(2)}) collective-permute-start(bf16[128,1408]{1,0:T(8,128)(2,1)} %fusion.14), channel_id=1, source_target_pairs={{0,8},{1,5},{2,10},{3,7},{8,16},{9,1},{10,18},{11,3},{16,24},{17,9... | collective-permute-start | bytes 1081352 | tf_op jit(solution)/shard_map/ppermute | solution.py:849
  267.3 11.2 %copy-start.1 = (bf16[8,2,128,768]{3,2,1,0:T(8,128)(2,1)S(1)}, bf16[8,2,128,768]{3,2,1,0:T(8,128)(2,1)}, u32[]{:S(2)}) copy-start(bf16[8,2,128,768]{3,2,1,0:T(8,128)(2,1)} %get-tuple-element.227) | copy-start | bytes 9437188
  269.4 8.8 %collective-permute-start.25 = (bf16[256,768]{1,0:T(8,128)(2,1)}, bf16[256,768]{1,0:T(8,128)(2,1)S(1)}, u32[]{:S(2)}, u32[]{:S(2)}) collective-permute-start(bf16[256,768]{1,0:T(8,128)(2,1)} %add_convert_fusion.17), channel_id=1, source_target_pairs={{0,8},{1,5},{2,10},{3,7},{8,16},{9,1},{10,18},{11,3},{16,24},{17,9... | collective-permute-start | bytes 1179656 | tf_op jit(solution)/shard_map/ppermute | solution.py:849
  274.6 9.1 %collective-permute-start.35 = (bf16[480,512]{1,0:T(8,128)(2,1)}, bf16[480,512]{1,0:T(8,128)(2,1)}, u32[]{:S(2)}, u32[]{:S(2)}) collective-permute-start(bf16[480,512]{1,0:T(8,128)(2,1)} %add_convert_fusion.6), channel_id=1, source_target_pairs={{0,8},{1,5},{2,10},{3,7},{8,16},{9,1},{10,18},{11,3},{16,24},{17,9... | collective-permute-start | bytes 1474568 | tf_op jit(solution)/shard_map/ppermute | solution.py:849
  275.1 15.2 %collective-permute-start.45 = (bf16[128,1408]{1,0:T(8,128)(2,1)}, bf16[128,1408]{1,0:T(8,128)(2,1)S(1)}, u32[]{:S(2)}, u32[]{:S(2)}) collective-permute-start(bf16[128,1408]{1,0:T(8,128)(2,1)} %get-tuple-element.266), channel_id=1, source_target_pairs={{0,2},{1,3},{2,0},{3,1},{4,6},{5,7},{6,4},{7,5},{8,10},{9,11},{10,... | collective-permute-start | bytes 1081352 | tf_op jit(solution)/shard_map/ppermute | solution.py:862
  276.2 18.1 %collective-permute-start.27 = (bf16[128,1408]{1,0:T(8,128)(2,1)}, bf16[128,1408]{1,0:T(8,128)(2,1)S(1)}, u32[]{:S(2)}, u32[]{:S(2)}) collective-permute-start(bf16[128,1408]{1,0:T(8,128)(2,1)} %get-tuple-element.269), channel_id=1, source_target_pairs={{0,2},{1,3},{2,0},{3,1},{4,6},{5,7},{6,4},{7,5},{8,10},{9,11},{10,... | collective-permute-start | bytes 1081352 | tf_op jit(solution)/shard_map/ppermute | solution.py:862
  277.1 53.0 %collective-permute-start.48 = (bf16[128,1408]{1,0:T(8,128)(2,1)}, bf16[128,1408]{1,0:T(8,128)(2,1)}, u32[]{:S(2)}, u32[]{:S(2)}) collective-permute-start(bf16[128,1408]{1,0:T(8,128)(2,1)} %get-tuple-element.268), channel_id=1, source_target_pairs={{0,2},{1,3},{2,0},{3,1},{4,6},{5,7},{6,4},{7,5},{8,10},{9,11},{10,... | collective-permute-start | bytes 1081352 | tf_op jit(solution)/shard_map/ppermute | solution.py:862
  278.3 9.2 %collective-permute-start.44 = (bf16[128,1408]{1,0:T(8,128)(2,1)}, bf16[128,1408]{1,0:T(8,128)(2,1)S(1)}, u32[]{:S(2)}, u32[]{:S(2)}) collective-permute-start(bf16[128,1408]{1,0:T(8,128)(2,1)} %fusion.12), channel_id=1, source_target_pairs={{0,8},{1,5},{2,10},{3,7},{8,16},{9,1},{10,18},{11,3},{16,24},{17,9... | collective-permute-start | bytes 1081352 | tf_op jit(solution)/shard_map/ppermute | solution.py:849
  283.7 8.0 %collective-permute-start.26 = (bf16[256,768]{1,0:T(8,128)(2,1)S(1)}, bf16[256,768]{1,0:T(8,128)(2,1)S(1)}, u32[]{:S(2)}, u32[]{:S(2)}) collective-permute-start(bf16[256,768]{1,0:T(8,128)(2,1)S(1)} %add_convert_fusion.16), channel_id=1, source_target_pairs={{0,8},{1,5},{2,10},{3,7},{8,16},{9,1},{10,18},{11,3},{16,24},{17,9... | collective-permute-start | bytes 1179656 | tf_op jit(solution)/shard_map/ppermute | solution.py:849
  287.5 9.5 %collective-permute-start.36 = (bf16[480,512]{1,0:T(8,128)(2,1)S(1)}, bf16[480,512]{1,0:T(8,128)(2,1)S(1)}, u32[]{:S(2)}, u32[]{:S(2)}) collective-permute-start(bf16[480,512]{1,0:T(8,128)(2,1)S(1)} %add_convert_fusion.5), channel_id=1, source_target_pairs={{0,8},{1,5},{2,10},{3,7},{8,16},{9,1},{10,18},{11,3},{16,24},{17,9... | collective-permute-start | bytes 1474568 | tf_op jit(solution)/shard_map/ppermute | solution.py:849
  290.3 8.6 %copy-start.15 = (bf16[128,1408]{1,0:T(8,128)(2,1)}, bf16[128,1408]{1,0:T(8,128)(2,1)S(1)}, u32[]{:S(2)}) copy-start(bf16[128,1408]{1,0:T(8,128)(2,1)S(1)} %collective-permute-done.45) | copy-start | bytes 1081348
  290.3 53.2 %collective-permute-start.50 = (bf16[128,1408]{1,0:T(8,128)(2,1)}, bf16[128,1408]{1,0:T(8,128)(2,1)}, u32[]{:S(2)}, u32[]{:S(2)}) collective-permute-start(bf16[128,1408]{1,0:T(8,128)(2,1)} %get-tuple-element.267), channel_id=1, source_target_pairs={{0,2},{1,3},{2,0},{3,1},{4,6},{5,7},{6,4},{7,5},{8,10},{9,11},{10,... | collective-permute-start | bytes 1081352 | tf_op jit(solution)/shard_map/ppermute | solution.py:862
  291.7 23.5 %collective-permute-start.46 = (bf16[128,1408]{1,0:T(8,128)(2,1)}, bf16[128,1408]{1,0:T(8,128)(2,1)}, u32[]{:S(2)}, u32[]{:S(2)}) collective-permute-start(bf16[128,1408]{1,0:T(8,128)(2,1)} %fusion.10), channel_id=1, source_target_pairs={{0,8},{1,5},{2,10},{3,7},{8,16},{9,1},{10,18},{11,3},{16,24},{17,9... | collective-permute-start | bytes 1081352 | tf_op jit(solution)/shard_map/ppermute | solution.py:849
  294.3 16.2 %collective-permute-start.28 = (bf16[256,768]{1,0:T(8,128)(2,1)S(1)}, bf16[256,768]{1,0:T(8,128)(2,1)}, u32[]{:S(2)}, u32[]{:S(2)}) collective-permute-start(bf16[256,768]{1,0:T(8,128)(2,1)S(1)} %add_convert_fusion.15), channel_id=1, source_target_pairs={{0,8},{1,5},{2,10},{3,7},{8,16},{9,1},{10,18},{11,3},{16,24},{17,9... | collective-permute-start | bytes 1179656 | tf_op jit(solution)/shard_map/ppermute | solution.py:849
  298.3 13.9 %collective-permute-start.37 = (bf16[480,512]{1,0:T(8,128)(2,1)S(1)}, bf16[480,512]{1,0:T(8,128)(2,1)}, u32[]{:S(2)}, u32[]{:S(2)}) collective-permute-start(bf16[480,512]{1,0:T(8,128)(2,1)S(1)} %add_convert_fusion.4), channel_id=1, source_target_pairs={{0,8},{1,5},{2,10},{3,7},{8,16},{9,1},{10,18},{11,3},{16,24},{17,9... | collective-permute-start | bytes 1474568 | tf_op jit(solution)/shard_map/ppermute | solution.py:849
  311.8 7.8 %collective-permute-start.29 = (bf16[256,768]{1,0:T(8,128)(2,1)S(1)}, bf16[256,768]{1,0:T(8,128)(2,1)S(1)}, u32[]{:S(2)}, u32[]{:S(2)}) collective-permute-start(bf16[256,768]{1,0:T(8,128)(2,1)S(1)} %add_convert_fusion.14), channel_id=1, source_target_pairs={{0,8},{1,5},{2,10},{3,7},{8,16},{9,1},{10,18},{11,3},{16,24},{17,9... | collective-permute-start | bytes 1179656 | tf_op jit(solution)/shard_map/ppermute | solution.py:849
  313.7 15.1 %copy-start.14 = (bf16[128,1408]{1,0:T(8,128)(2,1)S(1)}, bf16[128,1408]{1,0:T(8,128)(2,1)}, u32[]{:S(2)}) copy-start(bf16[128,1408]{1,0:T(8,128)(2,1)} %copy-done.13) | copy-start | bytes 1081348
  313.7 11.2 %collective-permute-start.38 = (bf16[480,512]{1,0:T(8,128)(2,1)S(1)}, bf16[480,512]{1,0:T(8,128)(2,1)S(1)}, u32[]{:S(2)}, u32[]{:S(2)}) collective-permute-start(bf16[480,512]{1,0:T(8,128)(2,1)S(1)} %add_convert_fusion.3), channel_id=1, source_target_pairs={{0,8},{1,5},{2,10},{3,7},{8,16},{9,1},{10,18},{11,3},{16,24},{17,9... | collective-permute-start | bytes 1474568 | tf_op jit(solution)/shard_map/ppermute | solution.py:849
  316.6 12.2 %collective-permute-start.47 = (bf16[128,1408]{1,0:T(8,128)(2,1)S(1)}, bf16[128,1408]{1,0:T(8,128)(2,1)S(1)}, u32[]{:S(2)}, u32[]{:S(2)}) collective-permute-start(bf16[128,1408]{1,0:T(8,128)(2,1)S(1)} %fusion.8), channel_id=1, source_target_pairs={{0,8},{1,5},{2,10},{3,7},{8,16},{9,1},{10,18},{11,3},{16,24},{17,9... | collective-permute-start | bytes 1081352 | tf_op jit(solution)/shard_map/ppermute | solution.py:849
  320.8 12.2 %collective-permute-start.30 = (bf16[256,768]{1,0:T(8,128)(2,1)S(1)}, bf16[256,768]{1,0:T(8,128)(2,1)S(1)}, u32[]{:S(2)}, u32[]{:S(2)}) collective-permute-start(bf16[256,768]{1,0:T(8,128)(2,1)S(1)} %add_convert_fusion.13), channel_id=1, source_target_pairs={{0,8},{1,5},{2,10},{3,7},{8,16},{9,1},{10,18},{11,3},{16,24},{17,9... | collective-permute-start | bytes 1179656 | tf_op jit(solution)/shard_map/ppermute | solution.py:849
  326.3 12.0 %collective-permute-start.39 = (bf16[480,512]{1,0:T(8,128)(2,1)S(1)}, bf16[480,512]{1,0:T(8,128)(2,1)S(1)}, u32[]{:S(2)}, u32[]{:S(2)}) collective-permute-start(bf16[480,512]{1,0:T(8,128)(2,1)S(1)} %add_convert_fusion.2), channel_id=1, source_target_pairs={{0,8},{1,5},{2,10},{3,7},{8,16},{9,1},{10,18},{11,3},{16,24},{17,9... | collective-permute-start | bytes 1474568 | tf_op jit(solution)/shard_map/ppermute | solution.py:849
  330.1 12.1 %collective-permute-start.49 = (bf16[128,1408]{1,0:T(8,128)(2,1)S(1)}, bf16[128,1408]{1,0:T(8,128)(2,1)S(1)}, u32[]{:S(2)}, u32[]{:S(2)}) collective-permute-start(bf16[128,1408]{1,0:T(8,128)(2,1)S(1)} %fusion.6), channel_id=1, source_target_pairs={{0,8},{1,5},{2,10},{3,7},{8,16},{9,1},{10,18},{11,3},{16,24},{17,9... | collective-permute-start | bytes 1081352 | tf_op jit(solution)/shard_map/ppermute | solution.py:849
  334.2 12.2 %collective-permute-start.31 = (bf16[256,768]{1,0:T(8,128)(2,1)S(1)}, bf16[256,768]{1,0:T(8,128)(2,1)S(1)}, u32[]{:S(2)}, u32[]{:S(2)}) collective-permute-start(bf16[256,768]{1,0:T(8,128)(2,1)S(1)} %add_convert_fusion.12), channel_id=1, source_target_pairs={{0,8},{1,5},{2,10},{3,7},{8,16},{9,1},{10,18},{11,3},{16,24},{17,9... | collective-permute-start | bytes 1179656 | tf_op jit(solution)/shard_map/ppermute | solution.py:849
  339.6 9.3 %collective-permute-start.40 = (bf16[480,512]{1,0:T(8,128)(2,1)S(1)}, bf16[480,512]{1,0:T(8,128)(2,1)S(1)}, u32[]{:S(2)}, u32[]{:S(2)}) collective-permute-start(bf16[480,512]{1,0:T(8,128)(2,1)S(1)} %add_convert_fusion.1), channel_id=1, source_target_pairs={{0,2},{1,3},{2,0},{3,1},{4,6},{5,7},{6,4},{7,5},{8,10},{9,11},{10,... | collective-permute-start | bytes 1474568 | tf_op jit(solution)/shard_map/ppermute | solution.py:862
  343.5 7.5 %collective-permute-start.51 = (bf16[128,1408]{1,0:T(8,128)(2,1)S(1)}, bf16[128,1408]{1,0:T(8,128)(2,1)S(1)}, u32[]{:S(2)}, u32[]{:S(2)}) collective-permute-start(bf16[128,1408]{1,0:T(8,128)(2,1)S(1)} %fusion.4), channel_id=1, source_target_pairs={{0,8},{1,5},{2,10},{3,7},{8,16},{9,1},{10,18},{11,3},{16,24},{17,9... | collective-permute-start | bytes 1081352 | tf_op jit(solution)/shard_map/ppermute | solution.py:849
  348.2 10.7 %collective-permute-start.32 = (bf16[256,768]{1,0:T(8,128)(2,1)}, bf16[256,768]{1,0:T(8,128)(2,1)S(1)}, u32[]{:S(2)}, u32[]{:S(2)}) collective-permute-start(bf16[256,768]{1,0:T(8,128)(2,1)} %add_convert_fusion.11), channel_id=1, source_target_pairs={{0,8},{1,5},{2,10},{3,7},{8,16},{9,1},{10,18},{11,3},{16,24},{17,9... | collective-permute-start | bytes 1179656 | tf_op jit(solution)/shard_map/ppermute | solution.py:849
  349.8 4.5 %collective-permute-start.41 = (bf16[480,512]{1,0:T(8,128)(2,1)}, bf16[480,512]{1,0:T(8,128)(2,1)}, u32[]{:S(2)}, u32[]{:S(2)}) collective-permute-start(bf16[480,512]{1,0:T(8,128)(2,1)} %add_convert_fusion.refs_0_.out_ref), channel_id=1, source_target_pairs={{0,1},{1,0},{2,3},{3,2},{4,5},{5,4},{6,7},{7,6},{8,9},{9,8},{10,11... | collective-permute-start | bytes 1474568 | tf_op jit(solution)/shard_map/ppermute | solution.py:858
  353.1 10.3 %collective-permute-start.52 = (bf16[128,1408]{1,0:T(8,128)(2,1)}, bf16[128,1408]{1,0:T(8,128)(2,1)}, u32[]{:S(2)}, u32[]{:S(2)}) collective-permute-start(bf16[128,1408]{1,0:T(8,128)(2,1)} %fusion.2), channel_id=1, source_target_pairs={{0,2},{1,3},{2,0},{3,1},{4,6},{5,7},{6,4},{7,5},{8,10},{9,11},{10,... | collective-permute-start | bytes 1081352 | tf_op jit(solution)/shard_map/ppermute | solution.py:862
  360.9 13.5 %collective-permute-start.42 = (bf16[256,768]{1,0:T(8,128)(2,1)S(1)}, bf16[256,768]{1,0:T(8,128)(2,1)S(1)}, u32[]{:S(2)}, u32[]{:S(2)}) collective-permute-start(bf16[256,768]{1,0:T(8,128)(2,1)S(1)} %add_convert_fusion.10), channel_id=1, source_target_pairs={{0,2},{1,3},{2,0},{3,1},{4,6},{5,7},{6,4},{7,5},{8,10},{9,11},{10,... | collective-permute-start | bytes 1179656 | tf_op jit(solution)/shard_map/ppermute | solution.py:862
  364.6 4.9 %collective-permute-start.53 = (bf16[128,1408]{1,0:T(8,128)(2,1)S(1)}, bf16[128,1408]{1,0:T(8,128)(2,1)S(1)}, u32[]{:S(2)}, u32[]{:S(2)}) collective-permute-start(bf16[128,1408]{1,0:T(8,128)(2,1)S(1)} %get-tuple-element.275.refs_0_), channel_id=1, source_target_pairs={{0,1},{1,0},{2,3},{3,2},{4,5},{5,4},{6,7},{7,6},{8,9},{9,8},{10,11... | collective-permute-start | bytes 1081352 | tf_op jit(solution)/shard_map/ppermute | solution.py:858
  364.7 4.8 %collective-permute-start.54 = (bf16[128,1408]{1,0:T(8,128)(2,1)S(1)}, bf16[128,1408]{1,0:T(8,128)(2,1)S(1)}, u32[]{:S(2)}, u32[]{:S(2)}) collective-permute-start(bf16[128,1408]{1,0:T(8,128)(2,1)S(1)} %get-tuple-element.274.refs_1_), channel_id=1, source_target_pairs={{0,1},{1,0},{2,3},{3,2},{4,5},{5,4},{6,7},{7,6},{8,9},{9,8},{10,11... | collective-permute-start | bytes 1081352 | tf_op jit(solution)/shard_map/ppermute | solution.py:858
  374.5 5.5 %collective-permute-start.55 = (bf16[256,768]{1,0:T(8,128)(2,1)S(1)}, bf16[256,768]{1,0:T(8,128)(2,1)S(1)}, u32[]{:S(2)}, u32[]{:S(2)}) collective-permute-start(bf16[256,768]{1,0:T(8,128)(2,1)S(1)} %add_convert_fusion.9.qfv_ref), channel_id=1, source_target_pairs={{0,1},{1,0},{2,3},{3,2},{4,5},{5,4},{6,7},{7,6},{8,9},{9,8},{10,11... | collective-permute-start | bytes 1179656 | tf_op jit(solution)/shard_map/ppermute | solution.py:858
  (15 other events, 26.4 us)

commit v2 on v1

--- a/solution.py
+++ b/solution.py
@@ -681,7 +681,7 @@
     own_dots, up_dots, gate_dots, g_ref, gm_ref, ga_ref = held[:6]
     outs, gain_outs = held[-6:-3], held[-3:]
     kind = pl.program_id(0)
-    dots = dots_s.at[kind]
+    dots = dots_s.at[pl.ds(2 * kind, 2)]
     update_kernel(
         pick, step_rate, 2, core_ref, w_ref, m_ref, a_ref, qfv_ref, out_ref, *outs, dots
     )
@@ -709,22 +709,24 @@
     down_rows = out.shape[0] - shard
 
     def pick(core_index, proj, last):
-        gradient = last[down_rows:].astype(wide)
+        chosen = []
         for kind in range(3):
             parts = [proj[pair * shard :, kind * PAIR :][:shard, :PAIR] for pair in range(2)]
-            chosen = jnp.concatenate(parts, axis=1).astype(wide)
-            gradient = jnp.where(pl.program_id(0) == kind, chosen, gradient)
-        return gradient
+            chosen.append(jnp.concatenate(parts, axis=1).astype(wide))
+        chosen.append(last[down_rows:].astype(wide))
+        early = pl.program_id(0) == 0
+        both = [jnp.where(early, chosen[k], chosen[k + 2]) for k in range(2)]
+        return jnp.concatenate(both, axis=0)
 
     struct = jax.ShapeDtypeStruct
-    state_spec = pl.BlockSpec((1, shard, width // 2), lambda kind, half: (kind, 0, half[0]))
+    state_spec = pl.BlockSpec((2, shard, width // 2), lambda kind, half: (kind, 0, half[0]))
     in_specs = [state_spec] * 3 + [whole(qfv.shape), whole(out.shape)]
     out_specs = [state_spec] * 3
     out_shape = [struct(state[0].shape, wide)] * 3
     operands = [half_ref, *state, qfv, out]
     aliases, scratch, gain_step = {}, [], None
     if gains is None:
-        out_specs += [pl.BlockSpec((1, shard, HEAD_DIM), lambda kind, half: (kind, 0, 0))]
+        out_specs += [pl.BlockSpec((2, shard, HEAD_DIM), lambda kind, half: (kind, 0, 0))]
         out_shape += [struct((4, shard, HEAD_DIM), wide)]
     else:
         before, dots, gain_state, gain_step = gains
@@ -741,7 +743,7 @@
         functools.partial(update_attention_kernel, pick, step_rate, gain_step),
         grid_spec=pltpu.PrefetchScalarGridSpec(
             num_scalar_prefetch=1,
-            grid=(4,),
+            grid=(2,),
             in_specs=in_specs,
             out_specs=out_specs,
             scratch_shapes=scratch,

time: 391 us -> 388 us (level)
  no operation moved by 1% of the time
where the time goes in v2:
time: 388 us; the launch traced here: 384 us
  Pallas kernels  179 us (46%)
  waiting for transfers between devices  102 us (26%)
  other arithmetic  48.8 us (13%)
  starting transfers between devices  43.1 us (11%)
  local copies, waits for them, and re-layouts  10.4 us (3%)
    pallas_call x1, Pallas kernels, ffn(): pl.pallas_call(functools.partial(ffn_kernel, owners), grid_spec=pltpu.Pre...  58.1 us
    ppermute x6, waiting for transfers between devices, ring_shift(): return lax.ppermute(tensor, 'fsdp', pairs)  46.4 us
    pallas_call x4, Pallas kernels, mixer_backward(): pl.pallas_call(functools.partial(mixer_backward_kernel, slot, per_half, f...  34.2 us
    ppermute x22, waiting for transfers between devices, ring_next(): return lax.ppermute(tensor, ('fsdp', 'dp'), pairs)  30 us
    pallas_call x2, Pallas kernels, mixer_forward(): pl.pallas_call(functools.partial(kernel, slot), grid_spec=pltpu.PrefetchS...  25.2 us
    ppermute x18, waiting for transfers between devices, column_swap(): lax.ppermute(tensor, 'dp', [(d, d ^ 2) for d in range(lax.axis_size('dp'))])  24.5 us
    pallas_call x6, Pallas kernels, place(): pl.pallas_call(functools.partial(place_kernel, which, kept, shapes), grid...  22.7 us
    convert_element_type x14, other arithmetic, step(): (moved.astype(wide) + self.term().astype(wide)).astype(low)  19.8 us
  transfers between devices with their start and end apart: 56, of which 29 were waited for; matrix products, arithmetic and copies ran while one was open for 13% of the time, Pallas kernels for 28%

profile of v2, /device:TPU:0, one launch (start us, length us, event | category | flops | bytes accessed | tf_op | source)
XLA Modules:
  0.0 384.3 jit_solution(17139777910628405132)
XLA Ops:
  0.7 3.1 pack_all.1
  3.8 3.0 collective-permute-start
  7.3 3.3 place.6
  10.7 24.3 %collective-permute-done.refs_0_ = bf16[128,4992]{1,0:T(8,128)(2,1)S(1)} collective-permute-done((bf16[128,4992]{1,0:T(8,128)(2,1)}, bf16[128,4992]{1,0:T(8,128)(2,1)S(1)}, u32[]{:S(2)}, u32[]{:S(2)}) %collective-permute-start) | collective-permute-done | bytes 1277984 | tf_op jit(solution)/shard_map/ppermute | solution.py:856
  35.0 1.5 collective-permute-done.1.refs_1_
  37.6 1.6 collective-permute-start.2
  40.7 1.6 collective-permute-start.4
  42.8 3.4 norm_rows.1.nt_hbm
  46.2 2.9 fusion.e_ref
  49.1 3.9 %place.7 = (bf16[1024,2048]{1,0:T(8,128)(2,1)}, bf16[1024,2816]{1,0:T(8,128)(2,1)}, bf16[2816,512]{1,0:T(8,128)(2,1)}, bf16[16,1024]{1,0:T(8,128)(2,1)}) custom-call(s32[8]{0:T(128)} %compare_select_fusion.2.origin_ref, s32[1]{0:T(128)} %bitcast.1.column_ref, ...), custom_call_target="tpu_custom_call", output_to_operand_aliasing={{0}: (4, {}), {1}: (5, {}), {2}: (6, {}), {3}: (7, {})} | custom-call | bytes 10223616 | tf_op jit(solution)/shard_map/place/pallas_call | solution.py:971
  53.0 3.9 %collective-permute-done.5.refs_3_ = bf16[128,1408]{1,0:T(8,128)(2,1)} collective-permute-done((bf16[128,1408]{1,0:T(8,128)(2,1)S(1)}, bf16[128,1408]{1,0:T(8,128)(2,1)}, u32[]{:S(2)}, u32[]{:S(2)}) %collective-permute-start.5) | collective-permute-done | bytes 360480 | tf_op jit(solution)/shard_map/ppermute | solution.py:864
  57.0 9.4 %collective-permute-done.2.refs_0_ = bf16[128,4992]{1,0:T(8,128)(2,1)} collective-permute-done((bf16[128,4992]{1,0:T(8,128)(2,1)S(1)}, bf16[128,4992]{1,0:T(8,128)(2,1)}, u32[]{:S(2)}, u32[]{:S(2)}) %collective-permute-start.2) | collective-permute-done | bytes 1277984 | tf_op jit(solution)/shard_map/ppermute | solution.py:856
  68.8 1.6 collective-permute-start.6
  72.8 1.6 collective-permute-start.8
  74.9 4.6 %place.8 = (bf16[1024,2048]{1,0:T(8,128)(2,1)}, bf16[1024,2816]{1,0:T(8,128)(2,1)}, bf16[2816,512]{1,0:T(8,128)(2,1)}, bf16[16,1024]{1,0:T(8,128)(2,1)}) custom-call(s32[8]{0:T(128)} %compare_select_fusion.2.origin_ref, s32[1]{0:T(128)} %bitcast.1.column_ref, ...), custom_call_target="tpu_custom_call", output_to_operand_aliasing={{0}: (6, {}), {1}: (7, {}), {2}: (8, {}), {3}: (9, {})} | custom-call | bytes 13107200 | tf_op jit(solution)/shard_map/place/pallas_call | solution.py:971
  79.5 4.7 %collective-permute-done.8.refs_2_ = bf16[128,1408]{1,0:T(8,128)(2,1)} collective-permute-done((bf16[128,1408]{1,0:T(8,128)(2,1)S(1)}, bf16[128,1408]{1,0:T(8,128)(2,1)}, u32[]{:S(2)}, u32[]{:S(2)}) %collective-permute-start.8) | collective-permute-done | bytes 360480 | tf_op jit(solution)/shard_map/ppermute | solution.py:864
  84.2 3.9 %collective-permute-done.9.refs_3_ = bf16[128,1408]{1,0:T(8,128)(2,1)} collective-permute-done((bf16[128,1408]{1,0:T(8,128)(2,1)S(1)}, bf16[128,1408]{1,0:T(8,128)(2,1)}, u32[]{:S(2)}, u32[]{:S(2)}) %collective-permute-start.9) | collective-permute-done | bytes 360480 | tf_op jit(solution)/shard_map/ppermute | solution.py:864
  88.0 8.5 %collective-permute-done.6.refs_0_ = bf16[128,4992]{1,0:T(8,128)(2,1)S(1)} collective-permute-done((bf16[128,4992]{1,0:T(8,128)(2,1)}, bf16[128,4992]{1,0:T(8,128)(2,1)S(1)}, u32[]{:S(2)}, u32[]{:S(2)}) %collective-permute-start.6) | collective-permute-done | bytes 1277984 | tf_op jit(solution)/shard_map/ppermute | solution.py:856
  99.1 1.8 collective-permute-start.10
  101.0 1.6 collective-permute-start.11
  103.1 4.5 %place.9 = (bf16[1024,2048]{1,0:T(8,128)(2,1)}, bf16[1024,2816]{1,0:T(8,128)(2,1)}, bf16[2816,512]{1,0:T(8,128)(2,1)}, bf16[16,1024]{1,0:T(8,128)(2,1)}) custom-call(s32[8]{0:T(128)} %compare_select_fusion.2.origin_ref, s32[1]{0:T(128)} %bitcast.1.column_ref, ...), custom_call_target="tpu_custom_call", output_to_operand_aliasing={{0}: (6, {}), {1}: (7, {}), {2}: (8, {}), {3}: (9, {})} | custom-call | bytes 13107200 | tf_op jit(solution)/shard_map/place/pallas_call | solution.py:971
  107.6 2.6 collective-permute-done.11.refs_1_
  110.2 4.0 %collective-permute-done.12.refs_2_ = bf16[128,1408]{1,0:T(8,128)(2,1)} collective-permute-done((bf16[128,1408]{1,0:T(8,128)(2,1)S(1)}, bf16[128,1408]{1,0:T(8,128)(2,1)}, u32[]{:S(2)}, u32[]{:S(2)}) %collective-permute-start.12) | collective-permute-done | bytes 360480 | tf_op jit(solution)/shard_map/ppermute | solution.py:864
  114.2 2.8 collective-permute-done.10.refs_0_
  116.9 3.6 place.10
  121.7 1.6 collective-permute-start.13
  123.3 9.9 %mixer_forward.2 = (bf16[768,512]{1,0:T(8,128)(2,1)}, f32[768,512]{1,0:T(8,128)}, f32[768,512]{1,0:T(8,128)}, bf16[768,512]{1,0:T(8,128)(2,1)}, bf16[768,512]{1,0:T(8,128)(2,1)}, /*index=5*/f32[8,1024]{1,0:T(8,128)}) custom-call(s32[1]{0:T(128)} %bitcast.core_ref.half_ref, bf16[768,1024]{1,0:T(8,128)(2,1)} %bitcast.82, ...), custom_call_target="tpu_custom_call" | custom-call | flops 6241124352 | bytes 13631488 | tf_op jit(solution)/shard_map/mixer_forward/pallas_call | solution.py:239
  133.9 2.7 place.11.wm_ref
  137.8 15.3 %mixer_forward.3 = (bf16[768,512]{1,0:T(8,128)(2,1)}, f32[768,512]{1,0:T(8,128)}, f32[768,512]{1,0:T(8,128)}, bf16[768,512]{1,0:T(8,128)(2,1)}, bf16[768,512]{1,...) custom-call(s32[1]{0:T(128)S(6)} %sub.55.half_ref.core_ref, ...), custom_call_target="tpu_custom_call" | custom-call | flops 6241124352 | bytes 13631488 | tf_op jit(solution)/shard_map/mixer_forward/pallas_call | solution.py:239
  153.1 58.1 %ffn.1 = (bf16[2,1024,1408]{2,1,0:T(8,128)(2,1)}, bf16[2,1024,1408]{2,1,0:T(8,128)(2,1)}, bf16[3840,512]{1,0:T(8,128)(2,1)}, bf16[3840,512]{1,0:T(8,128)(2,1)}, ...) custom-call(s32[2]{0:T(128)} %pad_add_fusion.core_ref, ...), custom_call_target="tpu_custom_call" | custom-call | flops 39862665216 | bytes 50331648 | tf_op jit(solution)/shard_map/ffn/pallas_call | solution.py:420
  211.8 8.6 %mixer_backward.4 = (bf16[8,2,128,768]{3,2,1,0:T(8,128)(2,1)}, bf16[768,1536]{1,0:T(8,128)(2,1)}) custom-call(s32[1]{0:T(128)S(6)} %sub.55.half_ref.core_ref, bf16[1024,768]{1,0:T(8,128)(2,1)} %norm_rows.1.nt_hbm, f32[8,1024]{1,0:T(8,128)} %get-tuple-element.194.g_ref, f32[768,512]{1,0:T(8,128)} %get-tuple-element.201.q_ref, ...), custom_call_target="tpu_custom_call" | custom-call | flops 2717908992 | bytes 5505024 | tf_op jit(solution)/shard_map/mixer_backward/pallas_call | solution.py:547
  221.0 4.3 %fusion.21 = (bf16[128,1408]{1,0:T(8,128)(2,1)}, bf16[128,1408]{1,0:T(8,128)(2,1)}, bf16[128,1408]{1,0:T(8,128)(2,1)}, bf16[128,1408]{1,0:T(8,128)(2,1)}, bf16[1...) fusion(bf16[2,1024,1408]{2,1,0:T(8,128)(2,1)} %collective-permu, ...), kind=kLoop, calls=%fused_computation.57 | loop fusion | flops 5767168 | bytes 8650784 | tf_op jit(solution)/shard_map/convert_element_type | solution.py:1020
  226.2 8.6 %mixer_backward.5 = (bf16[8,2,128,768]{3,2,1,0:T(8,128)(2,1)}, bf16[768,1536]{1,0:T(8,128)(2,1)}) custom-call(s32[1]{0:T(128)S(6)} %sub.55.half_ref.core_ref, bf16[1024,768]{1,0:T(8,128)(2,1)} %norm_rows.1.nt_hbm, f32[8,1024]{1,0:T(8,128)} %get-tuple-element.194.g_ref, ...), custom_call_target="tpu_custom_call", output_to_operand_aliasing={{0}: (8, {}), {1}: (9, {})} | custom-call | flops 2717908992 | bytes 5505024 | tf_op jit(solution)/shard_map/mixer_backward/pallas_call | solution.py:547
  237.4 1.6 collective-permute-start.22
  241.8 8.5 %mixer_backward.6 = (bf16[8,2,128,768]{3,2,1,0:T(8,128)(2,1)}, bf16[768,1536]{1,0:T(8,128)(2,1)}) custom-call(s32[1]{0:T(128)} %bitcast.core_ref.half_ref, bf16[1024,768]{1,0:T(8,128)(2,1)} %norm_rows.1.nt_hbm, f32[8,1024]{1,0:T(8,128)} %get-tuple-element.194.g_ref, f32[768,512]{1,0:T(8,128)} %get-tuple-element.217.q_ref, ...), custom_call_target="tpu_custom_call" | custom-call | flops 2717908992 | bytes 5505024 | tf_op jit(solution)/shard_map/mixer_backward/pallas_call | solution.py:547
  253.6 2.0 fusion.14
  255.6 2.5 collective-permute-done.23
  258.8 8.5 %mixer_backward.7 = (bf16[8,2,128,768]{3,2,1,0:T(8,128)(2,1)}, bf16[768,1536]{1,0:T(8,128)(2,1)}) custom-call(s32[1]{0:T(128)} %bitcast.core_ref.half_ref, bf16[1024,768]{1,0:T(8,128)(2,1)} %norm_rows.1.nt_hbm, f32[8,1024]{1,0:T(8,128)} %get-tuple-element.194.g_ref, ...), custom_call_target="tpu_custom_call", output_to_operand_aliasing={{0}: (8, {}), {1}: (9, {})} | custom-call | flops 2717908992 | bytes 5505024 | tf_op jit(solution)/shard_map/mixer_backward/pallas_call | solution.py:547
  267.3 2.1 add_convert_fusion.17
  270.0 2.2 fusion.12
  272.3 2.3 add_convert_fusion.6
  279.6 4.1 %collective-permute-done.35 = bf16[480,512]{1,0:T(8,128)(2,1)} collective-permute-done((bf16[480,512]{1,0:T(8,128)(2,1)}, bf16[480,512]{1,0:T(8,128)(2,1)}, u32[]{:S(2)}, u32[]{:S(2)}) %collective-permute-start.35) | collective-permute-done | bytes 491552 | tf_op jit(solution)/shard_map/ppermute | solution.py:851
  284.2 1.5 add_convert_fusion.5
  285.7 1.7 collective-permute-done.44
  288.2 2.1 fusion.10
  294.6 2.3 collective-permute-done.36
  298.9 11.6 %input_gradient.1 = f32[768,1024]{1,0:T(8,128)} custom-call(bf16[768,1024]{1,0:T(8,128)(2,1)} %bitcast.84, f32[8,1024]{1,0:T(8,128)} %get-tuple-element.194.g_ref, bf16[768,1536]{1,0:T(8,128)(2,1)} %get-tuple-element.230.dm_ref, bf16[768,1536]{1,0:T(8,128)(2,1)} %get-tuple-element.211.do_ref, bf16[1024,2048]{1,0:T(8,128)(2,1)} %get-tuple-element.187.w_ref.wom_hbm.wm_ref, ...), custom_call_target="tpu_custom_call" | custom-call | flops 4831838208 | bytes 18874368 | tf_op jit(solution)/shard_map/input_gradient/pallas_call | solution.py:600
  312.2 1.5 add_convert_fusion.3
  313.7 1.5 collective-permute-start.38
  316.6 1.5 collective-permute-start.47
  318.1 1.6 collective-permute-done.29
  321.1 3.8 collective-permute-done.38
  326.6 2.2 collective-permute-done.47
  330.4 2.6 collective-permute-done.30
  334.5 3.8 collective-permute-done.39
  343.9 2.5 collective-permute-done.31
  346.4 1.9 add_convert_fusion.11
  351.0 2.1 fusion.2
  354.3 4.6 %update_ffn_out.1 = (f32[352,1024]{1,0:T(8,128)}, f32[352,1024]{1,0:T(8,128)}, f32[352,1024]{1,0:T(8,128)}, f32[2,352,128]{2,1,0:T(8,128)}) custom-call(s32[1]{0:T(128)} %bitcast.core_ref.half_ref, f32[352,1024]{1,0:T(8,128)} %w_ref.7, f32[352,1024]{1,0:T(8,128)} %m_ref.5, f32[352,1024]{1,0:T(8,128)} %a_ref.5, ...), custom_call_target="tpu_custom_call" | custom-call | flops 4325376 | bytes 9371648 | tf_op jit(solution)/shard_map/update_ffn_out/pallas_call | solution.py:656
  361.9 1.5 collective-permute-done.52
  365.4 4.0 %update_ffn_in.2 = (f32[2,128,2816]{2,1,0:T(8,128)}, f32[2,128,2816]{2,1,0:T(8,128)}, f32[2,128,2816]{2,1,0:T(8,128)}, f32[2,64,128]{2,1,0:T(8,128)}) custom-call(s32[1]{0:T(128)} %bitcast.core_ref.half_ref, f32[2,128,2816]{2,1,0:T(8,128)} %w_ref.9, f32[2,128,2816]{2,1,0:T(8,128)} %m_ref.7, f32[2,128,2816]{2,1,0:T(8,128)} %a_ref.7, ...), custom_call_target="tpu_custom_call" | custom-call | flops 8650752 | bytes 18743296 | tf_op jit(solution)/shard_map/update_ffn_in/pallas_call | solution.py:656
  370.3 4.0 %update_ffn_in.3 = (f32[2,128,2816]{2,1,0:T(8,128)}, f32[2,128,2816]{2,1,0:T(8,128)}, f32[2,128,2816]{2,1,0:T(8,128)}, f32[2,64,128]{2,1,0:T(8,128)}) custom-call(s32[1]{0:T(128)S(6)} %sub.55.half_ref.core_ref, f32[2,128,2816]{2,1,0:T(8,128)} %w_ref.9, f32[2,128,2816]{2,1,0:T(8,128)} %m_ref.7, ...), custom_call_target="tpu_custom_call", output_to_operand_aliasing={{0}: (6, {}), {1}: (7, {}), {2}: (8, {})} | custom-call | flops 8650752 | bytes 18743296 | tf_op jit(solution)/shard_map/update_ffn_in/pallas_call | solution.py:656
  375.3 3.8 update_attention.2
  379.9 4.0 %update_attention.3 = (f32[4,128,1024]{2,1,0:T(8,128)}, f32[4,128,1024]{2,1,0:T(8,128)}, f32[4,128,1024]{2,1,0:T(8,128)}, f32[3,128]{1,0:T(4,128)}, f32[3,128]{1,0:T(4,128)}, /*index=5*/f32[3,128]{1,0:T(4,128)}) custom-call(s32[1]{0:T(128)S(6)} %sub.55.half_ref.core_ref, ...), custom_call_target="tpu_custom_call", output_to_operand_aliasing={{0}: (12, {}), {1}: (13, {}), {2}: (14, {})} | custom-call | flops 3145728 | bytes 6815744 | tf_op jit(solution)/shard_map/update_attention/pallas_call | solution.py:742
  (156 shorter events, 66.1 us)
Async XLA Ops:
  0.7 6.1 %copy-start.22 = (s32[8]{0:T(128)S(1)}, s32[8]{0:T(128)}, u32[]{:S(2)}) copy-start(s32[8]{0:T(128)} %constant.225.clone) | copy-start | bytes 100
  3.8 39.0 %copy-start.21 = (s32[2,1]{0,1:T(1,128)S(1)}, s32[2,1]{0,1:T(1,128)}, u32[]{:S(2)}) copy-start(s32[2,1]{0,1:T(1,128)} %param.18) | copy-start | bytes 28
  3.8 31.2 %collective-permute-start = (bf16[128,4992]{1,0:T(8,128)(2,1)}, bf16[128,4992]{1,0:T(8,128)(2,1)S(1)}, u32[]{:S(2)}, u32[]{:S(2)}) collective-permute-start(bf16[128,4992]{1,0:T(8,128)(2,1)} %get-tuple-element.140.refs_0_), channel_id=1, source_target_pairs={{0,8},{8,16},{16,24},{24,28},{28,20},{20,12},{12,4},{4,0},{1,9},{9... | collective-permute-start | bytes 3833864 | tf_op jit(solution)/shard_map/ppermute | solution.py:856
  6.8 29.7 %collective-permute-start.1 = (bf16[128,4992]{1,0:T(8,128)(2,1)}, bf16[128,4992]{1,0:T(8,128)(2,1)S(1)}, u32[]{:S(2)}, u32[]{:S(2)}) collective-permute-start(bf16[128,4992]{1,0:T(8,128)(2,1)} %get-tuple-element.140.refs_0_), channel_id=1, source_target_pairs={{0,4},{8,0},{16,8},{24,16},{28,24},{20,28},{12,20},{4,12},{1,5},{9... | collective-permute-start | bytes 3833864 | tf_op jit(solution)/shard_map/ppermute | solution.py:856
  35.0 14.1 %copy-start.5 = (bf16[128,4992]{1,0:T(8,128)(2,1)}, bf16[128,4992]{1,0:T(8,128)(2,1)S(1)}, u32[]{:S(2)}) copy-start(bf16[128,4992]{1,0:T(8,128)(2,1)S(1)} %collective-permute-done.refs_0_) | copy-start | bytes 3833860
  37.6 28.7 %collective-permute-start.2 = (bf16[128,4992]{1,0:T(8,128)(2,1)S(1)}, bf16[128,4992]{1,0:T(8,128)(2,1)}, u32[]{:S(2)}, u32[]{:S(2)}) collective-permute-start(bf16[128,4992]{1,0:T(8,128)(2,1)S(1)} %collective-permute-done.refs_0_), channel_id=1, source_target_pairs={{0,8},{8,16},{16,24},{24,28},{28,20},{20,12},{12,4},{4,0},{1,9},{9... | collective-permute-start | bytes 3833864 | tf_op jit(solution)/shard_map/ppermute | solution.py:856
  39.2 28.6 %collective-permute-start.3 = (bf16[128,4992]{1,0:T(8,128)(2,1)}, bf16[128,4992]{1,0:T(8,128)(2,1)S(1)}, u32[]{:S(2)}, u32[]{:S(2)}) collective-permute-start(bf16[128,4992]{1,0:T(8,128)(2,1)} %copy-done.6), channel_id=1, source_target_pairs={{0,4},{8,0},{16,8},{24,16},{28,24},{20,28},{12,20},{4,12},{1,5},{9... | collective-permute-start | bytes 3833864 | tf_op jit(solution)/shard_map/ppermute | solution.py:856
  40.7 12.4 %collective-permute-start.4 = (bf16[128,1408]{1,0:T(8,128)(2,1)S(1)}, bf16[128,1408]{1,0:T(8,128)(2,1)}, u32[]{:S(2)}, u32[]{:S(2)}) collective-permute-start(bf16[128,1408]{1,0:T(8,128)(2,1)S(1)} %slice.21), channel_id=1, source_target_pairs={{0,2},{1,3},{2,0},{3,1},{4,6},{5,7},{6,4},{7,5},{8,10},{9,11},{10,... | collective-permute-start | bytes 1081352 | tf_op jit(solution)/shard_map/ppermute | solution.py:864
  42.2 14.7 %collective-permute-start.5 = (bf16[128,1408]{1,0:T(8,128)(2,1)S(1)}, bf16[128,1408]{1,0:T(8,128)(2,1)}, u32[]{:S(2)}, u32[]{:S(2)}) collective-permute-start(bf16[128,1408]{1,0:T(8,128)(2,1)S(1)} %slice.22), channel_id=1, source_target_pairs={{0,2},{1,3},{2,0},{3,1},{4,6},{5,7},{6,4},{7,5},{8,10},{9,11},{10,... | collective-permute-start | bytes 1081352 | tf_op jit(solution)/shard_map/ppermute | solution.py:864
  68.8 27.7 %collective-permute-start.6 = (bf16[128,4992]{1,0:T(8,128)(2,1)}, bf16[128,4992]{1,0:T(8,128)(2,1)S(1)}, u32[]{:S(2)}, u32[]{:S(2)}) collective-permute-start(bf16[128,4992]{1,0:T(8,128)(2,1)} %collective-permute-done.2.refs_0_), channel_id=1, source_target_pairs={{0,8},{8,16},{16,24},{24,28},{28,20},{20,12},{12,4},{4,0},{1,9},{9... | collective-permute-start | bytes 3833864 | tf_op jit(solution)/shard_map/ppermute | solution.py:856
  70.3 27.5 %collective-permute-start.7 = (bf16[128,4992]{1,0:T(8,128)(2,1)}, bf16[128,4992]{1,0:T(8,128)(2,1)S(1)}, u32[]{:S(2)}, u32[]{:S(2)}) collective-permute-start(bf16[128,4992]{1,0:T(8,128)(2,1)} %copy-done.4), channel_id=1, source_target_pairs={{0,4},{8,0},{16,8},{24,16},{28,24},{20,28},{12,20},{4,12},{1,5},{9... | collective-permute-start | bytes 3833864 | tf_op jit(solution)/shard_map/ppermute | solution.py:856
  72.8 11.3 %collective-permute-start.8 = (bf16[128,1408]{1,0:T(8,128)(2,1)S(1)}, bf16[128,1408]{1,0:T(8,128)(2,1)}, u32[]{:S(2)}, u32[]{:S(2)}) collective-permute-start(bf16[128,1408]{1,0:T(8,128)(2,1)S(1)} %slice.23), channel_id=1, source_target_pairs={{0,2},{1,3},{2,0},{3,1},{4,6},{5,7},{6,4},{7,5},{8,10},{9,11},{10,... | collective-permute-start | bytes 1081352 | tf_op jit(solution)/shard_map/ppermute | solution.py:864
  74.4 13.6 %collective-permute-start.9 = (bf16[128,1408]{1,0:T(8,128)(2,1)S(1)}, bf16[128,1408]{1,0:T(8,128)(2,1)}, u32[]{:S(2)}, u32[]{:S(2)}) collective-permute-start(bf16[128,1408]{1,0:T(8,128)(2,1)S(1)} %slice.24), channel_id=1, source_target_pairs={{0,2},{1,3},{2,0},{3,1},{4,6},{5,7},{6,4},{7,5},{8,10},{9,11},{10,... | collective-permute-start | bytes 1081352 | tf_op jit(solution)/shard_map/ppermute | solution.py:864
  96.5 6.6 %copy-start.2 = (bf16[128,4992]{1,0:T(8,128)(2,1)}, bf16[128,4992]{1,0:T(8,128)(2,1)S(1)}, u32[]{:S(2)}) copy-start(bf16[128,4992]{1,0:T(8,128)(2,1)S(1)} %collective-permute-done.6.refs_0_) | copy-start | bytes 3833860
  99.1 17.8 %collective-permute-start.10 = (bf16[128,4992]{1,0:T(8,128)(2,1)}, bf16[128,4992]{1,0:T(8,128)(2,1)}, u32[]{:S(2)}, u32[]{:S(2)}) collective-permute-start(bf16[128,4992]{1,0:T(8,128)(2,1)} %broadcast_select_fusion), channel_id=1, source_target_pairs={{0,8},{1,5},{2,10},{3,7},{8,16},{9,1},{10,18},{11,3},{16,24},{17,9... | collective-permute-start | bytes 3833864 | tf_op jit(solution)/shard_map/ppermute | solution.py:851
  101.0 9.2 %collective-permute-start.11 = (bf16[128,1408]{1,0:T(8,128)(2,1)S(1)}, bf16[128,1408]{1,0:T(8,128)(2,1)S(1)}, u32[]{:S(2)}, u32[]{:S(2)}) collective-permute-start(bf16[128,1408]{1,0:T(8,128)(2,1)S(1)} %slice.25), channel_id=1, source_target_pairs={{0,2},{1,3},{2,0},{3,1},{4,6},{5,7},{6,4},{7,5},{8,10},{9,11},{10,... | collective-permute-start | bytes 1081352 | tf_op jit(solution)/shard_map/ppermute | solution.py:864
  102.5 11.7 %collective-permute-start.12 = (bf16[128,1408]{1,0:T(8,128)(2,1)S(1)}, bf16[128,1408]{1,0:T(8,128)(2,1)}, u32[]{:S(2)}, u32[]{:S(2)}) collective-permute-start(bf16[128,1408]{1,0:T(8,128)(2,1)S(1)} %slice.26), channel_id=1, source_target_pairs={{0,2},{1,3},{2,0},{3,1},{4,6},{5,7},{6,4},{7,5},{8,10},{9,11},{10,... | collective-permute-start | bytes 1081352 | tf_op jit(solution)/shard_map/ppermute | solution.py:864
  110.2 6.7 %copy-start.18 = (bf16[128,1408]{1,0:T(8,128)(2,1)}, bf16[128,1408]{1,0:T(8,128)(2,1)S(1)}, u32[]{:S(2)}) copy-start(bf16[128,1408]{1,0:T(8,128)(2,1)S(1)} %collective-permute-done.11.refs_1_) | copy-start | bytes 1081348
  120.6 12.6 %collective-permute-start.14 = (bf16[1024,2048]{1,0:T(8,128)(2,1)}, bf16[1024,2048]{1,0:T(8,128)(2,1)}, u32[]{:S(2)}, u32[]{:S(2)}) collective-permute-start(bf16[1024,2048]{1,0:T(8,128)(2,1)} %get-tuple-element.187.w_ref.wom_hbm.wm_ref), channel_id=1, source_target_pairs={{0,1},{1,0},{2,3},{3,2},{4,5},{5,4},{6,7},{7,6},{8,9},{9,8},{10,11... | collective-permute-start | bytes 12582920 | tf_op jit(solution)/shard_map/ppermute | solution.py:860
  121.7 11.5 %collective-permute-start.13 = (bf16[128,1408]{1,0:T(8,128)(2,1)S(1)}, bf16[128,1408]{1,0:T(8,128)(2,1)S(1)}, u32[]{:S(2)}, u32[]{:S(2)}) collective-permute-start(bf16[128,1408]{1,0:T(8,128)(2,1)S(1)} %slice.27), channel_id=1, source_target_pairs={{0,2},{1,3},{2,0},{3,1},{4,6},{5,7},{6,4},{7,5},{8,10},{9,11},{10,... | collective-permute-start | bytes 1081352 | tf_op jit(solution)/shard_map/ppermute | solution.py:864
  136.6 16.5 %collective-permute-start.15 = (bf16[1024,2816]{1,0:T(8,128)(2,1)}, bf16[1024,2816]{1,0:T(8,128)(2,1)}, u32[]{:S(2)}, u32[]{:S(2)}) collective-permute-start(bf16[1024,2816]{1,0:T(8,128)(2,1)} %place.11.wm_ref), channel_id=1, source_target_pairs={{0,1},{1,0},{2,3},{3,2},{4,5},{5,4},{6,7},{7,6},{8,9},{9,8},{10,11... | collective-permute-start | bytes 17301512 | tf_op jit(solution)/shard_map/ppermute | solution.py:860
  136.9 16.2 %collective-permute-start.16 = (bf16[2816,512]{1,0:T(8,128)(2,1)S(1)}, bf16[2816,512]{1,0:T(8,128)(2,1)}, u32[]{:S(2)}, u32[]{:S(2)}) collective-permute-start(bf16[2816,512]{1,0:T(8,128)(2,1)S(1)} %copy-done), channel_id=1, source_target_pairs={{0,1},{1,0},{2,3},{3,2},{4,5},{5,4},{6,7},{7,6},{8,9},{9,8},{10,11... | collective-permute-start | bytes 8650760 | tf_op jit(solution)/shard_map/ppermute | solution.py:860
  211.2 9.8 %collective-permute-start.17 = (bf16[2,1024,1408]{2,1,0:T(8,128)(2,1)}, bf16[2,1024,1408]{2,1,0:T(8,128)(2,1)}, u32[]{:S(2)}, u32[]{:S(2)}) collective-permute-start(bf16[2,1024,1408]{2,1,0:T(8,128)(2,1)} %get-tuple-element.208), channel_id=1, source_target_pairs={{0,1},{1,0},{2,3},{3,2},{4,5},{5,4},{6,7},{7,6},{8,9},{9,8},{10,11... | collective-permute-start | bytes 17301512 | tf_op jit(solution)/shard_map/ppermute | solution.py:860
  211.5 23.3 %collective-permute-start.19 = (bf16[3840,512]{1,0:T(8,128)(2,1)}, bf16[3840,512]{1,0:T(8,128)(2,1)}, u32[]{:S(2)}, u32[]{:S(2)}) collective-permute-start(bf16[3840,512]{1,0:T(8,128)(2,1)} %get-tuple-element.215), channel_id=1, source_target_pairs={{0,1},{1,0},{2,3},{3,2},{4,5},{5,4},{6,7},{7,6},{8,9},{9,8},{10,11... | collective-permute-start | bytes 11796488 | tf_op jit(solution)/shard_map/ppermute | solution.py:860
  225.3 10.8 %collective-permute-start.18 = (bf16[128,1408]{1,0:T(8,128)(2,1)S(1)}, bf16[128,1408]{1,0:T(8,128)(2,1)S(1)}, u32[]{:S(2)}, u32[]{:S(2)}) collective-permute-start(bf16[128,1408]{1,0:T(8,128)(2,1)S(1)} %get-tuple-element.273), channel_id=1, source_target_pairs={{0,2},{1,3},{2,0},{3,1},{4,6},{5,7},{6,4},{7,5},{8,10},{9,11},{10,... | collective-permute-start | bytes 1081352 | tf_op jit(solution)/shard_map/ppermute | solution.py:864
  237.3 30.0 %collective-permute-start.24 = (bf16[2048,768]{1,0:T(8,128)(2,1)}, bf16[2048,768]{1,0:T(8,128)(2,1)}, u32[]{:S(2)}, u32[]{:S(2)}) collective-permute-start(bf16[2048,768]{1,0:T(8,128)(2,1)} %bitcast.86), channel_id=1, source_target_pairs={{0,1},{1,0},{2,3},{3,2},{4,5},{5,4},{6,7},{7,6},{8,9},{9,8},{10,11... | collective-permute-start | bytes 9437192 | tf_op jit(solution)/shard_map/ppermute | solution.py:860
  237.4 12.9 %collective-permute-start.22 = (bf16[480,512]{1,0:T(8,128)(2,1)S(1)}, bf16[480,512]{1,0:T(8,128)(2,1)S(1)}, u32[]{:S(2)}, u32[]{:S(2)}) collective-permute-start(bf16[480,512]{1,0:T(8,128)(2,1)S(1)} %add_convert_fusion.8), channel_id=1, source_target_pairs={{0,8},{1,5},{2,10},{3,7},{8,16},{9,1},{10,18},{11,3},{16,24},{17,9... | collective-permute-start | bytes 1474568 | tf_op jit(solution)/shard_map/ppermute | solution.py:851
  239.0 14.6 %collective-permute-start.21 = (bf16[128,1408]{1,0:T(8,128)(2,1)S(1)}, bf16[128,1408]{1,0:T(8,128)(2,1)S(1)}, u32[]{:S(2)}, u32[]{:S(2)}) collective-permute-start(bf16[128,1408]{1,0:T(8,128)(2,1)S(1)} %get-tuple-element.272), channel_id=1, source_target_pairs={{0,2},{1,3},{2,0},{3,1},{4,6},{5,7},{6,4},{7,5},{8,10},{9,11},{10,... | collective-permute-start | bytes 1081352 | tf_op jit(solution)/shard_map/ppermute | solution.py:864
  240.1 17.9 %collective-permute-start.23 = (bf16[128,1408]{1,0:T(8,128)(2,1)S(1)}, bf16[128,1408]{1,0:T(8,128)(2,1)S(1)}, u32[]{:S(2)}, u32[]{:S(2)}) collective-permute-start(bf16[128,1408]{1,0:T(8,128)(2,1)S(1)} %get-tuple-element.271), channel_id=1, source_target_pairs={{0,2},{1,3},{2,0},{3,1},{4,6},{5,7},{6,4},{7,5},{8,10},{9,11},{10,... | collective-permute-start | bytes 1081352 | tf_op jit(solution)/shard_map/ppermute | solution.py:864
  241.0 11.9 %collective-permute-start.20 = (bf16[128,1408]{1,0:T(8,128)(2,1)S(1)}, bf16[128,1408]{1,0:T(8,128)(2,1)S(1)}, u32[]{:S(2)}, u32[]{:S(2)}) collective-permute-start(bf16[128,1408]{1,0:T(8,128)(2,1)S(1)} %fusion.15), channel_id=1, source_target_pairs={{0,8},{1,5},{2,10},{3,7},{8,16},{9,1},{10,18},{11,3},{16,24},{17,9... | collective-permute-start | bytes 1081352 | tf_op jit(solution)/shard_map/ppermute | solution.py:851
  250.4 26.7 %collective-permute-start.43 = (bf16[128,1408]{1,0:T(8,128)(2,1)}, bf16[128,1408]{1,0:T(8,128)(2,1)}, u32[]{:S(2)}, u32[]{:S(2)}) collective-permute-start(bf16[128,1408]{1,0:T(8,128)(2,1)} %get-tuple-element.270), channel_id=1, source_target_pairs={{0,2},{1,3},{2,0},{3,1},{4,6},{5,7},{6,4},{7,5},{8,10},{9,11},{10,... | collective-permute-start | bytes 1081352 | tf_op jit(solution)/shard_map/ppermute | solution.py:864
  252.9 17.1 %collective-permute-start.33 = (bf16[480,512]{1,0:T(8,128)(2,1)S(1)}, bf16[480,512]{1,0:T(8,128)(2,1)}, u32[]{:S(2)}, u32[]{:S(2)}) collective-permute-start(bf16[480,512]{1,0:T(8,128)(2,1)S(1)} %add_convert_fusion.7), channel_id=1, source_target_pairs={{0,8},{1,5},{2,10},{3,7},{8,16},{9,1},{10,18},{11,3},{16,24},{17,9... | collective-permute-start | bytes 1474568 | tf_op jit(solution)/shard_map/ppermute | solution.py:851
  258.0 12.0 %collective-permute-start.34 = (bf16[128,1408]{1,0:T(8,128)(2,1)}, bf16[128,1408]{1,0:T(8,128)(2,1)}, u32[]{:S(2)}, u32[]{:S(2)}) collective-permute-start(bf16[128,1408]{1,0:T(8,128)(2,1)} %fusion.14), channel_id=1, source_target_pairs={{0,8},{1,5},{2,10},{3,7},{8,16},{9,1},{10,18},{11,3},{16,24},{17,9... | collective-permute-start | bytes 1081352 | tf_op jit(solution)/shard_map/ppermute | solution.py:851
  267.3 11.2 %copy-start.1 = (bf16[8,2,128,768]{3,2,1,0:T(8,128)(2,1)S(1)}, bf16[8,2,128,768]{3,2,1,0:T(8,128)(2,1)}, u32[]{:S(2)}) copy-start(bf16[8,2,128,768]{3,2,1,0:T(8,128)(2,1)} %get-tuple-element.227) | copy-start | bytes 9437188
  269.4 8.8 %collective-permute-start.25 = (bf16[256,768]{1,0:T(8,128)(2,1)}, bf16[256,768]{1,0:T(8,128)(2,1)S(1)}, u32[]{:S(2)}, u32[]{:S(2)}) collective-permute-start(bf16[256,768]{1,0:T(8,128)(2,1)} %add_convert_fusion.17), channel_id=1, source_target_pairs={{0,8},{1,5},{2,10},{3,7},{8,16},{9,1},{10,18},{11,3},{16,24},{17,9... | collective-permute-start | bytes 1179656 | tf_op jit(solution)/shard_map/ppermute | solution.py:851
  274.6 9.1 %collective-permute-start.35 = (bf16[480,512]{1,0:T(8,128)(2,1)}, bf16[480,512]{1,0:T(8,128)(2,1)}, u32[]{:S(2)}, u32[]{:S(2)}) collective-permute-start(bf16[480,512]{1,0:T(8,128)(2,1)} %add_convert_fusion.6), channel_id=1, source_target_pairs={{0,8},{1,5},{2,10},{3,7},{8,16},{9,1},{10,18},{11,3},{16,24},{17,9... | collective-permute-start | bytes 1474568 | tf_op jit(solution)/shard_map/ppermute | solution.py:851
  275.1 15.2 %collective-permute-start.45 = (bf16[128,1408]{1,0:T(8,128)(2,1)}, bf16[128,1408]{1,0:T(8,128)(2,1)S(1)}, u32[]{:S(2)}, u32[]{:S(2)}) collective-permute-start(bf16[128,1408]{1,0:T(8,128)(2,1)} %get-tuple-element.266), channel_id=1, source_target_pairs={{0,2},{1,3},{2,0},{3,1},{4,6},{5,7},{6,4},{7,5},{8,10},{9,11},{10,... | collective-permute-start | bytes 1081352 | tf_op jit(solution)/shard_map/ppermute | solution.py:864
  276.2 18.1 %collective-permute-start.27 = (bf16[128,1408]{1,0:T(8,128)(2,1)}, bf16[128,1408]{1,0:T(8,128)(2,1)S(1)}, u32[]{:S(2)}, u32[]{:S(2)}) collective-permute-start(bf16[128,1408]{1,0:T(8,128)(2,1)} %get-tuple-element.269), channel_id=1, source_target_pairs={{0,2},{1,3},{2,0},{3,1},{4,6},{5,7},{6,4},{7,5},{8,10},{9,11},{10,... | collective-permute-start | bytes 1081352 | tf_op jit(solution)/shard_map/ppermute | solution.py:864
  277.1 53.0 %collective-permute-start.48 = (bf16[128,1408]{1,0:T(8,128)(2,1)}, bf16[128,1408]{1,0:T(8,128)(2,1)}, u32[]{:S(2)}, u32[]{:S(2)}) collective-permute-start(bf16[128,1408]{1,0:T(8,128)(2,1)} %get-tuple-element.268), channel_id=1, source_target_pairs={{0,2},{1,3},{2,0},{3,1},{4,6},{5,7},{6,4},{7,5},{8,10},{9,11},{10,... | collective-permute-start | bytes 1081352 | tf_op jit(solution)/shard_map/ppermute | solution.py:864
  278.3 9.2 %collective-permute-start.44 = (bf16[128,1408]{1,0:T(8,128)(2,1)}, bf16[128,1408]{1,0:T(8,128)(2,1)S(1)}, u32[]{:S(2)}, u32[]{:S(2)}) collective-permute-start(bf16[128,1408]{1,0:T(8,128)(2,1)} %fusion.12), channel_id=1, source_target_pairs={{0,8},{1,5},{2,10},{3,7},{8,16},{9,1},{10,18},{11,3},{16,24},{17,9... | collective-permute-start | bytes 1081352 | tf_op jit(solution)/shard_map/ppermute | solution.py:851
  283.7 8.0 %collective-permute-start.26 = (bf16[256,768]{1,0:T(8,128)(2,1)S(1)}, bf16[256,768]{1,0:T(8,128)(2,1)S(1)}, u32[]{:S(2)}, u32[]{:S(2)}) collective-permute-start(bf16[256,768]{1,0:T(8,128)(2,1)S(1)} %add_convert_fusion.16), channel_id=1, source_target_pairs={{0,8},{1,5},{2,10},{3,7},{8,16},{9,1},{10,18},{11,3},{16,24},{17,9... | collective-permute-start | bytes 1179656 | tf_op jit(solution)/shard_map/ppermute | solution.py:851
  287.5 9.5 %collective-permute-start.36 = (bf16[480,512]{1,0:T(8,128)(2,1)S(1)}, bf16[480,512]{1,0:T(8,128)(2,1)S(1)}, u32[]{:S(2)}, u32[]{:S(2)}) collective-permute-start(bf16[480,512]{1,0:T(8,128)(2,1)S(1)} %add_convert_fusion.5), channel_id=1, source_target_pairs={{0,8},{1,5},{2,10},{3,7},{8,16},{9,1},{10,18},{11,3},{16,24},{17,9... | collective-permute-start | bytes 1474568 | tf_op jit(solution)/shard_map/ppermute | solution.py:851
  290.3 8.6 %copy-start.15 = (bf16[128,1408]{1,0:T(8,128)(2,1)}, bf16[128,1408]{1,0:T(8,128)(2,1)S(1)}, u32[]{:S(2)}) copy-start(bf16[128,1408]{1,0:T(8,128)(2,1)S(1)} %collective-permute-done.45) | copy-start | bytes 1081348
  290.3 53.2 %collective-permute-start.50 = (bf16[128,1408]{1,0:T(8,128)(2,1)}, bf16[128,1408]{1,0:T(8,128)(2,1)}, u32[]{:S(2)}, u32[]{:S(2)}) collective-permute-start(bf16[128,1408]{1,0:T(8,128)(2,1)} %get-tuple-element.267), channel_id=1, source_target_pairs={{0,2},{1,3},{2,0},{3,1},{4,6},{5,7},{6,4},{7,5},{8,10},{9,11},{10,... | collective-permute-start | bytes 1081352 | tf_op jit(solution)/shard_map/ppermute | solution.py:864
  291.7 23.5 %collective-permute-start.46 = (bf16[128,1408]{1,0:T(8,128)(2,1)}, bf16[128,1408]{1,0:T(8,128)(2,1)}, u32[]{:S(2)}, u32[]{:S(2)}) collective-permute-start(bf16[128,1408]{1,0:T(8,128)(2,1)} %fusion.10), channel_id=1, source_target_pairs={{0,8},{1,5},{2,10},{3,7},{8,16},{9,1},{10,18},{11,3},{16,24},{17,9... | collective-permute-start | bytes 1081352 | tf_op jit(solution)/shard_map/ppermute | solution.py:851
  294.3 16.2 %collective-permute-start.28 = (bf16[256,768]{1,0:T(8,128)(2,1)S(1)}, bf16[256,768]{1,0:T(8,128)(2,1)}, u32[]{:S(2)}, u32[]{:S(2)}) collective-permute-start(bf16[256,768]{1,0:T(8,128)(2,1)S(1)} %add_convert_fusion.15), channel_id=1, source_target_pairs={{0,8},{1,5},{2,10},{3,7},{8,16},{9,1},{10,18},{11,3},{16,24},{17,9... | collective-permute-start | bytes 1179656 | tf_op jit(solution)/shard_map/ppermute | solution.py:851
  298.3 13.9 %collective-permute-start.37 = (bf16[480,512]{1,0:T(8,128)(2,1)S(1)}, bf16[480,512]{1,0:T(8,128)(2,1)}, u32[]{:S(2)}, u32[]{:S(2)}) collective-permute-start(bf16[480,512]{1,0:T(8,128)(2,1)S(1)} %add_convert_fusion.4), channel_id=1, source_target_pairs={{0,8},{1,5},{2,10},{3,7},{8,16},{9,1},{10,18},{11,3},{16,24},{17,9... | collective-permute-start | bytes 1474568 | tf_op jit(solution)/shard_map/ppermute | solution.py:851
  311.8 7.8 %collective-permute-start.29 = (bf16[256,768]{1,0:T(8,128)(2,1)S(1)}, bf16[256,768]{1,0:T(8,128)(2,1)S(1)}, u32[]{:S(2)}, u32[]{:S(2)}) collective-permute-start(bf16[256,768]{1,0:T(8,128)(2,1)S(1)} %add_convert_fusion.14), channel_id=1, source_target_pairs={{0,8},{1,5},{2,10},{3,7},{8,16},{9,1},{10,18},{11,3},{16,24},{17,9... | collective-permute-start | bytes 1179656 | tf_op jit(solution)/shard_map/ppermute | solution.py:851
  313.7 15.1 %copy-start.14 = (bf16[128,1408]{1,0:T(8,128)(2,1)S(1)}, bf16[128,1408]{1,0:T(8,128)(2,1)}, u32[]{:S(2)}) copy-start(bf16[128,1408]{1,0:T(8,128)(2,1)} %copy-done.13) | copy-start | bytes 1081348
  313.7 11.2 %collective-permute-start.38 = (bf16[480,512]{1,0:T(8,128)(2,1)S(1)}, bf16[480,512]{1,0:T(8,128)(2,1)S(1)}, u32[]{:S(2)}, u32[]{:S(2)}) collective-permute-start(bf16[480,512]{1,0:T(8,128)(2,1)S(1)} %add_convert_fusion.3), channel_id=1, source_target_pairs={{0,8},{1,5},{2,10},{3,7},{8,16},{9,1},{10,18},{11,3},{16,24},{17,9... | collective-permute-start | bytes 1474568 | tf_op jit(solution)/shard_map/ppermute | solution.py:851
  316.6 12.2 %collective-permute-start.47 = (bf16[128,1408]{1,0:T(8,128)(2,1)S(1)}, bf16[128,1408]{1,0:T(8,128)(2,1)S(1)}, u32[]{:S(2)}, u32[]{:S(2)}) collective-permute-start(bf16[128,1408]{1,0:T(8,128)(2,1)S(1)} %fusion.8), channel_id=1, source_target_pairs={{0,8},{1,5},{2,10},{3,7},{8,16},{9,1},{10,18},{11,3},{16,24},{17,9... | collective-permute-start | bytes 1081352 | tf_op jit(solution)/shard_map/ppermute | solution.py:851
  320.8 12.2 %collective-permute-start.30 = (bf16[256,768]{1,0:T(8,128)(2,1)S(1)}, bf16[256,768]{1,0:T(8,128)(2,1)S(1)}, u32[]{:S(2)}, u32[]{:S(2)}) collective-permute-start(bf16[256,768]{1,0:T(8,128)(2,1)S(1)} %add_convert_fusion.13), channel_id=1, source_target_pairs={{0,8},{1,5},{2,10},{3,7},{8,16},{9,1},{10,18},{11,3},{16,24},{17,9... | collective-permute-start | bytes 1179656 | tf_op jit(solution)/shard_map/ppermute | solution.py:851
  326.3 12.0 %collective-permute-start.39 = (bf16[480,512]{1,0:T(8,128)(2,1)S(1)}, bf16[480,512]{1,0:T(8,128)(2,1)S(1)}, u32[]{:S(2)}, u32[]{:S(2)}) collective-permute-start(bf16[480,512]{1,0:T(8,128)(2,1)S(1)} %add_convert_fusion.2), channel_id=1, source_target_pairs={{0,8},{1,5},{2,10},{3,7},{8,16},{9,1},{10,18},{11,3},{16,24},{17,9... | collective-permute-start | bytes 1474568 | tf_op jit(solution)/shard_map/ppermute | solution.py:851
  330.1 12.1 %collective-permute-start.49 = (bf16[128,1408]{1,0:T(8,128)(2,1)S(1)}, bf16[128,1408]{1,0:T(8,128)(2,1)S(1)}, u32[]{:S(2)}, u32[]{:S(2)}) collective-permute-start(bf16[128,1408]{1,0:T(8,128)(2,1)S(1)} %fusion.6), channel_id=1, source_target_pairs={{0,8},{1,5},{2,10},{3,7},{8,16},{9,1},{10,18},{11,3},{16,24},{17,9... | collective-permute-start | bytes 1081352 | tf_op jit(solution)/shard_map/ppermute | solution.py:851
  334.2 12.2 %collective-permute-start.31 = (bf16[256,768]{1,0:T(8,128)(2,1)S(1)}, bf16[256,768]{1,0:T(8,128)(2,1)S(1)}, u32[]{:S(2)}, u32[]{:S(2)}) collective-permute-start(bf16[256,768]{1,0:T(8,128)(2,1)S(1)} %add_convert_fusion.12), channel_id=1, source_target_pairs={{0,8},{1,5},{2,10},{3,7},{8,16},{9,1},{10,18},{11,3},{16,24},{17,9... | collective-permute-start | bytes 1179656 | tf_op jit(solution)/shard_map/ppermute | solution.py:851
  339.6 9.3 %collective-permute-start.40 = (bf16[480,512]{1,0:T(8,128)(2,1)S(1)}, bf16[480,512]{1,0:T(8,128)(2,1)S(1)}, u32[]{:S(2)}, u32[]{:S(2)}) collective-permute-start(bf16[480,512]{1,0:T(8,128)(2,1)S(1)} %add_convert_fusion.1), channel_id=1, source_target_pairs={{0,2},{1,3},{2,0},{3,1},{4,6},{5,7},{6,4},{7,5},{8,10},{9,11},{10,... | collective-permute-start | bytes 1474568 | tf_op jit(solution)/shard_map/ppermute | solution.py:864
  343.5 7.5 %collective-permute-start.51 = (bf16[128,1408]{1,0:T(8,128)(2,1)S(1)}, bf16[128,1408]{1,0:T(8,128)(2,1)S(1)}, u32[]{:S(2)}, u32[]{:S(2)}) collective-permute-start(bf16[128,1408]{1,0:T(8,128)(2,1)S(1)} %fusion.4), channel_id=1, source_target_pairs={{0,8},{1,5},{2,10},{3,7},{8,16},{9,1},{10,18},{11,3},{16,24},{17,9... | collective-permute-start | bytes 1081352 | tf_op jit(solution)/shard_map/ppermute | solution.py:851
  348.2 10.7 %collective-permute-start.32 = (bf16[256,768]{1,0:T(8,128)(2,1)}, bf16[256,768]{1,0:T(8,128)(2,1)S(1)}, u32[]{:S(2)}, u32[]{:S(2)}) collective-permute-start(bf16[256,768]{1,0:T(8,128)(2,1)} %add_convert_fusion.11), channel_id=1, source_target_pairs={{0,8},{1,5},{2,10},{3,7},{8,16},{9,1},{10,18},{11,3},{16,24},{17,9... | collective-permute-start | bytes 1179656 | tf_op jit(solution)/shard_map/ppermute | solution.py:851
  349.8 4.5 %collective-permute-start.41 = (bf16[480,512]{1,0:T(8,128)(2,1)}, bf16[480,512]{1,0:T(8,128)(2,1)}, u32[]{:S(2)}, u32[]{:S(2)}) collective-permute-start(bf16[480,512]{1,0:T(8,128)(2,1)} %add_convert_fusion.refs_0_.out_ref), channel_id=1, source_target_pairs={{0,1},{1,0},{2,3},{3,2},{4,5},{5,4},{6,7},{7,6},{8,9},{9,8},{10,11... | collective-permute-start | bytes 1474568 | tf_op jit(solution)/shard_map/ppermute | solution.py:860
  353.1 10.3 %collective-permute-start.52 = (bf16[128,1408]{1,0:T(8,128)(2,1)}, bf16[128,1408]{1,0:T(8,128)(2,1)}, u32[]{:S(2)}, u32[]{:S(2)}) collective-permute-start(bf16[128,1408]{1,0:T(8,128)(2,1)} %fusion.2), channel_id=1, source_target_pairs={{0,2},{1,3},{2,0},{3,1},{4,6},{5,7},{6,4},{7,5},{8,10},{9,11},{10,... | collective-permute-start | bytes 1081352 | tf_op jit(solution)/shard_map/ppermute | solution.py:864
  360.9 13.5 %collective-permute-start.42 = (bf16[256,768]{1,0:T(8,128)(2,1)S(1)}, bf16[256,768]{1,0:T(8,128)(2,1)S(1)}, u32[]{:S(2)}, u32[]{:S(2)}) collective-permute-start(bf16[256,768]{1,0:T(8,128)(2,1)S(1)} %add_convert_fusion.10), channel_id=1, source_target_pairs={{0,2},{1,3},{2,0},{3,1},{4,6},{5,7},{6,4},{7,5},{8,10},{9,11},{10,... | collective-permute-start | bytes 1179656 | tf_op jit(solution)/shard_map/ppermute | solution.py:864
  364.6 4.9 %collective-permute-start.53 = (bf16[128,1408]{1,0:T(8,128)(2,1)S(1)}, bf16[128,1408]{1,0:T(8,128)(2,1)S(1)}, u32[]{:S(2)}, u32[]{:S(2)}) collective-permute-start(bf16[128,1408]{1,0:T(8,128)(2,1)S(1)} %get-tuple-element.275.refs_0_), channel_id=1, source_target_pairs={{0,1},{1,0},{2,3},{3,2},{4,5},{5,4},{6,7},{7,6},{8,9},{9,8},{10,11... | collective-permute-start | bytes 1081352 | tf_op jit(solution)/shard_map/ppermute | solution.py:860
  364.7 4.8 %collective-permute-start.54 = (bf16[128,1408]{1,0:T(8,128)(2,1)S(1)}, bf16[128,1408]{1,0:T(8,128)(2,1)S(1)}, u32[]{:S(2)}, u32[]{:S(2)}) collective-permute-start(bf16[128,1408]{1,0:T(8,128)(2,1)S(1)} %get-tuple-element.274.refs_1_), channel_id=1, source_target_pairs={{0,1},{1,0},{2,3},{3,2},{4,5},{5,4},{6,7},{7,6},{8,9},{9,8},{10,11... | collective-permute-start | bytes 1081352 | tf_op jit(solution)/shard_map/ppermute | solution.py:860
  374.5 4.6 %collective-permute-start.55 = (bf16[256,768]{1,0:T(8,128)(2,1)S(1)}, bf16[256,768]{1,0:T(8,128)(2,1)S(1)}, u32[]{:S(2)}, u32[]{:S(2)}) collective-permute-start(bf16[256,768]{1,0:T(8,128)(2,1)S(1)} %add_convert_fusion.9.qfv_ref), channel_id=1, source_target_pairs={{0,1},{1,0},{2,3},{3,2},{4,5},{5,4},{6,7},{7,6},{8,9},{9,8},{10,11... | collective-permute-start | bytes 1179656 | tf_op jit(solution)/shard_map/ppermute | solution.py:860
  (15 other events, 26.4 us)
